TPU v7x, 32 devices: a whole 2x2x4 slice. The times are simulated.
32 devices in a mesh: sec: 4 (over z), tile: 8 (over y, x, core).
Axes of the slice: x: 2, y: 2, z: 4, core: 2. Of those that a mesh axis runs over, the one named last changes fastest.
Arguments:
- sections: float32 [8, 512, 4096], P('sec', 'tile'), may hold values from -6 to 6
- displacement: float32 [8, 2, 512, 4096], P('sec', None, 'tile'), may hold values from -3 to 3
- warp_offsets: int32 [8, 8, 2], P('sec', 'tile'), may hold values from -5 to 4
- warp_fractions: int32 [8, 8, 2], P('sec', 'tile'), may hold values from 0 to 255
- pair_weights: int32 [8, 2], P('sec'), may hold values from 1 to 4
Outputs:
- aligned_field: float32 [8, 2, 512, 4096], P('sec', None, 'tile')
All inputs are finite; a program needn't handle non-finite values.
Results may differ from a plain program's by a relative error of at most 0.0003.
Values sent between devices are 32-bit elements; how exact they have to be, the bound alone decides.
No kernel may reach another device: no remote copies, remote signals or barrier semaphores. Data moves between devices by JAX's collectives and lax.ppermute only.
A program may use at most 64 MiB of HBM per device.

v0:
```python
import jax
import jax.numpy as jnp
from jax import lax
from jax.sharding import PartitionSpec as P

ITERS = 2
SWEEPS = 3


relax_rate = 0.2
force_scale = 0.5
softening = 0.25


def padded_2(block, sides, width):
    for axis, dim in sides:
        count = lax.axis_size(axis)
        forward = [(i, i + 1) for i in range(count - 1)]
        backward = [(target, source) for source, target in forward]
        low = lax.ppermute(
            lax.slice_in_dim(block, block.shape[dim] - width, None, axis=dim), axis, forward
        )
        high = lax.ppermute(lax.slice_in_dim(block, 0, width, axis=dim), axis, backward)
        block = jnp.concatenate([low, block, high], axis=dim)
    return block


def bilinear_blend(block, fraction):
    frac_row = fraction[0].astype(block.dtype) / 256.0
    frac_col = fraction[1].astype(block.dtype) / 256.0
    upper = (1.0 - frac_col) * block[:-1, :-1] + frac_col * block[:-1, 1:]
    lower = (1.0 - frac_col) * block[1:, :-1] + frac_col * block[1:, 1:]
    return (1.0 - frac_row) * upper + frac_row * lower


def relax_rows(padded):
    interior = padded[:, :, 1:-1]
    beside = jnp.pad(interior, ((0, 0), (0, 0), (0, 0), (1, 1)))
    return interior + relax_rate * (
        padded[:, :, 2:] + padded[:, :, :-2] + beside[..., 2:] + beside[..., :-2] - 4.0 * interior
    )


def local(sections, displacement, warp_offsets, warp_fractions, pair_weights):
    local_sections, strip_rows, strip_width = sections.shape
    sec_pos = lax.axis_index("sec")
    sec_count = lax.axis_size("sec")
    rims = padded_2(sections, (("tile", 1),), 5)
    widened = jnp.pad(rims, ((0, 0), (0, 0), (5, 5)))

    def warp_plane(plane, shift_pair, fraction):
        start_row = 5 + shift_pair[0]
        start_col = 5 + shift_pair[1]
        block = lax.dynamic_slice(plane, (start_row, start_col), (strip_rows + 1, strip_width + 1))
        return bilinear_blend(block, fraction)

    warped = jax.vmap(warp_plane)(widened, warp_offsets[:, 0], warp_fractions[:, 0])
    stretched = padded_2(warped, (("tile", 1),), 1)
    grad_rows = 0.5 * (stretched[:, 2:] - stretched[:, :-2])
    edged = jnp.pad(warped, ((0, 0), (0, 0), (1, 1)))
    grad_cols = 0.5 * (edged[:, :, 2:] - edged[:, :, :-2])
    denominator = grad_rows * grad_rows + grad_cols * grad_cols + softening
    scales = pair_weights.astype(jnp.float32)
    section_number = sec_pos * local_sections + jnp.arange(local_sections, dtype=jnp.int32)
    lower_valid = section_number > 0
    upper_valid = section_number < local_sections * sec_count - 1
    current_field = displacement
    for iteration in range(ITERS):
        linear = warped + current_field[:, 0] * grad_rows + current_field[:, 1] * grad_cols
        nearby = padded_2(linear, (("sec", 0),), 1)
        lower_diff = jnp.where(lower_valid[:, None, None], nearby[:-2] - linear, 0.0)
        upper_diff = jnp.where(upper_valid[:, None, None], nearby[2:] - linear, 0.0)
        coupling = scales[:, 0, None, None] * lower_diff / (denominator + lower_diff * lower_diff)
        coupling = coupling + scales[:, 1, None, None] * upper_diff / (
            denominator + upper_diff * upper_diff
        )
        moved = current_field + force_scale * jnp.stack(
            [coupling * grad_rows, coupling * grad_cols], axis=1
        )
        for sweep_index in range(SWEEPS):
            extended = padded_2(moved, (("tile", 2),), 1)
            moved = relax_rows(extended)
        current_field = moved
    return current_field


def solution(mesh):
    return jax.shard_map(
        local,
        mesh=mesh,
        in_specs=(
            P("sec", "tile", None),
            P("sec", None, "tile", None),
            P("sec", "tile", None),
            P("sec", "tile", None),
            P("sec", None),
        ),
        out_specs=P("sec", None, "tile", None),
        check_vma=False,
    )
```

profile of v0, /device:TPU:4, one launch (start us, length us, event | category | flops | bytes accessed | tf_op | source)
XLA Modules:
  0.0 181.2 jit_solution(9790738501569162769)
XLA Ops:
  3.0 4.5 %collective-permute-start.1 = (f32[2,5,4096]{2,1,0:T(8,128)S(1)}, f32[2,5,4096]{2,1,0:T(8,128)S(1)}, u32[]{:S(2)}, u32[]{:S(2)}) collective-permute-start(f32[2,5,4096]{2,1,0:T(8,128)S(1)} %get-tuple-element.53), channel_id=1, source_target_pairs={{1,0},{2,1},{3,2},{4,3},{5,4},{6,5},{7,6},{9,8},{10,9},{11,10},{12... | collective-permute-start | bytes 491528 | tf_op jit(solution)/shard_map/ppermute | solution.py:23
  11.4 4.0 %select_maximum_fusion = f32[2,74,4106]{2,1,0:T(8,128)} fusion(f32[2,5,4096]{2,1,0:T(8,128)S(1)} %collective-permute-done.1, f32[2,64,4096]{2,1,0:T(8,128)} %param.5, f32[2,5,4096]{2,1,0:T(8,128)S(1)} %collective-permute-done), kind=kLoop, calls=%fused_computation.58 | loop fusion | flops 4861504 | bytes 4855584 | tf_op jit(solution)/shard_map/concatenate | solution.py:24
  15.4 8.4 %while.1 = (s32[]{:T(128)}, f32[2,74,4106]{2,1,0:T(8,128)}, s32[2,3]{1,0:T(2,128)S(1)}, f32[2,65,4097]{2,1,0:T(8,128)S(1)}, s32[]{:T(128)}) while((s32[]{:T(128)}, f32[2,74,4106]{2,1,0:T(8,128)}, s32[2,3]{1,0:T(2,128)S(1)}, f32[2,65,4097]{2,1,0:T(8,128)S(1)}, s32[]{:T(128)}) %tuple.38), condition=%wide.while_cond, body=%wide.while_body.sunk | while | flops 2 | bytes 2281869 | solution.py:54
  16.1 3.5 %dynamic-slice_dynamic-update-slice_fusion.2 = f32[2,65,4097]{2,1,0:T(8,128)S(1)} fusion(f32[2,65,4097]{2,1,0:T(8,128)S(1)} %get-tuple-element.99, s32[]{:T(128)S(6)} %copy.28, f32[2,74,4106]{2,1,0:T(8,128)} %get-tuple-element.102, s32[]{:T(128)} %bitcast.46, s32[]{:T(128)} %bitcast.47, s32[]{:T(128)} %bitcast.48), kind=kLoop, calls=%fused_computation.clone.1 | loop fusion | bytes 2281748 | tf_op jit(solution)/shard_map/vmap()/gather
  20.3 3.5 %dynamic-slice_dynamic-update-slice_fusion.2 = f32[2,65,4097]{2,1,0:T(8,128)S(1)} fusion(f32[2,65,4097]{2,1,0:T(8,128)S(1)} %get-tuple-element.99, s32[]{:T(128)S(6)} %copy.28, f32[2,74,4106]{2,1,0:T(8,128)} %get-tuple-element.102, s32[]{:T(128)} %bitcast.46, s32[]{:T(128)} %bitcast.47, s32[]{:T(128)} %bitcast.48), kind=kLoop, calls=%fused_computation.clone.1 | loop fusion | bytes 2281748 | tf_op jit(solution)/shard_map/vmap()/gather
  25.3 4.8 %collective-permute-start.2 = (f32[2,1,4096]{2,1,0:T(1,128)S(1)}, f32[2,1,4096]{2,1,0:T(1,128)S(1)}, u32[]{:S(2)}, u32[]{:S(2)}) collective-permute-start(f32[2,1,4096]{2,1,0:T(1,128)S(1)} %get-tuple-element.50), channel_id=1, source_target_pairs={{1,0},{2,1},{3,2},{4,3},{5,4},{6,5},{7,6},{9,8},{10,9},{11,10},{12... | collective-permute-start | bytes 98312 | tf_op jit(solution)/shard_map/ppermute | solution.py:23
  32.1 4.2 %collective-permute-done.3 = f32[2,1,4096]{2,1,0:T(1,128)S(1)} collective-permute-done((f32[2,1,4096]{2,1,0:T(1,128)S(1)}, f32[2,1,4096]{2,1,0:T(1,128)S(1)}, u32[]{:S(2)}, u32[]{:S(2)}) %collective-permute-start.3) | collective-permute-done | bytes 32800 | tf_op jit(solution)/shard_map/ppermute | solution.py:20
  40.3 4.5 %collective-permute-start.4 = (f32[1,64,4096]{2,1,0:T(8,128)}, f32[1,64,4096]{2,1,0:T(8,128)}, u32[]{:S(2)}, u32[]{:S(2)}) collective-permute-start(f32[1,64,4096]{2,1,0:T(8,128)} %get-tuple-element.48), channel_id=1, source_target_pairs={{0,8},{8,16},{16,24},{1,9},{9,17},{17,25},{2,10},{10,18},{18,26},{... | collective-permute-start | bytes 3145736 | tf_op jit(solution)/shard_map/ppermute | solution.py:20
  46.3 17.4 %collective-permute-done.4 = f32[1,64,4096]{2,1,0:T(8,128)} collective-permute-done((f32[1,64,4096]{2,1,0:T(8,128)}, f32[1,64,4096]{2,1,0:T(8,128)}, u32[]{:S(2)}, u32[]{:S(2)}) %collective-permute-start.4) | collective-permute-done | bytes 1048608 | tf_op jit(solution)/shard_map/ppermute | solution.py:20
  63.6 4.9 %collective-permute-done.5 = f32[1,64,4096]{2,1,0:T(8,128)} collective-permute-done((f32[1,64,4096]{2,1,0:T(8,128)S(1)}, f32[1,64,4096]{2,1,0:T(8,128)}, u32[]{:S(2)}, u32[]{:S(2)}) %collective-permute-start.5) | collective-permute-done | bytes 1048608 | tf_op jit(solution)/shard_map/ppermute | solution.py:23
  68.5 5.1 %multiply_bitcast_fusion.3 = (f32[2,1,64,4096]{3,2,0,1:T(8,128)S(1)}, f32[2,64,4096]{2,1,0:T(8,128)S(1)}) fusion(f32[2,64,4096]{2,1,0:T(8,128)} %copy-done, f32[2,1,4096]{2,1,0:T(1,128)S(1)} %collective-permute-done.3, f32[2,1,4096]{2,1,0:T(1,128)S(1)} %collective-permute-done.2, f32[2,64,4096]{2,1,0:T(8,128)} %copy-done.2, ...), kind=kLoop, calls=%fused_computation.91 | loop fusion | flops 12582912 | bytes 12648468 | tf_op jit(solution)/shard_map/stack | solution.py:77
  76.8 4.3 %collective-permute-start.6 = (f32[2,2,1,4096]{3,2,1,0:T(1,128)S(1)}, f32[2,2,1,4096]{3,2,1,0:T(1,128)S(1)}, u32[]{:S(2)}, u32[]{:S(2)}) collective-permute-start(f32[2,2,1,4096]{3,2,1,0:T(1,128)S(1)} %get-tuple-element.44), channel_id=1, source_target_pairs={{1,0},{2,1},{3,2},{4,3},{5,4},{6,5},{7,6},{9,8},{10,9},{11,10},{12... | collective-permute-start | bytes 196616 | tf_op jit(solution)/shard_map/ppermute | solution.py:23
  83.0 4.5 %collective-permute-done.7 = f32[2,2,1,4096]{3,2,1,0:T(1,128)S(1)} collective-permute-done((f32[2,2,1,4096]{3,2,1,0:T(1,128)S(1)}, f32[2,2,1,4096]{3,2,1,0:T(1,128)S(1)}, u32[]{:S(2)}, u32[]{:S(2)}) %collective-permute-start.7) | collective-permute-done | bytes 65568 | tf_op jit(solution)/shard_map/ppermute | solution.py:20
  94.4 4.1 %collective-permute-done.9 = f32[2,2,1,4096]{3,2,1,0:T(1,128)S(1)} collective-permute-done((f32[2,2,1,4096]{3,2,1,0:T(1,128)S(1)}, f32[2,2,1,4096]{3,2,1,0:T(1,128)S(1)}, u32[]{:S(2)}, u32[]{:S(2)}) %collective-permute-start.9) | collective-permute-done | bytes 65568 | tf_op jit(solution)/shard_map/ppermute | solution.py:20
  105.4 4.1 %collective-permute-done.11 = f32[2,2,1,4096]{3,2,1,0:T(1,128)S(1)} collective-permute-done((f32[2,2,1,4096]{3,2,1,0:T(1,128)S(1)}, f32[2,2,1,4096]{3,2,1,0:T(1,128)S(1)}, u32[]{:S(2)}, u32[]{:S(2)}) %collective-permute-start.11) | collective-permute-done | bytes 65568 | tf_op jit(solution)/shard_map/ppermute | solution.py:20
  112.9 2.6 %collective-permute-start.12 = (f32[1,64,4096]{2,1,0:T(8,128)S(1)}, f32[1,64,4096]{2,1,0:T(8,128)S(1)}, u32[]{:S(2)}, u32[]{:S(2)}) collective-permute-start(f32[1,64,4096]{2,1,0:T(8,128)S(1)} %get-tuple-element.46), channel_id=1, source_target_pairs={{0,8},{8,16},{16,24},{1,9},{9,17},{17,25},{2,10},{10,18},{18,26},{... | collective-permute-start | bytes 3145736 | tf_op jit(solution)/shard_map/ppermute | solution.py:20
  116.8 18.5 %collective-permute-done.12 = f32[1,64,4096]{2,1,0:T(8,128)S(1)} collective-permute-done((f32[1,64,4096]{2,1,0:T(8,128)S(1)}, f32[1,64,4096]{2,1,0:T(8,128)S(1)}, u32[]{:S(2)}, u32[]{:S(2)}) %collective-permute-start.12) | collective-permute-done | bytes 1048608 | tf_op jit(solution)/shard_map/ppermute | solution.py:20
  135.2 4.2 %collective-permute-done.13 = f32[1,64,4096]{2,1,0:T(8,128)S(1)} collective-permute-done((f32[1,64,4096]{2,1,0:T(8,128)S(1)}, f32[1,64,4096]{2,1,0:T(8,128)S(1)}, u32[]{:S(2)}, u32[]{:S(2)}) %collective-permute-start.13) | collective-permute-done | bytes 1048608 | tf_op jit(solution)/shard_map/ppermute | solution.py:23
  141.8 4.3 %fusion.36 = f32[2,2,64,4096]{3,2,1,0:T(8,128)S(1)} fusion(f32[2,2,64,4096]{3,2,1,0:T(8,128)S(1)} %fusion.29, f32[2,2,1,4096]{3,2,1,0:T(1,128)S(1)} %collective-permute-done.11, f32[2,2,1,4096]{3,2,1,0:T(1,128)S(1)} %collective-permute-done.10, f32[2,1,64,4096]{3,2,0,1:T(8,128)S(1)} %multiply_bitcast_fusion, f32[2,1,64,4096]{3,2,0,1:T(8,128)S(1)} %get-tuple-element.25), kind=kLoop, calls=%fused_computation.53 | loop fusion | flops 12582912 | bytes 12713984 | tf_op jit(solution)/shard_map/add | solution.py:77
  146.2 3.1 %collective-permute-start.14 = (f32[2,2,1,4096]{3,2,1,0:T(1,128)S(1)}, f32[2,2,1,4096]{3,2,1,0:T(1,128)S(1)}, u32[]{:S(2)}, u32[]{:S(2)}) collective-permute-start(f32[2,2,1,4096]{3,2,1,0:T(1,128)S(1)} %get-tuple-element.38), channel_id=1, source_target_pairs={{1,0},{2,1},{3,2},{4,3},{5,4},{6,5},{7,6},{9,8},{10,9},{11,10},{12... | collective-permute-start | bytes 196616 | tf_op jit(solution)/shard_map/ppermute | solution.py:23
  151.3 4.5 %collective-permute-done.15 = f32[2,2,1,4096]{3,2,1,0:T(1,128)S(1)} collective-permute-done((f32[2,2,1,4096]{3,2,1,0:T(1,128)S(1)}, f32[2,2,1,4096]{3,2,1,0:T(1,128)S(1)}, u32[]{:S(2)}, u32[]{:S(2)}) %collective-permute-start.15) | collective-permute-done | bytes 65568 | tf_op jit(solution)/shard_map/ppermute | solution.py:20
  162.6 4.1 %collective-permute-done.17 = f32[2,2,1,4096]{3,2,1,0:T(1,128)S(1)} collective-permute-done((f32[2,2,1,4096]{3,2,1,0:T(1,128)S(1)}, f32[2,2,1,4096]{3,2,1,0:T(1,128)S(1)}, u32[]{:S(2)}, u32[]{:S(2)}) %collective-permute-start.17) | collective-permute-done | bytes 65568 | tf_op jit(solution)/shard_map/ppermute | solution.py:20
  173.5 4.1 %collective-permute-done.19 = f32[2,2,1,4096]{3,2,1,0:T(1,128)S(1)} collective-permute-done((f32[2,2,1,4096]{3,2,1,0:T(1,128)S(1)}, f32[2,2,1,4096]{3,2,1,0:T(1,128)S(1)}, u32[]{:S(2)}, u32[]{:S(2)}) %collective-permute-start.19) | collective-permute-done | bytes 65568 | tf_op jit(solution)/shard_map/ppermute | solution.py:20
  177.5 3.7 %fusion.5 = f32[2,2,64,4096]{3,2,1,0:T(8,128)} fusion(f32[2,2,64,4096]{3,2,1,0:T(8,128)S(1)} %fusion.11, f32[2,2,1,4096]{3,2,1,0:T(1,128)S(1)} %collective-permute-done.19, f32[2,2,1,4096]{3,2,1,0:T(1,128)S(1)} %collective-permute-done.18), kind=kLoop, calls=%fused_computation.8 | loop fusion | flops 9437184 | bytes 8519680 | tf_op jit(solution)/shard_map/add | solution.py:39
  (70 shorter events, 58.4 us)
Async XLA Ops:
  1.1 8.6 %collective-permute-start = (f32[2,5,4096]{2,1,0:T(8,128)S(1)}, f32[2,5,4096]{2,1,0:T(8,128)S(1)}, u32[]{:S(2)}, u32[]{:S(2)}) collective-permute-start(f32[2,5,4096]{2,1,0:T(8,128)S(1)} %get-tuple-element.52), channel_id=1, source_target_pairs={{0,1},{1,2},{2,3},{3,4},{4,5},{5,6},{6,7},{8,9},{9,10},{10,11},{11... | collective-permute-start | bytes 491528 | tf_op jit(solution)/shard_map/ppermute | solution.py:20
  3.0 8.4 %collective-permute-start.1 = (f32[2,5,4096]{2,1,0:T(8,128)S(1)}, f32[2,5,4096]{2,1,0:T(8,128)S(1)}, u32[]{:S(2)}, u32[]{:S(2)}) collective-permute-start(f32[2,5,4096]{2,1,0:T(8,128)S(1)} %get-tuple-element.53), channel_id=1, source_target_pairs={{1,0},{2,1},{3,2},{4,3},{5,4},{6,5},{7,6},{9,8},{10,9},{11,10},{12... | collective-permute-start | bytes 491528 | tf_op jit(solution)/shard_map/ppermute | solution.py:23
  23.8 12.5 %copy-start.3 = (f32[2,2,64,4096]{3,2,1,0:T(8,128)S(1)}, f32[2,2,64,4096]{3,2,1,0:T(8,128)}, u32[]{:S(2)}) copy-start(f32[2,2,64,4096]{3,2,1,0:T(8,128)} %param.6) | copy-start | bytes 12582916
  25.3 12.5 %copy-start = (f32[2,64,4096]{2,1,0:T(8,128)}, f32[2,64,4096]{2,1,0:T(8,128)S(1)}, u32[]{:S(2)}) copy-start(f32[2,64,4096]{2,1,0:T(8,128)S(1)} %multiply_add_fusion) | copy-start | bytes 6291460
  25.3 6.7 %collective-permute-start.2 = (f32[2,1,4096]{2,1,0:T(1,128)S(1)}, f32[2,1,4096]{2,1,0:T(1,128)S(1)}, u32[]{:S(2)}, u32[]{:S(2)}) collective-permute-start(f32[2,1,4096]{2,1,0:T(1,128)S(1)} %get-tuple-element.50), channel_id=1, source_target_pairs={{1,0},{2,1},{3,2},{4,3},{5,4},{6,5},{7,6},{9,8},{10,9},{11,10},{12... | collective-permute-start | bytes 98312 | tf_op jit(solution)/shard_map/ppermute | solution.py:23
  30.2 6.1 %collective-permute-start.3 = (f32[2,1,4096]{2,1,0:T(1,128)S(1)}, f32[2,1,4096]{2,1,0:T(1,128)S(1)}, u32[]{:S(2)}, u32[]{:S(2)}) collective-permute-start(f32[2,1,4096]{2,1,0:T(1,128)S(1)} %get-tuple-element.51), channel_id=1, source_target_pairs={{0,1},{1,2},{2,3},{3,4},{4,5},{5,6},{6,7},{8,9},{9,10},{10,11},{11... | collective-permute-start | bytes 98312 | tf_op jit(solution)/shard_map/ppermute | solution.py:20
  37.7 8.3 %copy-start.5 = (s32[2,2]{1,0:T(2,128)S(1)}, s32[2,2]{1,0:T(2,128)}, u32[]{:S(2)}) copy-start(s32[2,2]{1,0:T(2,128)} %param.9) | copy-start | bytes 52
  40.3 23.3 %collective-permute-start.4 = (f32[1,64,4096]{2,1,0:T(8,128)}, f32[1,64,4096]{2,1,0:T(8,128)}, u32[]{:S(2)}, u32[]{:S(2)}) collective-permute-start(f32[1,64,4096]{2,1,0:T(8,128)} %get-tuple-element.48), channel_id=1, source_target_pairs={{0,8},{8,16},{16,24},{1,9},{9,17},{17,25},{2,10},{10,18},{18,26},{... | collective-permute-start | bytes 3145736 | tf_op jit(solution)/shard_map/ppermute | solution.py:20
  44.8 23.8 %collective-permute-start.5 = (f32[1,64,4096]{2,1,0:T(8,128)S(1)}, f32[1,64,4096]{2,1,0:T(8,128)}, u32[]{:S(2)}, u32[]{:S(2)}) collective-permute-start(f32[1,64,4096]{2,1,0:T(8,128)S(1)} %get-tuple-element.49), channel_id=1, source_target_pairs={{8,0},{16,8},{24,16},{9,1},{17,9},{25,17},{10,2},{18,10},{26,18},{... | collective-permute-start | bytes 3145736 | tf_op jit(solution)/shard_map/ppermute | solution.py:23
  76.8 6.2 %collective-permute-start.6 = (f32[2,2,1,4096]{3,2,1,0:T(1,128)S(1)}, f32[2,2,1,4096]{3,2,1,0:T(1,128)S(1)}, u32[]{:S(2)}, u32[]{:S(2)}) collective-permute-start(f32[2,2,1,4096]{3,2,1,0:T(1,128)S(1)} %get-tuple-element.44), channel_id=1, source_target_pairs={{1,0},{2,1},{3,2},{4,3},{5,4},{6,5},{7,6},{9,8},{10,9},{11,10},{12... | collective-permute-start | bytes 196616 | tf_op jit(solution)/shard_map/ppermute | solution.py:23
  81.1 6.5 %collective-permute-start.7 = (f32[2,2,1,4096]{3,2,1,0:T(1,128)S(1)}, f32[2,2,1,4096]{3,2,1,0:T(1,128)S(1)}, u32[]{:S(2)}, u32[]{:S(2)}) collective-permute-start(f32[2,2,1,4096]{3,2,1,0:T(1,128)S(1)} %get-tuple-element.45), channel_id=1, source_target_pairs={{0,1},{1,2},{2,3},{3,4},{4,5},{5,6},{6,7},{8,9},{9,10},{10,11},{11... | collective-permute-start | bytes 196616 | tf_op jit(solution)/shard_map/ppermute | solution.py:20
  90.0 4.3 %collective-permute-start.8 = (f32[2,2,1,4096]{3,2,1,0:T(1,128)S(1)}, f32[2,2,1,4096]{3,2,1,0:T(1,128)S(1)}, u32[]{:S(2)}, u32[]{:S(2)}) collective-permute-start(f32[2,2,1,4096]{3,2,1,0:T(1,128)S(1)} %get-tuple-element.42), channel_id=1, source_target_pairs={{1,0},{2,1},{3,2},{4,3},{5,4},{6,5},{7,6},{9,8},{10,9},{11,10},{12... | collective-permute-start | bytes 196616 | tf_op jit(solution)/shard_map/ppermute | solution.py:23
  91.9 6.5 %collective-permute-start.9 = (f32[2,2,1,4096]{3,2,1,0:T(1,128)S(1)}, f32[2,2,1,4096]{3,2,1,0:T(1,128)S(1)}, u32[]{:S(2)}, u32[]{:S(2)}) collective-permute-start(f32[2,2,1,4096]{3,2,1,0:T(1,128)S(1)} %get-tuple-element.43), channel_id=1, source_target_pairs={{0,1},{1,2},{2,3},{3,4},{4,5},{5,6},{6,7},{8,9},{9,10},{10,11},{11... | collective-permute-start | bytes 196616 | tf_op jit(solution)/shard_map/ppermute | solution.py:20
  100.9 4.5 %collective-permute-start.10 = (f32[2,2,1,4096]{3,2,1,0:T(1,128)S(1)}, f32[2,2,1,4096]{3,2,1,0:T(1,128)S(1)}, u32[]{:S(2)}, u32[]{:S(2)}) collective-permute-start(f32[2,2,1,4096]{3,2,1,0:T(1,128)S(1)} %get-tuple-element.40), channel_id=1, source_target_pairs={{1,0},{2,1},{3,2},{4,3},{5,4},{6,5},{7,6},{9,8},{10,9},{11,10},{12... | collective-permute-start | bytes 196616 | tf_op jit(solution)/shard_map/ppermute | solution.py:23
  102.8 9.0 %copy-start.1 = (f32[2,64,4096]{2,1,0:T(8,128)S(1)}, f32[2,64,4096]{2,1,0:T(8,128)}, u32[]{:S(2)}) copy-start(f32[2,64,4096]{2,1,0:T(8,128)} %copy-done) | copy-start | bytes 6291460
  102.8 6.6 %collective-permute-start.11 = (f32[2,2,1,4096]{3,2,1,0:T(1,128)S(1)}, f32[2,2,1,4096]{3,2,1,0:T(1,128)S(1)}, u32[]{:S(2)}, u32[]{:S(2)}) collective-permute-start(f32[2,2,1,4096]{3,2,1,0:T(1,128)S(1)} %get-tuple-element.41), channel_id=1, source_target_pairs={{0,1},{1,2},{2,3},{3,4},{4,5},{5,6},{6,7},{8,9},{9,10},{10,11},{11... | collective-permute-start | bytes 196616 | tf_op jit(solution)/shard_map/ppermute | solution.py:20
  112.9 22.3 %collective-permute-start.12 = (f32[1,64,4096]{2,1,0:T(8,128)S(1)}, f32[1,64,4096]{2,1,0:T(8,128)S(1)}, u32[]{:S(2)}, u32[]{:S(2)}) collective-permute-start(f32[1,64,4096]{2,1,0:T(8,128)S(1)} %get-tuple-element.46), channel_id=1, source_target_pairs={{0,8},{8,16},{16,24},{1,9},{9,17},{17,25},{2,10},{10,18},{18,26},{... | collective-permute-start | bytes 3145736 | tf_op jit(solution)/shard_map/ppermute | solution.py:20
  115.5 23.9 %collective-permute-start.13 = (f32[1,64,4096]{2,1,0:T(8,128)S(1)}, f32[1,64,4096]{2,1,0:T(8,128)S(1)}, u32[]{:S(2)}, u32[]{:S(2)}) collective-permute-start(f32[1,64,4096]{2,1,0:T(8,128)S(1)} %get-tuple-element.47), channel_id=1, source_target_pairs={{8,0},{16,8},{24,16},{9,1},{17,9},{25,17},{10,2},{18,10},{26,18},{... | collective-permute-start | bytes 3145736 | tf_op jit(solution)/shard_map/ppermute | solution.py:23
  146.2 5.1 %collective-permute-start.14 = (f32[2,2,1,4096]{3,2,1,0:T(1,128)S(1)}, f32[2,2,1,4096]{3,2,1,0:T(1,128)S(1)}, u32[]{:S(2)}, u32[]{:S(2)}) collective-permute-start(f32[2,2,1,4096]{3,2,1,0:T(1,128)S(1)} %get-tuple-element.38), channel_id=1, source_target_pairs={{1,0},{2,1},{3,2},{4,3},{5,4},{6,5},{7,6},{9,8},{10,9},{11,10},{12... | collective-permute-start | bytes 196616 | tf_op jit(solution)/shard_map/ppermute | solution.py:23
  149.3 6.5 %collective-permute-start.15 = (f32[2,2,1,4096]{3,2,1,0:T(1,128)S(1)}, f32[2,2,1,4096]{3,2,1,0:T(1,128)S(1)}, u32[]{:S(2)}, u32[]{:S(2)}) collective-permute-start(f32[2,2,1,4096]{3,2,1,0:T(1,128)S(1)} %get-tuple-element.39), channel_id=1, source_target_pairs={{0,1},{1,2},{2,3},{3,4},{4,5},{5,6},{6,7},{8,9},{9,10},{10,11},{11... | collective-permute-start | bytes 196616 | tf_op jit(solution)/shard_map/ppermute | solution.py:20
  158.2 4.3 %collective-permute-start.16 = (f32[2,2,1,4096]{3,2,1,0:T(1,128)S(1)}, f32[2,2,1,4096]{3,2,1,0:T(1,128)S(1)}, u32[]{:S(2)}, u32[]{:S(2)}) collective-permute-start(f32[2,2,1,4096]{3,2,1,0:T(1,128)S(1)} %get-tuple-element.36), channel_id=1, source_target_pairs={{1,0},{2,1},{3,2},{4,3},{5,4},{6,5},{7,6},{9,8},{10,9},{11,10},{12... | collective-permute-start | bytes 196616 | tf_op jit(solution)/shard_map/ppermute | solution.py:23
  160.2 6.5 %collective-permute-start.17 = (f32[2,2,1,4096]{3,2,1,0:T(1,128)S(1)}, f32[2,2,1,4096]{3,2,1,0:T(1,128)S(1)}, u32[]{:S(2)}, u32[]{:S(2)}) collective-permute-start(f32[2,2,1,4096]{3,2,1,0:T(1,128)S(1)} %get-tuple-element.37), channel_id=1, source_target_pairs={{0,1},{1,2},{2,3},{3,4},{4,5},{5,6},{6,7},{8,9},{9,10},{10,11},{11... | collective-permute-start | bytes 196616 | tf_op jit(solution)/shard_map/ppermute | solution.py:20
  169.1 4.3 %collective-permute-start.18 = (f32[2,2,1,4096]{3,2,1,0:T(1,128)S(1)}, f32[2,2,1,4096]{3,2,1,0:T(1,128)S(1)}, u32[]{:S(2)}, u32[]{:S(2)}) collective-permute-start(f32[2,2,1,4096]{3,2,1,0:T(1,128)S(1)} %get-tuple-element.34), channel_id=1, source_target_pairs={{1,0},{2,1},{3,2},{4,3},{5,4},{6,5},{7,6},{9,8},{10,9},{11,10},{12... | collective-permute-start | bytes 196616 | tf_op jit(solution)/shard_map/ppermute | solution.py:23
  171.1 6.5 %collective-permute-start.19 = (f32[2,2,1,4096]{3,2,1,0:T(1,128)S(1)}, f32[2,2,1,4096]{3,2,1,0:T(1,128)S(1)}, u32[]{:S(2)}, u32[]{:S(2)}) collective-permute-start(f32[2,2,1,4096]{3,2,1,0:T(1,128)S(1)} %get-tuple-element.35), channel_id=1, source_target_pairs={{0,1},{1,2},{2,3},{3,4},{4,5},{5,6},{6,7},{8,9},{9,10},{10,11},{11... | collective-permute-start | bytes 196616 | tf_op jit(solution)/shard_map/ppermute | solution.py:20
  (2 other events, 3.5 us)
where the time goes:
time: 182 us; the launch traced here: 181 us
  waiting for transfers between devices  76.4 us (42%)
  starting transfers between devices  51.5 us (28%)
  other arithmetic  37.9 us (21%)
  local copies, waits for them, and re-layouts  14.9 us (8%)
    ppermute x10, waiting for transfers between devices, padded_2(): lax.ppermute(lax.slice_in_dim(block, block.shape[dim] - width, None, axis...  65.5 us
    ppermute x10, starting transfers between devices, padded_2(): lax.ppermute(lax.slice_in_dim(block, 0, width, axis=dim), axis, backward)  27 us
    ppermute x10, starting transfers between devices, padded_2(): lax.ppermute(lax.slice_in_dim(block, block.shape[dim] - width, None, axis...  24.5 us
    add x6, other arithmetic, relax_rows(): interior + relax_rate * (padded[:, :, 2:] + padded[:, :, :-2] + beside[.....  15.4 us
    ppermute x10, waiting for transfers between devices, padded_2(): lax.ppermute(lax.slice_in_dim(block, 0, width, axis=dim), axis, backward)  10.9 us
    gather x6, local copies, waits for them, and re-layouts  8.33 us
    another operation x4, other arithmetic, local(): jnp.stack([coupling * grad_rows, coupling * grad_cols], axis=1)  7.71 us
    add x2, other arithmetic, local(): current_field + force_scale * jnp.stack([coupling * grad_rows, coupling *...  5.09 us
  transfers between devices with their start and end apart: 20, of which 13 were waited for; matrix products, arithmetic and copies ran while one was open for 1% of the time, Pallas kernels for 0%

commit v1 on v0

v1 whole, which is shorter than its diff:
```python
import functools

import jax
import jax.numpy as jnp
from jax import lax
from jax.experimental import pallas as pl
from jax.experimental.pallas import tpu as pltpu
from jax.sharding import PartitionSpec as P


relax_scale = 0.2 ** 3
softening = 0.25
F32 = jnp.float32
REACH = 12
BELOW = 6
PACKED = REACH + 2 * BELOW
LANES = 128
ROWS = 8
VMEM_LIMIT = 32 * 1024 * 1024


def iotas():
    return (
        lax.broadcasted_iota(jnp.int32, (ROWS, LANES), 0),
        lax.broadcasted_iota(jnp.int32, (ROWS, LANES), 1),
    )


def cols(j):
    return slice(j * LANES, (j + 1) * LANES)


def tile(i):
    if isinstance(i, int):
        return slice(i * ROWS, (i + 1) * ROWS)
    return pl.ds(pl.multiple_of(i * ROWS, ROWS), ROWS)


def row_before(here, above, row):
    return pltpu.roll(jnp.where(row == ROWS - 1, above, here), 1, 0)


def row_after(here, below, row):
    return pltpu.roll(jnp.where(row == 0, below, here), ROWS - 1, 0)


def col_before(here, left, lane):
    return pltpu.roll(jnp.where(lane == LANES - 1, left, here), 1, 1)


def col_after(here, right, lane):
    return pltpu.roll(jnp.where(lane == 0, right, here), LANES - 1, 1)


def plus_sum(up, here, down, left, right, row, lane):
    return (
        here
        + (row_before(here, up, row) + row_after(here, down, row))
        + (col_before(here, left, lane) + col_after(here, right, lane))
    )


def warp_tile(source, base, shift, line, store, columns):
    row, lane = iotas()
    row_shift, col_shift, row_part, col_part = shift
    first = base + jnp.where(row_shift < 0, -1, 0)
    within = jnp.where(row_shift < 0, row_shift + ROWS, row_shift)
    turn = jnp.where(within == 0, 0, ROWS - within)
    turn_next = ROWS - 1 - within
    for j in range(columns):
        a, b = source(first, j), source(first + 1, j)
        upper = pltpu.roll(jnp.where(row < within, b, a), turn, 0)
        lower = pltpu.roll(jnp.where(row < within + 1, b, a), turn_next, 0)
        line[:, cols(j + 1)] = (1.0 - row_part) * upper + row_part * lower
    start = jnp.where(col_shift < 0, 0, 1)
    side = jnp.where(col_shift < 0, col_shift + LANES, col_shift)
    back = jnp.where(side == 0, 0, LANES - side)

    def block(j):
        return line[:, pl.ds(pl.multiple_of((start + j) * LANES, LANES), LANES)]

    def moved(j):
        return pltpu.roll(jnp.where(lane < side, block(j + 1), block(j)), back, 1)

    here = moved(0)
    for j in range(columns):
        after = moved(j + 1)
        store(j, (1.0 - col_part) * here + col_part * col_after(here, after, lane))
        here = after


def clear_line(line, columns):
    zero = jnp.zeros((ROWS, LANES), F32)
    for j in (0, columns + 1, columns + 2):
        line[:, cols(j)] = zero


def gradients(get, i, columns, body):
    row, lane = iotas()
    zero = jnp.zeros((ROWS, LANES), F32)
    left, here = zero, get(i, 0)
    for j in range(columns):
        right = get(i, j + 1) if j + 1 < columns else zero
        grad_rows = 0.5 * (row_after(here, get(i + 1, j), row) - row_before(here, get(i - 1, j), row))
        grad_cols = 0.5 * (col_after(here, right, lane) - col_before(here, left, lane))
        body(j, here, grad_rows, grad_cols)
        left, here = here, right


def sweep(get, i, columns, body):
    row, lane = iotas()
    zero = jnp.zeros((ROWS, LANES), F32)
    left, here = zero, get(i, 0)
    for j in range(columns):
        right = get(i, j + 1) if j + 1 < columns else zero
        body(j, plus_sum(get(i - 1, j), here, get(i + 1, j), left, right, row, lane))
        left, here = here, right


def force(linear, lower, upper, grad_rows, grad_cols, weight_lower, weight_upper):
    denominator = grad_rows * grad_rows + grad_cols * grad_cols + softening
    lower_diff = lower - linear
    upper_diff = upper - linear
    below = denominator + lower_diff * lower_diff
    above = denominator + upper_diff * upper_diff
    top = (weight_lower * lower_diff) * above + (weight_upper * upper_diff) * below
    bottom = below * above
    inverse = pl.reciprocal(bottom, approx=True)
    inverse = inverse * (2.0 - bottom * inverse)
    return top * inverse


def half_weights(weights_ref, s, sections):
    number = lax.axis_index("sec") * sections + s
    lower = jnp.where(number > 0, weights_ref[s, 0], 0).astype(F32) * 0.5
    upper = jnp.where(number < sections * lax.axis_size("sec") - 1, weights_ref[s, 1], 0).astype(F32) * 0.5
    return lower, upper


def shift_of(offsets_ref, fractions_ref, s):
    return (
        offsets_ref[s, 0, 0],
        offsets_ref[s, 0, 1],
        fractions_ref[s, 0, 0].astype(F32) * (1.0 / 256.0),
        fractions_ref[s, 0, 1].astype(F32) * (1.0 / 256.0),
    )


def copy_in(pairs, sems):
    copies = [pltpu.make_async_copy(a, b, sems.at[k]) for k, (a, b) in enumerate(pairs)]
    for copy in copies:
        copy.start()
    return copies


def pack_kernel(offsets, fractions, sec_top, sec_end, field_top, field_end, to_next, to_last):
    sections, _, width = sec_top.shape
    _, lane = iotas()
    lane = lane[:1]
    for s in range(sections):
        values = jnp.zeros((1, LANES), F32)
        for k, value in enumerate(
            (offsets[s, 0, 0], offsets[s, 0, 1], fractions[s, 0, 0], fractions[s, 0, 1])
        ):
            values = jnp.where(lane == k, value.astype(F32), values)
        values = jnp.broadcast_to(values, (PACKED, LANES))
        last = sec_end.shape[1]
        to_next[s, :REACH, :width] = sec_end[s, last - REACH :, :]
        to_last[s, :REACH, :width] = sec_top[s, :REACH, :]
        for c in range(2):
            rows = slice(REACH + c * BELOW, REACH + (c + 1) * BELOW)
            to_next[s, rows, :width] = field_end[s, c, ROWS - BELOW :, :]
            to_last[s, rows, :width] = field_top[s, c, :BELOW, :]
        to_next[s, :, width:] = values
        to_last[s, :, width:] = values


def pack(sections, displacement, offsets, fractions):
    count, rows, width = sections.shape
    smem = pl.BlockSpec(memory_space=pltpu.SMEM)
    shape = jax.ShapeDtypeStruct((count, PACKED, width + LANES), F32)
    return pl.pallas_call(
        pack_kernel,
        grid=(1,),
        out_shape=[shape, shape],
        in_specs=[
            smem,
            smem,
            pl.BlockSpec((count, 16, width), lambda i: (0, 0, 0)),
            pl.BlockSpec((count, 16, width), lambda i: (0, rows // 16 - 1, 0)),
            pl.BlockSpec((count, 2, ROWS, width), lambda i: (0, 0, 0, 0)),
            pl.BlockSpec((count, 2, ROWS, width), lambda i: (0, 0, rows // ROWS - 1, 0)),
        ],
        out_specs=[pl.BlockSpec(shape.shape, lambda i: (0, 0, 0))] * 2,
        compiler_params=pltpu.CompilerParams(vmem_limit_bytes=VMEM_LIMIT),
        name="pack",
    )(offsets, fractions, sections, sections, displacement, displacement)


def first_inner_kernel(
    offsets, fractions, sections, field, warped, grow, gcol, linear, inner_field, *rest
):
    count, inner, width = linear.shape
    to_low, to_high, plane, line, whole, sems = rest
    columns = width // LANES
    rows = sections.shape[1]
    tiles = rows // ROWS
    loads = copy_in(
        [(sections.at[s], plane.at[s, pl.ds(ROWS, rows)]) for s in range(count)]
        + [
            (field.at[s, c, pl.ds(ROWS, inner)], inner_field.at[s, c])
            for s in range(count)
            for c in range(2)
        ],
        sems,
    )
    clear_line(line, columns)
    zero = jnp.zeros((ROWS, LANES), F32)
    for s in range(count):
        for j in range(columns):
            plane[s, :ROWS, cols(j)] = zero
            plane[s, rows + ROWS :, cols(j)] = zero
    stores = []
    for s in range(count):
        loads[s].wait()
        shift = shift_of(offsets, fractions, s)

        def warp(i, carry):
            def store(j, value):
                whole[s, tile(i), cols(j)] = value

            warp_tile(lambda k, j: plane[s, tile(k), cols(j)], i + 1, shift, line, store, columns)
            return carry

        lax.fori_loop(0, tiles, warp, 0)
        loads[count + 2 * s].wait()
        loads[count + 2 * s + 1].wait()

        def derive(i, carry):
            def body(j, here, grad_rows, grad_cols):
                at = (s, tile(i - 1), cols(j))
                warped[at] = here
                grow[at] = grad_rows
                gcol[at] = grad_cols
                linear[at] = (
                    here
                    + inner_field[s, 0, tile(i - 1), cols(j)] * grad_rows
                    + inner_field[s, 1, tile(i - 1), cols(j)] * grad_cols
                )

            gradients(lambda k, j: whole[s, tile(k), cols(j)], i, columns, body)
            return carry

        lax.fori_loop(1, tiles - 1, derive, 0)
        for end, target, sem in ((0, to_low, 0), (count - 1, to_high, 1)):
            if s == end:
                copy = pltpu.make_async_copy(linear.at[s], target.at[0], sems.at[3 * count + sem])
                copy.start()
                stores.append(copy)
    for copy in stores:
        copy.wait()


def vmem(*shape):
    return pltpu.VMEM(shape, F32)


def hbm(*shape):
    return jax.ShapeDtypeStruct(shape, F32)


SPEC_SMEM = pl.BlockSpec(memory_space=pltpu.SMEM)
SPEC_VMEM = pl.BlockSpec(memory_space=pltpu.VMEM)
SPEC_ANY = pl.BlockSpec(memory_space=pl.ANY)


def run(kernel, name, ins, outs, scratch, cost, aliases=None):
    def spec(kind):
        return {"s": SPEC_SMEM, "v": SPEC_VMEM, "a": SPEC_ANY}[kind]

    return pl.pallas_call(
        kernel,
        out_shape=[shape for _, shape in outs],
        in_specs=[spec(kind) for kind, _ in ins],
        out_specs=[spec(kind) for kind, _ in outs],
        scratch_shapes=scratch,
        input_output_aliases=aliases or {},
        cost_estimate=pl.CostEstimate(flops=cost, bytes_accessed=cost, transcendentals=0),
        compiler_params=pltpu.CompilerParams(vmem_limit_bytes=VMEM_LIMIT),
        name=name,
    )(*[value for _, value in ins])


def first_edge_kernel(
    offsets, fractions, sections, field, from_last, from_next, inner_warped,
    warped, grow, gcol, linear, edge_field, to_low, to_high,
    received, plane, line, whole, sems,
):
    count, _, width = linear.shape
    columns = width // LANES
    rows = sections.shape[1]
    row, lane = iotas()
    reach = 2 * ROWS
    pairs = []
    for side, source in ((0, from_last), (1, from_next)):
        pairs.append((source, received.at[side]))
    for s in range(count):
        pairs.append((sections.at[s, pl.ds(0, reach)], plane.at[s, 0, pl.ds(reach, reach)]))
        pairs.append((sections.at[s, pl.ds(rows - reach, reach)], plane.at[s, 1, pl.ds(0, reach)]))
        for c in range(2):
            pairs.append((field.at[s, c, pl.ds(0, ROWS)], edge_field.at[s, c, pl.ds(ROWS, ROWS)]))
            pairs.append(
                (field.at[s, c, pl.ds(rows - ROWS, ROWS)], edge_field.at[s, c, pl.ds(2 * ROWS, ROWS)])
            )
    loads = copy_in(pairs, sems)
    clear_line(line, columns)
    for copy in loads:
        copy.wait()
    zero = jnp.zeros((ROWS, LANES), F32)
    stores = []
    for s in range(count):
        for j in range(columns):
            plane[s, 0, :ROWS, cols(j)] = zero
            plane[s, 1, 3 * ROWS :, cols(j)] = zero
            for c in range(2):
                edge_field[s, c, :ROWS, cols(j)] = zero
                edge_field[s, c, 3 * ROWS :, cols(j)] = zero
        plane[s, 0, reach - REACH : reach, :] = received[0, s, :REACH, :width]
        plane[s, 1, reach : reach + REACH, :] = received[1, s, :REACH, :width]
        for c in range(2):
            part = slice(REACH + c * BELOW, REACH + (c + 1) * BELOW)
            edge_field[s, c, ROWS - BELOW : ROWS, :] = received[0, s, part, :width]
            edge_field[s, c, 3 * ROWS : 3 * ROWS + BELOW, :] = received[1, s, part, :width]
        own = shift_of(offsets, fractions, s)

        def theirs(side):
            block = received[side, s, 0:1, width:]
            one = lane[:1]
            values = [jnp.sum(jnp.where(one == k, block, 0.0)) for k in range(4)]
            return (
                values[0].astype(jnp.int32),
                values[1].astype(jnp.int32),
                values[2] * (1.0 / 256.0),
                values[3] * (1.0 / 256.0),
            )

        for side in range(2):
            other = theirs(side)
            shifts = (other, own) if side == 0 else (own, other)
            if side == 0:
                inside = inner_warped[s, :ROWS, :]
                whole[3 * ROWS : 4 * ROWS, :] = inside
            else:
                inside = inner_warped[s, inner_warped.shape[1] - ROWS :, :]
                whole[0:ROWS, :] = inside

            def warp(i, carry):
                shift = tuple(jnp.where(i == 1, a, b) for a, b in zip(*shifts))

                def store(j, value):
                    whole[tile(i), cols(j)] = value

                warp_tile(lambda k, j: plane[s, side, tile(k), cols(j)], i, shift, line, store, columns)
                return carry

            lax.fori_loop(1, 3, warp, 0)
            outer = slice(0, ROWS) if side == 0 else slice(3 * ROWS, 4 * ROWS)
            for j in range(columns):
                whole[outer, cols(j)] = zero

            def derive(i, carry):
                def body(j, here, grad_rows, grad_cols):
                    at = (s, tile(2 * side + i - 1), cols(j))
                    warped[at] = here
                    grow[at] = grad_rows
                    gcol[at] = grad_cols
                    u = edge_field[s, 0, tile(2 * side + i - 1), cols(j)]
                    v = edge_field[s, 1, tile(2 * side + i - 1), cols(j)]
                    linear[at] = here + u * grad_rows + v * grad_cols

                gradients(lambda k, j: whole[tile(k), cols(j)], i, columns, body)
                return carry

            lax.fori_loop(1, 3, derive, 0)
        for end, target, sem in ((0, to_low, 0), (count - 1, to_high, 1)):
            if s == end:
                copy = pltpu.make_async_copy(linear.at[s], target.at[0], sems.at[sem])
                copy.start()
                stores.append(copy)
    for copy in stores:
        copy.wait()


def inner_kernel(count, skip, last, *refs):
    if last:
        (weights, from_low, from_high, linear, grow, gcol, field,
         moved, result, low, high, work, spare, stage, sems) = refs
    else:
        (weights, from_low, from_high, linear, grow, gcol, field, warped,
         moved, next_field, next_linear, to_low, to_high, low, high, work, spare, sems) = refs
    _, rows, width = linear.shape
    tiles = rows // ROWS
    columns = width // LANES
    loads = copy_in([(from_low.at[0], low), (from_high.at[0], high)], sems)
    zero = jnp.zeros((ROWS, LANES), F32)
    stores = []
    for ref in (work, spare):
        for c in range(2):
            for j in range(columns):
                ref[c, :ROWS, cols(j)] = zero
                ref[c, (tiles + 1) * ROWS :, cols(j)] = zero
    for copy in loads:
        copy.wait()
    for s in range(count):
        weight_lower, weight_upper = half_weights(weights, s, count)

        def move(i, carry):
            for j in range(columns):
                at = (tile(i), cols(j))
                lower = low[at] if s == 0 else linear[(s - 1,) + at]
                upper = high[at] if s == count - 1 else linear[(s + 1,) + at]
                grad_rows = grow[s, tile(i + skip), cols(j)]
                grad_cols = gcol[s, tile(i + skip), cols(j)]
                half = force(
                    linear[(s,) + at], lower, upper, grad_rows, grad_cols, weight_lower, weight_upper
                )
                u = field[s, 0, tile(i), cols(j)] + half * grad_rows
                v = field[s, 1, tile(i), cols(j)] + half * grad_cols
                moved[s, 0, tile(i), cols(j)] = u
                moved[s, 1, tile(i), cols(j)] = v
                work[0, tile(i + 1), cols(j)] = u
                work[1, tile(i + 1), cols(j)] = v
            return carry

        lax.fori_loop(0, tiles, move, 0)
        for source, target in ((work, spare), (spare, work)):

            def relax(i, carry):
                for c in range(2):

                    def body(j, value):
                        target[c, tile(i), cols(j)] = value

                    sweep(lambda k, j: source[c, tile(k), cols(j)], i, columns, body)
                return carry

            lax.fori_loop(1, tiles + 1, relax, 0)

        def finish(i, carry):
            for c in range(2):

                def body(j, value):
                    if last:
                        stage[s, c, tile(i - 2), cols(j)] = value * relax_scale
                    else:
                        next_field[s, c, tile(i - 2), cols(j)] = value * relax_scale

                sweep(lambda k, j: work[c, tile(k), cols(j)], i, columns, body)
            if not last:
                for j in range(columns):
                    at = (s, tile(i - 2), cols(j))
                    there = (s, tile(i - 1), cols(j))
                    next_linear[at] = (
                        warped[there]
                        + next_field[s, 0, tile(i - 2), cols(j)] * grow[there]
                        + next_field[s, 1, tile(i - 2), cols(j)] * gcol[there]
                    )
            return carry

        lax.fori_loop(2, tiles, finish, 0)
        if last:
            inside = rows - 2 * ROWS
            start = (result.shape[2] - inside) // 2
            for c in range(2):
                copy = pltpu.make_async_copy(
                    stage.at[s, c], result.at[s, c, pl.ds(start, inside)], sems.at[2 + 2 * s + c]
                )
                copy.start()
                stores.append(copy)
        else:
            for end, target, sem in ((0, to_low, 2), (count - 1, to_high, 3)):
                if s == end:
                    copy = pltpu.make_async_copy(next_linear.at[s], target.at[0], sems.at[sem])
                    copy.start()
                    stores.append(copy)
    for copy in stores:
        copy.wait()


def edge_kernel(count, last, *refs):
    if last:
        (weights, from_low, from_high, linear, edge_grow, edge_gcol, grow, gcol, field, inner_moved, _,
         result, low, high, work, spare, stage, sems) = refs
        outer = 3
    else:
        (weights, from_low, from_high, linear, edge_grow, edge_gcol, edge_warped, grow, gcol, warped,
         field, inner_moved,
         next_field, next_linear, to_low, to_high, low, high, work, spare, sems) = refs
        outer = 2
    beside = 2
    total = outer + beside
    width = linear.shape[2]
    columns = width // LANES
    inner_tiles = inner_moved.shape[2] // ROWS
    grad_tiles = grow.shape[1] // ROWS
    got = pl.ds(0, from_low.shape[1])
    loads = copy_in([(from_low.at[0], low.at[got]), (from_high.at[0], high.at[got])], sems)
    zero = jnp.zeros((ROWS, LANES), F32)
    stores = []
    for ref in (work, spare):
        for c in range(2):
            for j in range(columns):
                ref[c, :ROWS, cols(j)] = zero
                ref[c, (total + 1) * ROWS :, cols(j)] = zero
    for copy in loads:
        copy.wait()
    strip = lax.axis_index("tile")
    inside = (
        jnp.where(strip > 0, 1.0, 0.0).astype(F32),
        jnp.where(strip < lax.axis_size("tile") - 1, 1.0, 0.0).astype(F32),
    )
    if last:
        misc = 4 * ROWS
        for ref in (low, high):
            ref[5 * ROWS : 6 * ROWS, :] = jnp.concatenate(
                [ref[misc + 3 : misc + 6, :], jnp.zeros((5, width), F32)], axis=0
            )
            ref[misc : misc + ROWS, :] = jnp.concatenate(
                [jnp.zeros((5, width), F32), ref[misc : misc + 3, :]], axis=0
            )

    def gradient(ref, edge_ref, s, side, k, j):
        if last:
            if side == 0:
                return edge_ref[s, tile(k), cols(j)] if k < 2 else ref[s, tile(0), cols(j)]
            return ref[s, tile(grad_tiles - 1), cols(j)] if k == 0 else edge_ref[s, tile(k + 1), cols(j)]
        return edge_ref[s, tile(2 * side + k), cols(j)]

    def place(side, k):
        if last:
            return (4, 0, 1)[k] if side == 0 else (2, 3, 5)[k]
        return 2 * side + k

    for s in range(count):
        weight_lower, weight_upper = half_weights(weights, s, count)
        for side in range(2):
            ahead = 1 if side == 0 else 1 + beside
            halo = 1 if side == 0 else total
            aside = 1 + outer if side == 0 else 1
            for k in range(outer):
                mine = outer * side + k
                there = place(side, k)
                for j in range(columns):
                    at = (tile(mine), cols(j))
                    lower = low[tile(there), cols(j)] if s == 0 else linear[(s - 1,) + at]
                    upper = high[tile(there), cols(j)] if s == count - 1 else linear[(s + 1,) + at]
                    grad_rows = gradient(grow, edge_grow, s, side, k, j)
                    grad_cols = gradient(gcol, edge_gcol, s, side, k, j)
                    half = force(
                        linear[(s,) + at], lower, upper, grad_rows, grad_cols, weight_lower, weight_upper
                    )
                    u = field[s, 0, tile(mine), cols(j)] + half * grad_rows
                    v = field[s, 1, tile(mine), cols(j)] + half * grad_cols
                    if ahead + k == halo:
                        u, v = u * inside[side], v * inside[side]
                    work[0, tile(ahead + k), cols(j)] = u
                    work[1, tile(ahead + k), cols(j)] = v
            first = 0 if side == 0 else inner_tiles - beside
            for c in range(2):
                for k in range(beside):
                    for j in range(columns):
                        work[c, tile(aside + k), cols(j)] = inner_moved[s, c, tile(first + k), cols(j)]
            for source, target in ((work, spare), (spare, work)):

                def relax(i, carry):
                    factor = jnp.where(i == halo, inside[side], 1.0)
                    for c in range(2):

                        def body(j, value):
                            target[c, tile(i), cols(j)] = value * factor

                        sweep(lambda k, j: source[c, tile(k), cols(j)], i, columns, body)
                    return carry

                lax.fori_loop(1, total + 1, relax, 0)

            if last:
                start = 2
                goal = 0 if side == 0 else result.shape[2] - 3 * ROWS

                def finish(i, carry):
                    for c in range(2):

                        def body(j, value):
                            stage[s, side, c, tile(i - start), cols(j)] = value * relax_scale

                        sweep(lambda k, j: work[c, tile(k), cols(j)], i, columns, body)
                    return carry

                lax.fori_loop(start, start + 3, finish, 0)
                for c in range(2):
                    copy = pltpu.make_async_copy(
                        stage.at[s, side, c],
                        result.at[s, c, pl.ds(goal, 3 * ROWS)],
                        sems.at[2 + 4 * s + 2 * side + c],
                    )
                    copy.start()
                    stores.append(copy)
            else:
                start = 1 if side == 0 else 2
                for k in range(3):
                    i = start + k
                    factor = inside[side] * relax_scale if i == halo else relax_scale
                    at_next = 3 * side + k
                    outer_k = k if side == 0 else k - 1
                    for c in range(2):

                        def body(j, value):
                            next_field[s, c, tile(at_next), cols(j)] = value * factor

                        sweep(lambda q, j: work[c, tile(q), cols(j)], i, columns, body)
                    for j in range(columns):
                        if 0 <= outer_k < 2:
                            there = (s, tile(2 * side + outer_k), cols(j))
                            parts = edge_warped[there], edge_grow[there], edge_gcol[there]
                        else:
                            there = (s, tile(0 if side == 0 else grad_tiles - 1), cols(j))
                            parts = warped[there], grow[there], gcol[there]
                        next_linear[s, tile(at_next), cols(j)] = (
                            parts[0]
                            + next_field[s, 0, tile(at_next), cols(j)] * parts[1]
                            + next_field[s, 1, tile(at_next), cols(j)] * parts[2]
                        )
    if not last:
        for end, target, stage, sem in ((0, to_low, low, 2), (count - 1, to_high, high, 3)):
            stage[: 2 * ROWS, :] = next_linear[end, ROWS : 3 * ROWS, :]
            stage[2 * ROWS : 4 * ROWS, :] = next_linear[end, 3 * ROWS : 5 * ROWS, :]
            stage[4 * ROWS : 5 * ROWS, :] = jnp.concatenate(
                [
                    next_linear[end, ROWS - 3 : ROWS, :],
                    next_linear[end, 5 * ROWS : 5 * ROWS + 3, :],
                    jnp.zeros((2, width), F32),
                ],
                axis=0,
            )
            copy = pltpu.make_async_copy(stage.at[pl.ds(0, 5 * ROWS)], target.at[0], sems.at[sem])
            copy.start()
            stores.append(copy)
    for copy in stores:
        copy.wait()


def exchange(low, high, axis):
    count = lax.axis_size(axis)
    forward = [(i, i + 1) for i in range(count - 1)]
    backward = [(i + 1, i) for i in range(count - 1)]
    return lax.ppermute(high, axis, forward), lax.ppermute(low, axis, backward)


def local(sections, displacement, offsets, fractions, weights):
    count, rows, width = sections.shape
    inner = rows - 2 * ROWS
    core = inner - 2 * ROWS
    sem = pltpu.SemaphoreType.DMA
    v, a, s = "v", "a", "s"

    warped, grow, gcol, linear, field, to_low, to_high = run(
        first_inner_kernel,
        "first_inner",
        [(s, offsets), (s, fractions), (a, sections), (a, displacement)],
        [(v, vmem(count, inner, width))] * 4
        + [(v, vmem(count, 2, inner, width))]
        + [(a, hbm(1, inner, width))] * 2,
        [
            vmem(count, rows + 2 * ROWS, width),
            vmem(ROWS, width + 3 * LANES),
            vmem(count, rows, width),
            sem((3 * count + 2,)),
        ],
        8_000_000,
    )
    low_1, high_1 = exchange(to_low, to_high, "sec")

    to_next, to_last = pack(sections, displacement, offsets, fractions)
    from_last, from_next = exchange(to_last, to_next, "tile")
    edge_warped, edge_grow, edge_gcol, edge_linear, edge_field, to_low, to_high = run(
        first_edge_kernel,
        "first_edge",
        [
            (s, offsets), (s, fractions), (a, sections), (a, displacement),
            (a, from_last), (a, from_next), (v, warped),
        ],
        [(v, vmem(count, 4 * ROWS, width))] * 4
        + [(v, vmem(count, 2, 4 * ROWS, width))]
        + [(a, hbm(1, 4 * ROWS, width))] * 2,
        [
            vmem(2, count, PACKED, width + LANES),
            vmem(count, 2, 4 * ROWS, width),
            vmem(ROWS, width + 3 * LANES),
            vmem(4 * ROWS, width),
            sem((2 + 6 * count,)),
        ],
        5_000_000,
    )
    low_2, high_2 = exchange(to_low, to_high, "sec")

    moved, next_field, next_linear, to_low, to_high = run(
        functools.partial(inner_kernel, count, 0, False),
        "inner",
        [
            (s, weights), (a, low_1), (a, high_1), (v, linear), (v, grow), (v, gcol), (v, field), (v, warped),
        ],
        [
            (v, vmem(count, 2, inner, width)),
            (v, vmem(count, 2, core, width)),
            (v, vmem(count, core, width)),
            (a, hbm(1, core, width)),
            (a, hbm(1, core, width)),
        ],
        [
            vmem(inner, width),
            vmem(inner, width),
            vmem(2, inner + 2 * ROWS, width),
            vmem(2, inner + 2 * ROWS, width),
            sem((4,)),
        ],
        8_000_000,
    )
    low_3, high_3 = exchange(to_low, to_high, "sec")

    edge_field, edge_linear, to_low, to_high = run(
        functools.partial(edge_kernel, count, False),
        "edge",
        [
            (s, weights), (a, low_2), (a, high_2), (v, edge_linear), (v, edge_grow), (v, edge_gcol),
            (v, edge_warped), (v, grow), (v, gcol), (v, warped), (v, edge_field), (v, moved),
        ],
        [
            (v, vmem(count, 2, 6 * ROWS, width)),
            (v, vmem(count, 6 * ROWS, width)),
            (a, hbm(1, 5 * ROWS, width)),
            (a, hbm(1, 5 * ROWS, width)),
        ],
        [
            vmem(5 * ROWS, width),
            vmem(5 * ROWS, width),
            vmem(2, 6 * ROWS, width),
            vmem(2, 6 * ROWS, width),
            sem((4,)),
        ],
        8_000_000,
    )
    low_4, high_4 = exchange(to_low, to_high, "sec")

    moved, result = run(
        functools.partial(inner_kernel, count, 1, True),
        "last_inner",
        [(s, weights), (a, low_3), (a, high_3), (v, next_linear), (v, grow), (v, gcol), (v, next_field)],
        [(v, vmem(count, 2, core, width)), (a, hbm(count, 2, rows, width))],
        [
            vmem(core, width),
            vmem(core, width),
            vmem(2, core + 2 * ROWS, width),
            vmem(2, core + 2 * ROWS, width),
            vmem(count, 2, core - 2 * ROWS, width),
            sem((2 + 2 * count,)),
        ],
        8_000_000,
    )
    (result,) = run(
        functools.partial(edge_kernel, count, True),
        "last_edge",
        [
            (s, weights), (a, low_4), (a, high_4), (v, edge_linear), (v, edge_grow), (v, edge_gcol),
            (v, grow), (v, gcol), (v, edge_field), (v, moved), (a, result),
        ],
        [(a, hbm(count, 2, rows, width))],
        [
            vmem(6 * ROWS, width),
            vmem(6 * ROWS, width),
            vmem(2, 7 * ROWS, width),
            vmem(2, 7 * ROWS, width),
            vmem(count, 2, 2, 3 * ROWS, width),
            sem((2 + 4 * count,)),
        ],
        8_000_000,
        aliases={10: 0},
    )
    return result


def solution(mesh):
    return jax.shard_map(
        local,
        mesh=mesh,
        in_specs=(
            P("sec", "tile", None),
            P("sec", None, "tile", None),
            P("sec", "tile", None),
            P("sec", "tile", None),
            P("sec", None),
        ),
        out_specs=P("sec", None, "tile", None),
        check_vma=False,
    )
```

time: 182 us -> 122 us (0.67)
  the two profiles are of different devices: /device:TPU:4 before, /device:TPU:2 now
where the time goes in v1:
time: 122 us
  Pallas kernels  54.3 us (45%)
  waiting for transfers between devices  32.3 us (26%)
  starting transfers between devices  26 us (21%)
  local copies, waits for them, and re-layouts  9.04 us (7%)
    pallas_call x6, Pallas kernels, run(): pl.pallas_call(kernel, out_shape=[shape for _, shape in outs], in_specs=[...  53.6 us
    ppermute x5, waiting for transfers between devices, exchange(): lax.ppermute(high, axis, forward)  18.2 us
    ppermute x5, starting transfers between devices, exchange(): lax.ppermute(high, axis, forward)  17 us
    ppermute x5, waiting for transfers between devices, exchange(): lax.ppermute(low, axis, backward)  14 us
    unnamed x18, local copies, waits for them, and re-layouts  9.04 us
    ppermute x5, starting transfers between devices, exchange(): lax.ppermute(low, axis, backward)  8.99 us
  transfers between devices with their start and end apart: 10, of which 5 were waited for; matrix products, arithmetic and copies ran while one was open for 0% of the time, Pallas kernels for 23%

profile of v1, /device:TPU:2, one launch (start us, length us, event | category | flops | bytes accessed | tf_op | source)
XLA Modules:
  0.0 122.0 jit_solution(12583599848610580433)
XLA Ops:
  0.0 2.2 %copy-done = f32[2,2,64,4096]{3,2,1,0:T(8,128)S(1)} copy-done((f32[2,2,64,4096]{3,2,1,0:T(8,128)S(1)}, f32[2,2,64,4096]{3,2,1,0:T(8,128)}, u32[]{:S(2)}) %copy-start) | copy-done | bytes 4194328
  2.2 1.6 %copy-done.1 = f32[2,64,4096]{2,1,0:T(8,128)S(1)} copy-done((f32[2,64,4096]{2,1,0:T(8,128)S(1)}, f32[2,64,4096]{2,1,0:T(8,128)}, u32[]{:S(2)}) %copy-start.1) | copy-done | bytes 2097176
  5.9 1.9 %collective-permute-start = (f32[2,24,4224]{2,1,0:T(8,128)S(1)}, f32[2,24,4224]{2,1,0:T(8,128)S(1)}, u32[]{:S(2)}, u32[]{:S(2)}) collective-permute-start(f32[2,24,4224]{2,1,0:T(8,128)S(1)} %get-tuple-element.32), channel_id=1, source_target_pairs={{0,1},{1,2},{2,3},{3,4},{4,5},{5,6},{6,7},{8,9},{9,10},{10,11},{11... | collective-permute-start | bytes 2433032 | tf_op jit(solution)/shard_map/ppermute | solution.py:657
  7.8 3.6 %collective-permute-start.1 = (f32[2,24,4224]{2,1,0:T(8,128)S(1)}, f32[2,24,4224]{2,1,0:T(8,128)S(1)}, u32[]{:S(2)}, u32[]{:S(2)}) collective-permute-start(f32[2,24,4224]{2,1,0:T(8,128)S(1)} %get-tuple-element.33), channel_id=1, source_target_pairs={{1,0},{2,1},{3,2},{4,3},{5,4},{6,5},{7,6},{9,8},{10,9},{11,10},{12... | collective-permute-start | bytes 2433032 | tf_op jit(solution)/shard_map/ppermute | solution.py:657
  11.5 6.8 %first_inner.1 = (f32[2,48,4096]{2,1,0:T(8,128)S(1)}, f32[2,48,4096]{2,1,0:T(8,128)S(1)}, f32[2,48,4096]{2,1,0:T(8,128)S(1)}, f32[2,48,4096]{2,1,0:T(8,128)S(1)}...) custom-call(s32[2,1,2]{2,1,0:T(1,128)S(1)} %copy-done.7, ...), custom_call_target="tpu_custom_call" | custom-call | flops 8000000 | bytes 8000000 | tf_op jit(solution)/shard_map/first_inner/pallas_call | solution.py:281
  18.3 3.5 %collective-permute-start.4 = (f32[1,48,4096]{2,1,0:T(8,128)S(1)}, f32[1,48,4096]{2,1,0:T(8,128)S(1)}, u32[]{:S(2)}, u32[]{:S(2)}) collective-permute-start(f32[1,48,4096]{2,1,0:T(8,128)S(1)} %get-tuple-element.44), channel_id=1, source_target_pairs={{0,8},{8,16},{16,24},{1,9},{9,17},{17,25},{2,10},{10,18},{18,26},{... | collective-permute-start | bytes 2359304 | tf_op jit(solution)/shard_map/ppermute | solution.py:657
  21.8 1.3 %collective-permute-start.5 = (f32[1,48,4096]{2,1,0:T(8,128)S(1)}, f32[1,48,4096]{2,1,0:T(8,128)S(1)}, u32[]{:S(2)}, u32[]{:S(2)}) collective-permute-start(f32[1,48,4096]{2,1,0:T(8,128)S(1)} %get-tuple-element.45), channel_id=1, source_target_pairs={{8,0},{16,8},{24,16},{9,1},{17,9},{25,17},{10,2},{18,10},{26,18},{... | collective-permute-start | bytes 2359304 | tf_op jit(solution)/shard_map/ppermute | solution.py:657
  23.2 4.0 %collective-permute-done.1.from_next = f32[2,24,4224]{2,1,0:T(8,128)S(1)} collective-permute-done((f32[2,24,4224]{2,1,0:T(8,128)S(1)}, f32[2,24,4224]{2,1,0:T(8,128)S(1)}, u32[]{:S(2)}, u32[]{:S(2)}) %collective-permute-start.1) | collective-permute-done | bytes 811040 | tf_op jit(solution)/shard_map/ppermute | solution.py:657
  27.2 6.2 %first_edge.1 = (f32[2,32,4096]{2,1,0:T(8,128)S(1)}, f32[2,32,4096]{2,1,0:T(8,128)S(1)}, f32[2,32,4096]{2,1,0:T(8,128)S(1)}, f32[2,32,4096]{2,1,0:T(8,128)S(1)},...) custom-call(s32[2,1,2]{2,1,0:T(1,128)S(1)} %copy-done.7, ...), custom_call_target="tpu_custom_call" | custom-call | flops 5000000 | bytes 5000000 | tf_op jit(solution)/shard_map/first_edge/pallas_call | solution.py:281
  33.4 1.3 %copy-done.2 = f32[2,2,32,4096]{3,2,1,0:T(8,128)} copy-done((f32[2,2,32,4096]{3,2,1,0:T(8,128)}, f32[2,2,32,4096]{3,2,1,0:T(8,128)S(1)}, u32[]{:S(2)}) %copy-start.2) | copy-done | bytes 2097176
  35.7 3.5 %collective-permute-start.2 = (f32[1,32,4096]{2,1,0:T(8,128)S(1)}, f32[1,32,4096]{2,1,0:T(8,128)S(1)}, u32[]{:S(2)}, u32[]{:S(2)}) collective-permute-start(f32[1,32,4096]{2,1,0:T(8,128)S(1)} %get-tuple-element.35), channel_id=1, source_target_pairs={{0,8},{8,16},{16,24},{1,9},{9,17},{17,25},{2,10},{10,18},{18,26},{... | collective-permute-start | bytes 1572872 | tf_op jit(solution)/shard_map/ppermute | solution.py:657
  39.2 1.3 %collective-permute-start.3 = (f32[1,32,4096]{2,1,0:T(8,128)S(1)}, f32[1,32,4096]{2,1,0:T(8,128)S(1)}, u32[]{:S(2)}, u32[]{:S(2)}) collective-permute-start(f32[1,32,4096]{2,1,0:T(8,128)S(1)} %get-tuple-element.36), channel_id=1, source_target_pairs={{8,0},{16,8},{24,16},{9,1},{17,9},{25,17},{10,2},{18,10},{26,18},{... | collective-permute-start | bytes 1572872 | tf_op jit(solution)/shard_map/ppermute | solution.py:657
  40.5 2.3 %collective-permute-done.5.refs_2_ = f32[1,48,4096]{2,1,0:T(8,128)S(1)} collective-permute-done((f32[1,48,4096]{2,1,0:T(8,128)S(1)}, f32[1,48,4096]{2,1,0:T(8,128)S(1)}, u32[]{:S(2)}, u32[]{:S(2)}) %collective-permute-start.5) | collective-permute-done | bytes 786464 | tf_op jit(solution)/shard_map/ppermute | solution.py:657
  42.8 9.1 %inner.1 = (f32[2,2,48,4096]{3,2,1,0:T(8,128)S(1)}, f32[2,2,32,4096]{3,2,1,0:T(8,128)S(1)}, f32[2,32,4096]{2,1,0:T(8,128)S(1)}, f32[1,32,4096]{2,1,0:T(8,128)S(1)}, f32[1,32,4096]{2,1,0:T(8,128)S(1)}) custom-call(s32[2,2]{1,0:T(2,128)S(1)} %copy-done.6, f32[1,48,4096]{2,1,0:T(8,128)S(1)} %collective-permute-done.4.refs_1_, ...), custom_call_target="tpu_custom_call" | custom-call | flops 8000000 | bytes 8000000 | tf_op jit(solution)/shard_map/inner/pallas_call | solution.py:281
  51.9 3.5 %collective-permute-done.3.refs_2_ = f32[1,32,4096]{2,1,0:T(8,128)S(1)} collective-permute-done((f32[1,32,4096]{2,1,0:T(8,128)S(1)}, f32[1,32,4096]{2,1,0:T(8,128)S(1)}, u32[]{:S(2)}, u32[]{:S(2)}) %collective-permute-start.3) | collective-permute-done | bytes 524320 | tf_op jit(solution)/shard_map/ppermute | solution.py:657
  55.4 1.6 %copy-done.3 = f32[2,2,32,4096]{3,2,1,0:T(8,128)S(1)} copy-done((f32[2,2,32,4096]{3,2,1,0:T(8,128)S(1)}, f32[2,2,32,4096]{3,2,1,0:T(8,128)}, u32[]{:S(2)}) %copy-start.3) | copy-done | bytes 2097176
  57.0 10.8 %edge.1 = (f32[2,2,48,4096]{3,2,1,0:T(8,128)S(1)}, f32[2,48,4096]{2,1,0:T(8,128)S(1)}, f32[1,40,4096]{2,1,0:T(8,128)S(1)}, f32[1,40,4096]{2,1,0:T(8,128)S(1)}) custom-call(s32[2,2]{1,0:T(2,128)S(1)} %copy-done.6, f32[1,32,4096]{2,1,0:T(8,128)S(1)} %collective-permute-done.2.refs_1_, f32[1,32,4096]{2,1,0:T(8,128)S(1)} %collective-permute-done.3.refs_2_, ...), custom_call_target="tpu_custom_call" | custom-call | flops 8000000 | bytes 8000000 | tf_op jit(solution)/shard_map/edge/pallas_call | solution.py:281
  67.8 3.5 %collective-permute-start.6 = (f32[1,40,4096]{2,1,0:T(8,128)S(1)}, f32[1,40,4096]{2,1,0:T(8,128)S(1)}, u32[]{:S(2)}, u32[]{:S(2)}) collective-permute-start(f32[1,40,4096]{2,1,0:T(8,128)S(1)} %get-tuple-element.49), channel_id=1, source_target_pairs={{0,8},{8,16},{16,24},{1,9},{9,17},{17,25},{2,10},{10,18},{18,26},{... | collective-permute-start | bytes 1966088 | tf_op jit(solution)/shard_map/ppermute | solution.py:657
  72.6 4.6 %collective-permute-start.8 = (f32[1,32,4096]{2,1,0:T(8,128)S(1)}, f32[1,32,4096]{2,1,0:T(8,128)S(1)}, u32[]{:S(2)}, u32[]{:S(2)}) collective-permute-start(f32[1,32,4096]{2,1,0:T(8,128)S(1)} %get-tuple-element.53), channel_id=1, source_target_pairs={{0,8},{8,16},{16,24},{1,9},{9,17},{17,25},{2,10},{10,18},{18,26},{... | collective-permute-start | bytes 1572872 | tf_op jit(solution)/shard_map/ppermute | solution.py:657
  77.2 1.5 %collective-permute-start.9 = (f32[1,32,4096]{2,1,0:T(8,128)S(1)}, f32[1,32,4096]{2,1,0:T(8,128)S(1)}, u32[]{:S(2)}, u32[]{:S(2)}) collective-permute-start(f32[1,32,4096]{2,1,0:T(8,128)S(1)} %get-tuple-element.54), channel_id=1, source_target_pairs={{8,0},{16,8},{24,16},{9,1},{17,9},{25,17},{10,2},{18,10},{26,18},{... | collective-permute-start | bytes 1572872 | tf_op jit(solution)/shard_map/ppermute | solution.py:657
  78.6 18.2 %collective-permute-done.8.refs_1_ = f32[1,32,4096]{2,1,0:T(8,128)S(1)} collective-permute-done((f32[1,32,4096]{2,1,0:T(8,128)S(1)}, f32[1,32,4096]{2,1,0:T(8,128)S(1)}, u32[]{:S(2)}, u32[]{:S(2)}) %collective-permute-start.8) | collective-permute-done | bytes 524320 | tf_op jit(solution)/shard_map/ppermute | solution.py:657
  96.9 4.2 %collective-permute-done.9.refs_2_ = f32[1,32,4096]{2,1,0:T(8,128)S(1)} collective-permute-done((f32[1,32,4096]{2,1,0:T(8,128)S(1)}, f32[1,32,4096]{2,1,0:T(8,128)S(1)}, u32[]{:S(2)}, u32[]{:S(2)}) %collective-permute-start.9) | collective-permute-done | bytes 524320 | tf_op jit(solution)/shard_map/ppermute | solution.py:657
  101.0 6.6 %last_inner.1 = (f32[2,2,32,4096]{3,2,1,0:T(8,128)S(1)}, f32[2,2,64,4096]{3,2,1,0:T(8,128)}) custom-call(s32[2,2]{1,0:T(2,128)S(1)} %copy-done.6, f32[1,32,4096]{2,1,0:T(8,128)S(1)} %collective-permute-done.8.refs_1_, f32[1,32,4096]{2,1,0:T(8,128)S(1)} %collective-permute-done.9.refs_2_, f32[2,32,4096]{2,1,0:T(8,128)S(1)} %get-tuple-element.55.refs_3_, ...), custom_call_target="tpu_custom_call" | custom-call | flops 8000000 | bytes 8000000 | tf_op jit(solution)/shard_map/last_inner/pallas_call | solution.py:281
  107.7 14.1 %last_edge.1 = f32[2,2,64,4096]{3,2,1,0:T(8,128)} custom-call(s32[2,2]{1,0:T(2,128)S(1)} %copy-done.6, f32[1,40,4096]{2,1,0:T(8,128)S(1)} %collective-permute-done.6.refs_1_, f32[1,40,4096]{2,1,0:T(8,128)S(1)} %collective-permute-done.7.refs_2_, f32[2,48,4096]{2,1,0:T(8,128)S(1)} %get-tuple-element.51.refs_3_, ...), custom_call_target="tpu_custom_call", output_to_operand_aliasing={{}: (10, {})} | custom-call | flops 8000000 | bytes 8000000 | tf_op jit(solution)/shard_map/last_edge/pallas_call | solution.py:281
  (21 shorter events, 4.4 us)
Async XLA Ops:
  0.0 2.2 %copy-start = (f32[2,2,64,4096]{3,2,1,0:T(8,128)S(1)}, f32[2,2,64,4096]{3,2,1,0:T(8,128)}, u32[]{:S(2)}) copy-start(f32[2,2,64,4096]{3,2,1,0:T(8,128)} %field.3) | copy-start | bytes 12582916
  2.2 1.6 %copy-start.1 = (f32[2,64,4096]{2,1,0:T(8,128)S(1)}, f32[2,64,4096]{2,1,0:T(8,128)}, u32[]{:S(2)}) copy-start(f32[2,64,4096]{2,1,0:T(8,128)} %sections.3) | copy-start | bytes 6291460
  3.8 0.7 copy-start.7
  4.5 0.7 copy-start.8
  5.9 17.2 %collective-permute-start = (f32[2,24,4224]{2,1,0:T(8,128)S(1)}, f32[2,24,4224]{2,1,0:T(8,128)S(1)}, u32[]{:S(2)}, u32[]{:S(2)}) collective-permute-start(f32[2,24,4224]{2,1,0:T(8,128)S(1)} %get-tuple-element.32), channel_id=1, source_target_pairs={{0,1},{1,2},{2,3},{3,4},{4,5},{5,6},{6,7},{8,9},{9,10},{10,11},{11... | collective-permute-start | bytes 2433032 | tf_op jit(solution)/shard_map/ppermute | solution.py:657
  7.8 19.3 %collective-permute-start.1 = (f32[2,24,4224]{2,1,0:T(8,128)S(1)}, f32[2,24,4224]{2,1,0:T(8,128)S(1)}, u32[]{:S(2)}, u32[]{:S(2)}) collective-permute-start(f32[2,24,4224]{2,1,0:T(8,128)S(1)} %get-tuple-element.33), channel_id=1, source_target_pairs={{1,0},{2,1},{3,2},{4,3},{5,4},{6,5},{7,6},{9,8},{10,9},{11,10},{12... | collective-permute-start | bytes 2433032 | tf_op jit(solution)/shard_map/ppermute | solution.py:657
  18.3 22.2 %collective-permute-start.4 = (f32[1,48,4096]{2,1,0:T(8,128)S(1)}, f32[1,48,4096]{2,1,0:T(8,128)S(1)}, u32[]{:S(2)}, u32[]{:S(2)}) collective-permute-start(f32[1,48,4096]{2,1,0:T(8,128)S(1)} %get-tuple-element.44), channel_id=1, source_target_pairs={{0,8},{8,16},{16,24},{1,9},{9,17},{17,25},{2,10},{10,18},{18,26},{... | collective-permute-start | bytes 2359304 | tf_op jit(solution)/shard_map/ppermute | solution.py:657
  21.8 20.9 %collective-permute-start.5 = (f32[1,48,4096]{2,1,0:T(8,128)S(1)}, f32[1,48,4096]{2,1,0:T(8,128)S(1)}, u32[]{:S(2)}, u32[]{:S(2)}) collective-permute-start(f32[1,48,4096]{2,1,0:T(8,128)S(1)} %get-tuple-element.45), channel_id=1, source_target_pairs={{8,0},{16,8},{24,16},{9,1},{17,9},{25,17},{10,2},{18,10},{26,18},{... | collective-permute-start | bytes 2359304 | tf_op jit(solution)/shard_map/ppermute | solution.py:657
  27.2 15.6 %copy-start.6 = (s32[2,2]{1,0:T(2,128)S(1)}, s32[2,2]{1,0:T(2,128)}, u32[]{:S(2)}) copy-start(s32[2,2]{1,0:T(2,128)} %refs_0_.7) | copy-start | bytes 52
  33.3 1.3 %copy-start.2 = (f32[2,2,32,4096]{3,2,1,0:T(8,128)}, f32[2,2,32,4096]{3,2,1,0:T(8,128)S(1)}, u32[]{:S(2)}) copy-start(f32[2,2,32,4096]{3,2,1,0:T(8,128)S(1)} %get-tuple-element.43.refs_10_) | copy-start | bytes 6291460
  34.7 1.0 copy-start.4
  35.7 16.2 %collective-permute-start.2 = (f32[1,32,4096]{2,1,0:T(8,128)S(1)}, f32[1,32,4096]{2,1,0:T(8,128)S(1)}, u32[]{:S(2)}, u32[]{:S(2)}) collective-permute-start(f32[1,32,4096]{2,1,0:T(8,128)S(1)} %get-tuple-element.35), channel_id=1, source_target_pairs={{0,8},{8,16},{16,24},{1,9},{9,17},{17,25},{2,10},{10,18},{18,26},{... | collective-permute-start | bytes 1572872 | tf_op jit(solution)/shard_map/ppermute | solution.py:657
  39.2 16.2 %collective-permute-start.3 = (f32[1,32,4096]{2,1,0:T(8,128)S(1)}, f32[1,32,4096]{2,1,0:T(8,128)S(1)}, u32[]{:S(2)}, u32[]{:S(2)}) collective-permute-start(f32[1,32,4096]{2,1,0:T(8,128)S(1)} %get-tuple-element.36), channel_id=1, source_target_pairs={{8,0},{16,8},{24,16},{9,1},{17,9},{25,17},{10,2},{18,10},{26,18},{... | collective-permute-start | bytes 1572872 | tf_op jit(solution)/shard_map/ppermute | solution.py:657
  42.8 12.6 %copy-start.5 = (f32[2,32,4096]{2,1,0:T(8,128)S(1)}, f32[2,32,4096]{2,1,0:T(8,128)}, u32[]{:S(2)}) copy-start(f32[2,32,4096]{2,1,0:T(8,128)} %copy-done.4) | copy-start | bytes 3145732
  55.4 1.6 %copy-start.3 = (f32[2,2,32,4096]{3,2,1,0:T(8,128)S(1)}, f32[2,2,32,4096]{3,2,1,0:T(8,128)}, u32[]{:S(2)}) copy-start(f32[2,2,32,4096]{3,2,1,0:T(8,128)} %copy-done.2) | copy-start | bytes 6291460
  67.8 39.9 %collective-permute-start.6 = (f32[1,40,4096]{2,1,0:T(8,128)S(1)}, f32[1,40,4096]{2,1,0:T(8,128)S(1)}, u32[]{:S(2)}, u32[]{:S(2)}) collective-permute-start(f32[1,40,4096]{2,1,0:T(8,128)S(1)} %get-tuple-element.49), channel_id=1, source_target_pairs={{0,8},{8,16},{16,24},{1,9},{9,17},{17,25},{2,10},{10,18},{18,26},{... | collective-permute-start | bytes 1966088 | tf_op jit(solution)/shard_map/ppermute | solution.py:657
  71.3 36.4 %collective-permute-start.7 = (f32[1,40,4096]{2,1,0:T(8,128)S(1)}, f32[1,40,4096]{2,1,0:T(8,128)S(1)}, u32[]{:S(2)}, u32[]{:S(2)}) collective-permute-start(f32[1,40,4096]{2,1,0:T(8,128)S(1)} %get-tuple-element.50), channel_id=1, source_target_pairs={{8,0},{16,8},{24,16},{9,1},{17,9},{25,17},{10,2},{18,10},{26,18},{... | collective-permute-start | bytes 1966088 | tf_op jit(solution)/shard_map/ppermute | solution.py:657
  72.6 24.3 %collective-permute-start.8 = (f32[1,32,4096]{2,1,0:T(8,128)S(1)}, f32[1,32,4096]{2,1,0:T(8,128)S(1)}, u32[]{:S(2)}, u32[]{:S(2)}) collective-permute-start(f32[1,32,4096]{2,1,0:T(8,128)S(1)} %get-tuple-element.53), channel_id=1, source_target_pairs={{0,8},{8,16},{16,24},{1,9},{9,17},{17,25},{2,10},{10,18},{18,26},{... | collective-permute-start | bytes 1572872 | tf_op jit(solution)/shard_map/ppermute | solution.py:657
  77.2 23.9 %collective-permute-start.9 = (f32[1,32,4096]{2,1,0:T(8,128)S(1)}, f32[1,32,4096]{2,1,0:T(8,128)S(1)}, u32[]{:S(2)}, u32[]{:S(2)}) collective-permute-start(f32[1,32,4096]{2,1,0:T(8,128)S(1)} %get-tuple-element.54), channel_id=1, source_target_pairs={{8,0},{16,8},{24,16},{9,1},{17,9},{25,17},{10,2},{18,10},{26,18},{... | collective-permute-start | bytes 1572872 | tf_op jit(solution)/shard_map/ppermute | solution.py:657

commit v2 on v0

v2 whole, which is shorter than its diff:
```python
import functools
import math

import jax
import jax.numpy as jnp
from jax import lax
from jax.experimental import pallas as pl
from jax.experimental.pallas import tpu as pltpu
from jax.sharding import PartitionSpec as P


relax_scale = 0.2**3
softening = 0.25
F32 = jnp.float32
REACH = 12
BELOW = 6
PACKED = REACH + 2 * BELOW
LANES = 128
ROWS = 8
VMEM_LIMIT = 20 * 1024 * 1024
CHUNK = 8


def iotas():
    return (
        lax.broadcasted_iota(jnp.int32, (ROWS, LANES), 0),
        lax.broadcasted_iota(jnp.int32, (ROWS, LANES), 1),
    )


def cols(j):
    return slice(j * LANES, (j + 1) * LANES)


def tile(i):
    if isinstance(i, int):
        return slice(i * ROWS, (i + 1) * ROWS)
    return pl.ds(pl.multiple_of(i * ROWS, ROWS), ROWS)


def eight(row):
    return pl.ds(row, ROWS)


def groups(first, last):
    starts = list(range(first, last - ROWS + 2, ROWS))
    if starts[-1] + ROWS - 1 < last:
        starts.append(last - ROWS + 1)
    return starts


def col_before(here, left, lane):
    return pltpu.roll(jnp.where(lane == LANES - 1, left, here), 1, 1)


def col_after(here, right, lane):
    return pltpu.roll(jnp.where(lane == 0, right, here), LANES - 1, 1)


def across(load, starts, columns, body):
    zero = jnp.zeros((ROWS, LANES), F32)
    left = [zero] * len(starts)
    here = [load(0, start) for start in starts]
    for j in range(columns):
        right = [load(j + 1, start) if j + 1 < columns else zero for start in starts]
        for k, start in enumerate(starts):
            body(j, start, left[k], here[k], right[k])
        left, here = here, right


def sweep(load, starts, columns, store):
    _, lane = iotas()

    def body(j, start, left, here, right):
        total = here + (load(j, start - 1) + load(j, start + 1))
        store(j, start, total + (col_before(here, left, lane) + col_after(here, right, lane)))

    across(load, starts, columns, body)


def derive(load, starts, columns, body):
    _, lane = iotas()

    def each(j, start, left, here, right):
        grad_rows = 0.5 * (load(j, start + 1) - load(j, start - 1))
        grad_cols = 0.5 * (col_after(here, right, lane) - col_before(here, left, lane))
        body(j, start, here, grad_rows, grad_cols)

    across(load, starts, columns, each)


def blend_rows(source, base, shift, store, columns):
    row, _ = iotas()
    row_shift, _, row_part, _ = shift
    first = base + jnp.where(row_shift < 0, -1, 0)
    within = jnp.where(row_shift < 0, row_shift + ROWS, row_shift)
    turn = jnp.where(within == 0, 0, ROWS - within)
    turn_next = ROWS - 1 - within
    for j in range(columns):
        a, b = source(first, j), source(first + 1, j)
        upper = pltpu.roll(jnp.where(row < within, b, a), turn, 0)
        lower = pltpu.roll(jnp.where(row < within + 1, b, a), turn_next, 0)
        store(j, (1.0 - row_part) * upper + row_part * lower)


def blend_cols(lines, jobs, columns):
    _, lane = iotas()
    parts = []
    for rows, (_, col_shift, _, col_part), store in jobs:
        start = jnp.where(col_shift < 0, 0, 1)
        side = jnp.where(col_shift < 0, col_shift + LANES, col_shift)
        back = jnp.where(side == 0, 0, LANES - side)
        parts.append((rows, start, side, back, col_part, store))

    def moved(j, part):
        rows, start, side, back = part[:4]
        return pltpu.roll(
            jnp.where(lane < side, lines[start + j + 1, rows, :], lines[start + j, rows, :]), back, 1
        )

    here = [moved(0, part) for part in parts]
    for j in range(columns):
        after = [moved(j + 1, part) for part in parts]
        for k, (_, _, _, _, col_part, store) in enumerate(parts):
            store(j, (1.0 - col_part) * here[k] + col_part * col_after(here[k], after[k], lane))
        here = after


def clear_lines(lines, columns):
    rows = lines.shape[1]
    for j in (0, columns + 1, columns + 2):
        lines[j] = jnp.zeros((rows, LANES), F32)


def force(linear, lower, upper, grad_rows, grad_cols, weight_lower, weight_upper):
    denominator = grad_rows * grad_rows + grad_cols * grad_cols + softening
    lower_diff = lower - linear
    upper_diff = upper - linear
    below = denominator + lower_diff * lower_diff
    above = denominator + upper_diff * upper_diff
    top = (weight_lower * lower_diff) * above + (weight_upper * upper_diff) * below
    bottom = below * above
    inverse = pl.reciprocal(bottom, approx=True)
    inverse = inverse * (2.0 - bottom * inverse)
    return top * inverse


def half_weights(weights_ref, s, sections):
    number = lax.axis_index("sec") * sections + s
    lower = jnp.where(number > 0, weights_ref[s, 0], 0).astype(F32) * 0.5
    upper = jnp.where(number < sections * lax.axis_size("sec") - 1, weights_ref[s, 1], 0).astype(F32) * 0.5
    return lower, upper


def shift_of(offsets_ref, fractions_ref, s):
    return (
        offsets_ref[s, 0, 0],
        offsets_ref[s, 0, 1],
        fractions_ref[s, 0, 0].astype(F32) * (1.0 / 256.0),
        fractions_ref[s, 0, 1].astype(F32) * (1.0 / 256.0),
    )


def copy_in(pairs, sems):
    copies = [pltpu.make_async_copy(a, b, sems.at[k]) for k, (a, b) in enumerate(pairs)]
    for copy in copies:
        copy.start()
    return copies


def over_columns(columns, body):
    chunk = math.gcd(CHUNK, columns)

    def step(k, carry):
        for u in range(chunk):
            body(k * chunk + u)
        return carry

    lax.fori_loop(0, columns // chunk, step, 0)


class Strip:
    def __init__(self, rows):
        self.rows = rows

    def mirror(self, side, starts):
        return starts if side == 0 else [self.rows - ROWS - start for start in starts]

    def keep(self, side, start):
        row, _ = iotas()
        strip = lax.axis_index("tile")
        if start < 0:
            return row >= jnp.where(strip > 0, -ROWS, -start)
        if start + ROWS > self.rows:
            return row < jnp.where(strip < lax.axis_size("tile") - 1, 2 * ROWS, self.rows - start)
        return None


def masked(keep, value):
    return value if keep is None else jnp.where(keep, value, 0.0)


def vmem(*shape):
    return pltpu.VMEM(shape, F32)


def hbm(*shape):
    return jax.ShapeDtypeStruct(shape, F32)


SPECS = {
    "s": pl.BlockSpec(memory_space=pltpu.SMEM),
    "v": pl.BlockSpec(memory_space=pltpu.VMEM),
    "h": pl.BlockSpec(memory_space=pltpu.HBM),
    "a": pl.BlockSpec(memory_space=pl.ANY),
}


def run(kernel, name, ins, outs, scratch, cost, aliases=None):
    return pl.pallas_call(
        kernel,
        out_shape=[shape for _, shape in outs],
        in_specs=[SPECS[kind] for kind, _ in ins],
        out_specs=[SPECS[kind] for kind, _ in outs],
        scratch_shapes=scratch,
        input_output_aliases=aliases or {},
        cost_estimate=pl.CostEstimate(flops=cost, bytes_accessed=cost, transcendentals=0),
        compiler_params=pltpu.CompilerParams(vmem_limit_bytes=VMEM_LIMIT),
        name=name,
    )(*[value for _, value in ins])


def pack_kernel(offsets, fractions, sections, field, to_next, to_last, plane, edge_field, sems):
    count, rows, width = sections.shape
    columns = width // LANES
    _, lane = iotas()
    lane = lane[:1]
    loads = load_edges(sections, field, plane, edge_field, sems)
    for s in range(count):
        values = jnp.zeros((1, LANES), F32)
        for k, value in enumerate(
            (offsets[s, 0, 0], offsets[s, 0, 1], fractions[s, 0, 0], fractions[s, 0, 1])
        ):
            values = jnp.where(lane == k, value.astype(F32), values)
        values = jnp.broadcast_to(values, (PACKED, LANES))
        to_next[s, columns] = values
        to_last[s, columns] = values
    for copy in loads:
        copy.wait()
    for s in range(count):
        for j in range(columns):
            to_next[s, j, :REACH, :] = plane[s, 1, 2 * ROWS - REACH :, cols(j)]
            to_last[s, j, :REACH, :] = plane[s, 0, :REACH, cols(j)]
            for c in range(2):
                part = slice(REACH + c * BELOW, REACH + (c + 1) * BELOW)
                to_next[s, j, part, :] = edge_field[s, c, 1, ROWS - BELOW :, cols(j)]
                to_last[s, j, part, :] = edge_field[s, c, 0, :BELOW, cols(j)]


def load_edges(sections, field, plane, edge_field, sems):
    count, rows, _ = sections.shape
    reach = 2 * ROWS
    pairs = []
    for s in range(count):
        pairs.append((sections.at[s, pl.ds(0, reach)], plane.at[s, 0]))
        pairs.append((sections.at[s, pl.ds(rows - reach, reach)], plane.at[s, 1]))
        for c in range(2):
            pairs.append((field.at[s, c, pl.ds(0, ROWS)], edge_field.at[s, c, 0]))
            pairs.append((field.at[s, c, pl.ds(rows - ROWS, ROWS)], edge_field.at[s, c, 1]))
    return copy_in(pairs, sems)


def edge_scratch(count, width):
    return [
        vmem(count, 2, 2 * ROWS, width),
        vmem(count, 2, 2, ROWS, width),
        pltpu.SemaphoreType.DMA((6 * count,)),
    ]


def first_inner_kernel(count, offsets, fractions, sections, field, *rest):
    warped, grow, gcol, field_band, *rest = rest
    linear, (plane, inner_field, lines, sems) = rest[:count], rest[count:]
    _, rows, width = sections.shape
    columns = width // LANES
    tiles = rows // ROWS
    inner = rows - 2 * ROWS
    loads = copy_in(
        [(sections.at[s], plane.at[s, pl.ds(ROWS, rows)]) for s in range(count)]
        + [
            (field.at[s, c, pl.ds(ROWS, inner)], inner_field.at[s, c])
            for s in range(count)
            for c in range(2)
        ],
        sems,
    )
    clear_lines(lines, columns)
    zero = jnp.zeros((ROWS, LANES), F32)
    for s in range(count):
        for j in range(columns):
            plane[s, :ROWS, cols(j)] = zero
            plane[s, rows + ROWS :, cols(j)] = zero
    for s in range(count):
        loads[s].wait()
        shift = shift_of(offsets, fractions, s)

        def rowwise(i, carry):
            def store(j, value):
                lines[j + 1, tile(i), :] = value

            blend_rows(lambda k, j: plane[s, tile(k), cols(j)], i + 1, shift, store, columns)
            return carry

        lax.fori_loop(0, tiles, rowwise, 0)

        def colwise(i, carry):
            def job(k):
                def store(j, value):
                    warped[s, j, tile(i * 4 + k), :] = value

                return tile(i * 4 + k), shift, store

            blend_cols(lines, [job(k) for k in range(4)], columns)
            return carry

        lax.fori_loop(0, tiles // 4, colwise, 0)
        loads[count + 2 * s].wait()
        loads[count + 2 * s + 1].wait()

        def body(j, start, here, grad_rows, grad_cols):
            at = (s, j, eight(start - ROWS))
            grow[at] = grad_rows
            gcol[at] = grad_cols
            u = inner_field[s, 0, start - ROWS : start, cols(j)]
            v = inner_field[s, 1, start - ROWS : start, cols(j)]
            field_band[s, 0, j, eight(start - ROWS), :] = u
            field_band[s, 1, j, eight(start - ROWS), :] = v
            linear[s][j, eight(start - ROWS), :] = here + u * grad_rows + v * grad_cols

        derive(
            lambda j, start: warped[s, j, eight(start), :],
            groups(ROWS, rows - ROWS - 1),
            columns,
            body,
        )


def first_edge_kernel(count, rows, offsets, fractions, sections, field, from_last, from_next, *rest):
    inner_warped, inner_grow, inner_gcol, warped, grow, gcol, field_band, *rest = rest
    linear, (plane, edge_field, sems, lines) = rest[:count], rest[count:]
    width = sections.shape[2]
    columns = width // LANES
    row, lane = iotas()
    loads = load_edges(sections, field, plane, edge_field, sems)
    clear_lines(lines, columns)
    for copy in loads:
        copy.wait()
    received = (from_last, from_next)
    for s in range(count):
        own = shift_of(offsets, fractions, s)

        def theirs(side):
            block = received[side][s, columns, 0:1, :]
            values = [jnp.sum(jnp.where(lane[:1] == k, block, 0.0)) for k in range(4)]
            return (
                values[0].astype(jnp.int32),
                values[1].astype(jnp.int32),
                values[2] * (1.0 / 256.0),
                values[3] * (1.0 / 256.0),
            )

        shifts = (theirs(0), own, own, theirs(1))

        def near(side, k, j):
            block = received[side]
            if side == 0:
                if k >= 2:
                    return plane[s, 0, tile(k - 2), cols(j)]
                if k == 1:
                    return block[s, j, eight(REACH - ROWS), :]
                return pltpu.roll(block[s, j, eight(0), :], 2 * ROWS - REACH, 0)
            if k < 2:
                return plane[s, 1, tile(k), cols(j)]
            if k == 2:
                return block[s, j, eight(0), :]
            return pltpu.roll(block[s, j, eight(REACH - ROWS), :], REACH - ROWS, 0)

        for side in range(2):
            for i in (1, 2):
                shift = shifts[2 * side + i - 1]
                row_shift, _, row_part, _ = shift
                within = jnp.where(row_shift < 0, row_shift + ROWS, row_shift)
                turn = jnp.where(within == 0, 0, ROWS - within)
                turn_next = ROWS - 1 - within
                negative = jnp.broadcast_to(row_shift, (ROWS, LANES)) < 0
                for j in range(columns):
                    before, here, after = (near(side, k, j) for k in (i - 1, i, i + 1))
                    a = jnp.where(negative, before, here)
                    b = jnp.where(negative, here, after)
                    upper = pltpu.roll(jnp.where(row < within, b, a), turn, 0)
                    lower = pltpu.roll(jnp.where(row < within + 1, b, a), turn_next, 0)
                    lines[j + 1, tile(2 * side + i - 1), :] = (1.0 - row_part) * upper + row_part * lower

        def job(k):
            side, at = ((0, 0), (0, 1), (1, 1), (1, 2))[k]

            def store(j, value):
                warped[s, side, j, tile(at), :] = value

            return tile(k), shifts[k], store

        blend_cols(lines, [job(k) for k in range(4)], columns)

        for j in range(columns):
            for side in range(2):
                beside = ROWS if side == 0 else rows - 2 * ROWS
                here = tile(2 if side == 0 else 0)
                warped[s, side, j, here, :] = inner_warped[s, j, eight(beside), :]
                grow[s, side, j, here, :] = inner_grow[s, j, eight(beside - ROWS), :]
                gcol[s, side, j, here, :] = inner_gcol[s, j, eight(beside - ROWS), :]
            for c in range(2):
                part = slice(REACH + c * BELOW, REACH + (c + 1) * BELOW)
                field_band[s, 0, c, j, ROWS - BELOW : ROWS, :] = from_last[s, j, part, :]
                field_band[s, 0, c, j, ROWS : 2 * ROWS, :] = edge_field[s, c, 0, :, cols(j)]
                field_band[s, 1, c, j, :ROWS, :] = edge_field[s, c, 1, :, cols(j)]
                field_band[s, 1, c, j, ROWS : ROWS + BELOW, :] = from_next[s, j, part, :]

        starts = [(0, -BELOW), (0, 0), (1, rows - ROWS), (1, rows - ROWS + BELOW)]

        def body(j, group, here, grad_rows, grad_cols):
            side, start, _ = group
            at = (s, side, j, eight(edge_at(rows, start)))
            grow[at] = grad_rows
            gcol[at] = grad_cols
            field_row = start + ROWS if side == 0 else start - (rows - ROWS)
            u = field_band[s, side, 0, j, eight(field_row), :]
            v = field_band[s, side, 1, j, eight(field_row), :]
            linear[s][eight(first_edge_row(rows, j, start)), :] = here + u * grad_rows + v * grad_cols

        def load(j, group):
            side, start, offset = group
            return warped[s, side, j, eight(edge_at(rows, start) + offset), :]

        derive(load, [Group(*start) for start in starts], columns, body)


class Group(tuple):
    def __new__(cls, side, start, offset=0):
        return super().__new__(cls, (side, start, offset))

    def __add__(self, n):
        return Group(self[0], self[1], self[2] + n)

    def __sub__(self, n):
        return Group(self[0], self[1], self[2] - n)


def edge_at(rows, row):
    return row + ROWS if row < rows // 2 else row - (rows - 2 * ROWS)


FIRST_EDGE = 2 * (ROWS + BELOW)
HALF = BELOW // 2
NEXT_EDGE = 2 * (ROWS + 4 + HALF)


def first_edge_row(rows, j, row):
    return j * FIRST_EDGE + (row + BELOW if row < rows // 2 else row - (rows - ROWS) + FIRST_EDGE // 2)


def next_edge_row(rows, j, row):
    return j * NEXT_EDGE + (row + HALF if row < rows // 2 else row - (rows - ROWS - 4) + NEXT_EDGE // 2)


def inner_kernel(count, rows, last, weights, *refs):
    low, high, *refs = refs
    linear, refs = refs[:count], refs[count:]
    if last:
        grow, gcol, field, moved, once, twice, result, stage, sems = refs
        first = ROWS + 4
    else:
        grow, gcol, warped, field, moved, once, twice, next_field, *next_linear = refs
        first = ROWS
    columns = low.shape[0]
    end = rows - first - 1
    for s in range(count):
        weight_lower, weight_upper = half_weights(weights, s, count)

        def column(j):
            for start in groups(first, end):
                at = (j, eight(start - first))
                lower = low[at] if s == 0 else linear[s - 1][at]
                upper = high[at] if s == count - 1 else linear[s + 1][at]
                grad_rows = grow[s, j, eight(start - ROWS), :]
                grad_cols = gcol[s, j, eight(start - ROWS), :]
                half = force(linear[s][at], lower, upper, grad_rows, grad_cols, weight_lower, weight_upper)
                for c, grad in enumerate((grad_rows, grad_cols)):
                    old = field[s, c, j, eight(start - first), :]
                    moved[s, c, j, eight(start - first), :] = old + half * grad

        over_columns(columns, column)
    stores = []
    for s in range(count):

        def plane(c, carry):
            def load(ref, base):
                return lambda j, start: ref[s, c, j, eight(start - base), :]

            def store_once(j, start, value):
                once[s, c, j, eight(start - first - 1), :] = value

            def store_twice(j, start, value):
                twice[s, c, j, eight(start - first - 2), :] = value

            def store_last(j, start, value):
                if last:
                    stage[s, c, start - 2 * ROWS : start - ROWS, cols(j)] = value * relax_scale
                else:
                    next_field[s, c, j, eight(start - first - 4), :] = value * relax_scale

            sweep(load(moved, first), groups(first + 1, end - 1), columns, store_once)
            sweep(load(once, first + 1), groups(first + 2, end - 2), columns, store_twice)
            sweep(load(twice, first + 2), groups(first + 4, end - 4), columns, store_last)
            return carry

        lax.fori_loop(0, 2, plane, 0)
        if last:
            copy = pltpu.make_async_copy(
                stage.at[s], result.at[s, :, pl.ds(2 * ROWS, rows - 4 * ROWS)], sems.at[s]
            )
            copy.start()
            stores.append(copy)
            continue

        def column(j):
            for start in groups(first + 4, end - 4):
                at = (s, j, eight(start - ROWS))
                inside = (j, eight(start - first - 4))
                next_linear[s][inside] = (
                    warped[s, j, eight(start), :]
                    + next_field[(s, 0) + inside] * grow[at]
                    + next_field[(s, 1) + inside] * gcol[at]
                )

        over_columns(columns, column)
    for copy in stores:
        copy.wait()


def edge_kernel(count, rows, last, weights, *refs):
    low, high, *refs = refs
    linear, refs = refs[:count], refs[count:]
    if last:
        (grow, gcol, field, inner_moved, inner_once, inner_twice, _, result,
         moved, once, twice, stage, sems) = refs
        inner_first = ROWS + 4
        starts = [-HALF, 4], [-2, 6], [-1, 7], [0, 8]
        copied = ROWS + 4, 14, 15
        bases = -4, -2, -1
        edge_row = next_edge_row
    else:
        (grow, gcol, warped, field, inner_moved, inner_once, inner_twice, next_field, *refs) = refs
        next_linear, (moved, once, twice) = refs[:count], refs[count:]
        inner_first = ROWS
        starts = [-BELOW, 0], [-5, 3], [-4, 4], [-HALF, 4]
        copied = ROWS, 11, 12
        bases = -ROWS, -5, -4
        edge_row = first_edge_row
    columns = grow.shape[2]
    strip = Strip(rows)
    span = 3 * ROWS

    def base(side, stage_number):
        return bases[stage_number] if side == 0 else rows - span - bases[stage_number]

    def field_at(s, c, j, side, start):
        if last:
            return field[s, c, side, j, eight(start + 4 if side == 0 else start - (rows - ROWS - 4)), :]
        return field[s, side, c, j, eight(start + ROWS if side == 0 else start - (rows - ROWS)), :]

    for s in range(count):
        weight_lower, weight_upper = half_weights(weights, s, count)
        for side in range(2):
            mine = strip.mirror(side, starts[0])
            keeps = [strip.keep(side, start) for start in mine]

            def column(j):
                for keep, start in zip(keeps, mine):
                    at = (eight(edge_row(rows, j, start)), slice(None))
                    lower = low[at] if s == 0 else linear[s - 1][at]
                    upper = high[at] if s == count - 1 else linear[s + 1][at]
                    grad_rows = grow[s, side, j, eight(edge_at(rows, start)), :]
                    grad_cols = gcol[s, side, j, eight(edge_at(rows, start)), :]
                    half = force(
                        linear[s][at], lower, upper, grad_rows, grad_cols, weight_lower, weight_upper
                    )
                    for c, grad in enumerate((grad_rows, grad_cols)):
                        value = masked(keep, field_at(s, c, j, side, start) + half * grad)
                        moved[s, c, side, j, eight(start - base(side, 0)), :] = value
                (there,) = strip.mirror(side, copied[:1])
                for c in range(2):
                    moved[s, c, side, j, eight(there - base(side, 0)), :] = inner_moved[
                        s, c, j, eight(there - inner_first), :
                    ]

            over_columns(columns, column)
    stores = []
    for s in range(count):

        def plane(c, carry):
            def walk(source, source_base, number, store):
                pairs = [Group(side, start) for side in range(2) for start in strip.mirror(side, starts[number])]
                keeps = {group: strip.keep(group[0], group[1]) for group in pairs}

                def load(j, group):
                    side, start, offset = group
                    return source(side, j, start + offset - source_base(side))

                def put(j, group, value):
                    side, start, _ = group
                    store(side, j, start, masked(keeps[group], value))

                sweep(load, pairs, columns, put)

            def fill(target, number, inner, inner_base):
                for side in range(2):
                    (there,) = strip.mirror(side, [copied[number]])
                    for j in range(columns):
                        target[side, j, eight(there - base(side, number)), :] = inner[
                            s, c, j, eight(there - inner_base), :
                        ]

            def store_once(side, j, start, value):
                once[side, j, eight(start - base(side, 1)), :] = value

            def store_twice(side, j, start, value):
                twice[side, j, eight(start - base(side, 2)), :] = value

            def store_last(side, j, start, value):
                if last:
                    at = start if side == 0 else start - (rows - 2 * ROWS)
                    stage[s, side, c, at : at + ROWS, cols(j)] = value * relax_scale
                else:
                    at = start + 4 if side == 0 else start - (rows - ROWS - 4)
                    next_field[s, c, side, j, eight(at), :] = value * relax_scale

            fill(once, 1, inner_once, inner_first + 1)
            fill(twice, 2, inner_twice, inner_first + 2)
            walk(
                lambda side, j, at: moved[s, c, side, j, eight(at), :],
                lambda side: base(side, 0), 1, store_once,
            )
            walk(lambda side, j, at: once[side, j, eight(at), :], lambda side: base(side, 1), 2, store_twice)
            walk(lambda side, j, at: twice[side, j, eight(at), :], lambda side: base(side, 2), 3, store_last)
            return carry

        lax.fori_loop(0, 2, plane, 0)
        if last:
            for side in range(2):
                copy = pltpu.make_async_copy(
                    stage.at[s, side],
                    result.at[s, :, pl.ds(0 if side == 0 else rows - 2 * ROWS, 2 * ROWS)],
                    sems.at[2 * s + side],
                )
                copy.start()
                stores.append(copy)
            continue

        def column(j):
            for side in range(2):
                for start in strip.mirror(side, starts[3]):
                    at = (s, side, j, eight(edge_at(rows, start)))
                    inside = (side, j, eight(start + 4 if side == 0 else start - (rows - ROWS - 4)))
                    next_linear[s][eight(next_edge_row(rows, j, start)), :] = (
                        warped[at]
                        + next_field[(s, 0) + inside] * grow[at]
                        + next_field[(s, 1) + inside] * gcol[at]
                    )

        over_columns(columns, column)
    for copy in stores:
        copy.wait()


def exchange(low, high, axis):
    count = lax.axis_size(axis)
    forward = [(i, i + 1) for i in range(count - 1)]
    backward = [(i + 1, i) for i in range(count - 1)]
    return lax.ppermute(high, axis, forward), lax.ppermute(low, axis, backward)


def local(sections, displacement, offsets, fractions, weights):
    count, rows, width = sections.shape
    columns = width // LANES
    inner = rows - 2 * ROWS
    core = inner - ROWS
    sem = pltpu.SemaphoreType.DMA
    s, v, h = "s", "v", "h"
    sections = pltpu.with_memory_space_constraint(sections, pltpu.HBM)
    displacement = pltpu.with_memory_space_constraint(displacement, pltpu.HBM)

    def band(*lead, height):
        return (v, vmem(*lead, columns, height, LANES))

    def many(items):
        return [(v, item) for item in items]

    to_next, to_last = run(
        pack_kernel,
        "pack",
        [(s, offsets), (s, fractions), (h, sections), (h, displacement)],
        [(v, vmem(count, columns + 1, PACKED, LANES))] * 2,
        edge_scratch(count, width),
        1_000_000,
    )
    from_last, from_next = exchange(to_last, to_next, "tile")

    warped, grow, gcol, field, *linear = run(
        functools.partial(first_inner_kernel, count),
        "first_inner",
        [(s, offsets), (s, fractions), (h, sections), (h, displacement)],
        [band(count, height=rows)]
        + [band(count, height=inner)] * 2
        + [band(count, 2, height=inner)]
        + [band(height=inner)] * count,
        [
            vmem(count, rows + 2 * ROWS, width),
            vmem(count, 2, inner, width),
            vmem(columns + 3, rows, LANES),
            sem((3 * count,)),
        ],
        8_000_000,
    )
    low_1, high_1 = exchange(linear[0], linear[-1], "sec")

    edge_warped, edge_grow, edge_gcol, edge_field, *edge_linear = run(
        functools.partial(first_edge_kernel, count, rows),
        "first_edge",
        [(s, offsets), (s, fractions), (h, sections), (h, displacement), (v, from_last), (v, from_next)]
        + many((warped, grow, gcol)),
        [band(count, 2, height=3 * ROWS)] * 3
        + [band(count, 2, 2, height=2 * ROWS)]
        + [(v, vmem(columns * FIRST_EDGE, LANES))] * count,
        edge_scratch(count, width) + [vmem(columns + 3, 4 * ROWS, LANES)],
        5_000_000,
    )
    low_2, high_2 = exchange(edge_linear[0], edge_linear[-1], "sec")

    moved, once, twice, next_field, *next_linear = run(
        functools.partial(inner_kernel, count, rows, False),
        "inner",
        [(s, weights)] + many((low_1, high_1, *linear, grow, gcol, warped, field)),
        [band(count, 2, height=inner)] * 3
        + [band(count, 2, height=core)]
        + [band(height=core)] * count,
        [],
        8_000_000,
    )
    low_3, high_3 = exchange(next_linear[0], next_linear[-1], "sec")

    span = [vmem(count, 2, 2, columns, 3 * ROWS, LANES)] + [vmem(2, columns, 3 * ROWS, LANES)] * 2
    edge_field, *edge_linear = run(
        functools.partial(edge_kernel, count, rows, False),
        "edge",
        [(s, weights)]
        + many((low_2, high_2, *edge_linear, edge_grow, edge_gcol, edge_warped, edge_field, moved, once, twice)),
        [(v, vmem(count, 2, 2, columns, 2 * ROWS, LANES))]
        + [(v, vmem(columns * NEXT_EDGE, LANES))] * count,
        span,
        8_000_000,
    )
    low_4, high_4 = exchange(edge_linear[0], edge_linear[-1], "sec")

    moved, once, twice, result = run(
        functools.partial(inner_kernel, count, rows, True),
        "last_inner",
        [(s, weights)] + many((low_3, high_3, *next_linear, grow, gcol, next_field)),
        [band(count, 2, height=core)] * 3 + [(h, hbm(count, 2, rows, width))],
        [vmem(count, 2, rows - 4 * ROWS, width), sem((count,))],
        80_000_000,
    )
    (result,) = run(
        functools.partial(edge_kernel, count, rows, True),
        "last_edge",
        [(s, weights)]
        + many((low_4, high_4, *edge_linear, edge_grow, edge_gcol, edge_field, moved, once, twice))
        + [(h, result)],
        [(h, hbm(count, 2, rows, width))],
        span + [vmem(count, 2, 2, 2 * ROWS, width), sem((2 * count,))],
        8_000_000,
        aliases={3 + count + 6: 0},
    )
    return result


def solution(mesh):
    return jax.shard_map(
        local,
        mesh=mesh,
        in_specs=(
            P("sec", "tile", None),
            P("sec", None, "tile", None),
            P("sec", "tile", None),
            P("sec", "tile", None),
            P("sec", None),
        ),
        out_specs=P("sec", None, "tile", None),
        check_vma=False,
    )
```

time: 182 us -> 89.3 us (0.49)
  the two profiles are of different devices: /device:TPU:4 before, /device:TPU:2 now
where the time goes in v2:
time: 89.3 us; the launch traced here: 87.7 us
  Pallas kernels  44.6 us (50%)
  starting transfers between devices  26 us (29%)
  waiting for transfers between devices  15.4 us (17%)
  local copies, waits for them, and re-layouts  1.36 us (2%)
    pallas_call x7, Pallas kernels, run(): pl.pallas_call(kernel, out_shape=[shape for _, shape in outs], in_specs=[...  44.6 us
    ppermute x5, starting transfers between devices, exchange(): lax.ppermute(high, axis, forward)  17 us
    ppermute x5, waiting for transfers between devices, exchange(): lax.ppermute(low, axis, backward)  10.9 us
    ppermute x5, starting transfers between devices, exchange(): lax.ppermute(low, axis, backward)  8.99 us
    ppermute x5, waiting for transfers between devices, exchange(): lax.ppermute(high, axis, forward)  4.48 us
  transfers between devices with their start and end apart: 10, of which 6 were waited for; matrix products, arithmetic and copies ran while one was open for 0% of the time, Pallas kernels for 41%

profile of v2, /device:TPU:2, one launch (start us, length us, event | category | flops | bytes accessed | tf_op | source)
XLA Modules:
  0.0 87.7 jit_solution(12420582518918518824)
XLA Ops:
  0.0 0.7 copy-done.1
  1.4 2.3 %pack.1 = (f32[2,33,24,128]{3,2,1,0:T(8,128)S(1)}, f32[2,33,24,128]{3,2,1,0:T(8,128)S(1)}) custom-call(s32[2,1,2]{2,1,0:T(1,128)S(1)} %copy-done.1, s32[2,1,2]{2,1,0:T(1,128)S(1)} %copy-done.2, f32[2,64,4096]{2,1,0:T(8,128)} %sections.5, f32[2,2,64,4096]{3,2,1,0:T(8,128)} %field.5), custom_call_target="tpu_custom_call" | custom-call | flops 1000000 | bytes 1000000 | tf_op jit(solution)/shard_map/pack/pallas_call | solution.py:220
  3.7 1.9 %collective-permute-start = (f32[2,33,24,128]{3,2,1,0:T(8,128)S(1)}, f32[2,33,24,128]{3,2,1,0:T(8,128)S(1)}, u32[]{:S(2)}, u32[]{:S(2)}) collective-permute-start(f32[2,33,24,128]{3,2,1,0:T(8,128)S(1)} %get-tuple-element.32), channel_id=1, source_target_pairs={{0,1},{1,2},{2,3},{3,4},{4,5},{5,6},{6,7},{8,9},{9,10},{10,11},{11... | collective-permute-start | bytes 2433032 | tf_op jit(solution)/shard_map/ppermute | solution.py:689
  5.6 3.6 %collective-permute-start.1 = (f32[2,33,24,128]{3,2,1,0:T(8,128)S(1)}, f32[2,33,24,128]{3,2,1,0:T(8,128)S(1)}, u32[]{:S(2)}, u32[]{:S(2)}) collective-permute-start(f32[2,33,24,128]{3,2,1,0:T(8,128)S(1)} %get-tuple-element.33), channel_id=1, source_target_pairs={{1,0},{2,1},{3,2},{4,3},{5,4},{6,5},{7,6},{9,8},{10,9},{11,10},{12... | collective-permute-start | bytes 2433032 | tf_op jit(solution)/shard_map/ppermute | solution.py:689
  9.3 9.2 %first_inner.1 = (f32[2,32,64,128]{3,2,1,0:T(8,128)S(1)}, f32[2,32,48,128]{3,2,1,0:T(8,128)S(1)}, f32[2,32,48,128]{3,2,1,0:T(8,128)S(1)}, f32[2,2,32,48,128]{4,3...) custom-call(s32[2,1,2]{2,1,0:T(1,128)S(1)} %copy-done.1, s32[2,1,2]{2,1,0:T(1,128)S(1)} %copy-done.2, ...), custom_call_target="tpu_custom_call" | custom-call | flops 8000000 | bytes 8000000 | tf_op jit(solution)/shard_map/first_inner/pallas_call | solution.py:220
  18.5 3.5 %collective-permute-start.4 = (f32[32,48,128]{2,1,0:T(8,128)S(1)}, f32[32,48,128]{2,1,0:T(8,128)S(1)}, u32[]{:S(2)}, u32[]{:S(2)}) collective-permute-start(f32[32,48,128]{2,1,0:T(8,128)S(1)} %get-tuple-element.43.refs_3_), channel_id=1, source_target_pairs={{0,8},{8,16},{16,24},{1,9},{9,17},{17,25},{2,10},{10,18},{18,26},{... | collective-permute-start | bytes 2359304 | tf_op jit(solution)/shard_map/ppermute | solution.py:689
  22.0 1.3 %collective-permute-start.5 = (f32[32,48,128]{2,1,0:T(8,128)S(1)}, f32[32,48,128]{2,1,0:T(8,128)S(1)}, u32[]{:S(2)}, u32[]{:S(2)}) collective-permute-start(f32[32,48,128]{2,1,0:T(8,128)S(1)} %get-tuple-element.44.refs_2_), channel_id=1, source_target_pairs={{8,0},{16,8},{24,16},{9,1},{17,9},{25,17},{10,2},{18,10},{26,18},{... | collective-permute-start | bytes 2359304 | tf_op jit(solution)/shard_map/ppermute | solution.py:689
  23.3 1.6 %collective-permute-done.1.from_next = f32[2,33,24,128]{3,2,1,0:T(8,128)S(1)} collective-permute-done((f32[2,33,24,128]{3,2,1,0:T(8,128)S(1)}, f32[2,33,24,128]{3,2,1,0:T(8,128)S(1)}, u32[]{:S(2)}, u32[]{:S(2)}) %collective-permute-start.1) | collective-permute-done | bytes 811040 | tf_op jit(solution)/shard_map/ppermute | solution.py:689
  25.0 7.0 %first_edge.1 = (f32[2,2,32,24,128]{4,3,2,1,0:T(8,128)S(1)}, f32[2,2,32,24,128]{4,3,2,1,0:T(8,128)S(1)}, f32[2,2,32,24,128]{4,3,2,1,0:T(8,128)S(1)}, f32[2,2,2,3...) custom-call(s32[2,1,2]{2,1,0:T(1,128)S(1)} %copy-done.1, s32[2,1,2]{2,1,0:T(1,128)S(1)} %copy-done.2, ...), custom_call_target="tpu_custom_call" | custom-call | flops 5000000 | bytes 5000000 | tf_op jit(solution)/shard_map/first_edge/pallas_call | solution.py:220
  32.0 3.5 %collective-permute-start.2 = (f32[896,128]{1,0:T(8,128)S(1)}, f32[896,128]{1,0:T(8,128)S(1)}, u32[]{:S(2)}, u32[]{:S(2)}) collective-permute-start(f32[896,128]{1,0:T(8,128)S(1)} %get-tuple-element.37.refs_3_), channel_id=1, source_target_pairs={{0,8},{8,16},{16,24},{1,9},{9,17},{17,25},{2,10},{10,18},{18,26},{... | collective-permute-start | bytes 1376264 | tf_op jit(solution)/shard_map/ppermute | solution.py:689
  35.5 1.3 %collective-permute-start.3 = (f32[896,128]{1,0:T(8,128)S(1)}, f32[896,128]{1,0:T(8,128)S(1)}, u32[]{:S(2)}, u32[]{:S(2)}) collective-permute-start(f32[896,128]{1,0:T(8,128)S(1)} %get-tuple-element.38.refs_2_), channel_id=1, source_target_pairs={{8,0},{16,8},{24,16},{9,1},{17,9},{25,17},{10,2},{18,10},{26,18},{... | collective-permute-start | bytes 1376264 | tf_op jit(solution)/shard_map/ppermute | solution.py:689
  36.8 3.1 %collective-permute-done.4.refs_0_ = f32[32,48,128]{2,1,0:T(8,128)S(1)} collective-permute-done((f32[32,48,128]{2,1,0:T(8,128)S(1)}, f32[32,48,128]{2,1,0:T(8,128)S(1)}, u32[]{:S(2)}, u32[]{:S(2)}) %collective-permute-start.4) | collective-permute-done | bytes 786464 | tf_op jit(solution)/shard_map/ppermute | solution.py:689
  39.9 4.4 %collective-permute-done.5.refs_1_ = f32[32,48,128]{2,1,0:T(8,128)S(1)} collective-permute-done((f32[32,48,128]{2,1,0:T(8,128)S(1)}, f32[32,48,128]{2,1,0:T(8,128)S(1)}, u32[]{:S(2)}, u32[]{:S(2)}) %collective-permute-start.5) | collective-permute-done | bytes 786464 | tf_op jit(solution)/shard_map/ppermute | solution.py:689
  44.3 7.3 %inner.1 = (f32[2,2,32,48,128]{4,3,2,1,0:T(8,128)S(1)}, f32[2,2,32,48,128]{4,3,2,1,0:T(8,128)S(1)}, f32[2,2,32,48,128]{4,3,2,1,0:T(8,128)S(1)}, f32[2,2,32,40,12...) custom-call(s32[2,2]{1,0:T(2,128)S(1)} %copy-done, ...), custom_call_target="tpu_custom_call" | custom-call | flops 8000000 | bytes 8000000 | tf_op jit(solution)/shard_map/inner/pallas_call | solution.py:220
  51.6 3.5 %collective-permute-start.8 = (f32[32,40,128]{2,1,0:T(8,128)S(1)}, f32[32,40,128]{2,1,0:T(8,128)S(1)}, u32[]{:S(2)}, u32[]{:S(2)}) collective-permute-start(f32[32,40,128]{2,1,0:T(8,128)S(1)} %get-tuple-element.52.refs_3_), channel_id=1, source_target_pairs={{0,8},{8,16},{16,24},{1,9},{9,17},{17,25},{2,10},{10,18},{18,26},{... | collective-permute-start | bytes 1966088 | tf_op jit(solution)/shard_map/ppermute | solution.py:689
  55.1 1.3 %collective-permute-start.9 = (f32[32,40,128]{2,1,0:T(8,128)S(1)}, f32[32,40,128]{2,1,0:T(8,128)S(1)}, u32[]{:S(2)}, u32[]{:S(2)}) collective-permute-start(f32[32,40,128]{2,1,0:T(8,128)S(1)} %get-tuple-element.53.refs_2_), channel_id=1, source_target_pairs={{8,0},{16,8},{24,16},{9,1},{17,9},{25,17},{10,2},{18,10},{26,18},{... | collective-permute-start | bytes 1966088 | tf_op jit(solution)/shard_map/ppermute | solution.py:689
  56.4 5.6 %edge.1 = (f32[2,2,2,32,16,128]{5,4,3,2,1,0:T(8,128)S(1)}, f32[960,128]{1,0:T(8,128)S(1)}, f32[960,128]{1,0:T(8,128)S(1)}) custom-call(s32[2,2]{1,0:T(2,128)S(1)} %copy-done, f32[896,128]{1,0:T(8,128)S(1)} %collective-permute-done.2.refs_0_, f32[896,128]{1,0:T(8,128)S(1)} %collective-permute-done.3.refs_1_, f32[896,128]{1,0:T(8,128)S(1)} %get-tuple-element.38.refs_2_, ...), custom_call_target="tpu_custom_call" | custom-call | flops 8000000 | bytes 8000000 | tf_op jit(solution)/shard_map/edge/pallas_call | solution.py:220
  62.1 4.6 %collective-permute-start.6 = (f32[960,128]{1,0:T(8,128)S(1)}, f32[960,128]{1,0:T(8,128)S(1)}, u32[]{:S(2)}, u32[]{:S(2)}) collective-permute-start(f32[960,128]{1,0:T(8,128)S(1)} %get-tuple-element.49.refs_3_), channel_id=1, source_target_pairs={{0,8},{8,16},{16,24},{1,9},{9,17},{17,25},{2,10},{10,18},{18,26},{... | collective-permute-start | bytes 1474568 | tf_op jit(solution)/shard_map/ppermute | solution.py:689
  66.6 1.5 %collective-permute-start.7 = (f32[960,128]{1,0:T(8,128)S(1)}, f32[960,128]{1,0:T(8,128)S(1)}, u32[]{:S(2)}, u32[]{:S(2)}) collective-permute-start(f32[960,128]{1,0:T(8,128)S(1)} %get-tuple-element.50.refs_2_), channel_id=1, source_target_pairs={{8,0},{16,8},{24,16},{9,1},{17,9},{25,17},{10,2},{18,10},{26,18},{... | collective-permute-start | bytes 1474568 | tf_op jit(solution)/shard_map/ppermute | solution.py:689
  68.1 1.4 %collective-permute-done.8.refs_0_ = f32[32,40,128]{2,1,0:T(8,128)S(1)} collective-permute-done((f32[32,40,128]{2,1,0:T(8,128)S(1)}, f32[32,40,128]{2,1,0:T(8,128)S(1)}, u32[]{:S(2)}, u32[]{:S(2)}) %collective-permute-start.8) | collective-permute-done | bytes 655392 | tf_op jit(solution)/shard_map/ppermute | solution.py:689
  69.5 4.2 %collective-permute-done.9.refs_1_ = f32[32,40,128]{2,1,0:T(8,128)S(1)} collective-permute-done((f32[32,40,128]{2,1,0:T(8,128)S(1)}, f32[32,40,128]{2,1,0:T(8,128)S(1)}, u32[]{:S(2)}, u32[]{:S(2)}) %collective-permute-start.9) | collective-permute-done | bytes 655392 | tf_op jit(solution)/shard_map/ppermute | solution.py:689
  73.7 6.8 %last_inner.1 = (f32[2,2,32,40,128]{4,3,2,1,0:T(8,128)S(1)}, f32[2,2,32,40,128]{4,3,2,1,0:T(8,128)S(1)}, f32[2,2,32,40,128]{4,3,2,1,0:T(8,128)S(1)}, f32[2,2,64,4096]{3,2,1,0:T(8,128)}) custom-call(s32[2,2]{1,0:T(2,128)S(1)} %copy-done, f32[32,40,128]{2,1,0:T(8,128)S(1)} %collective-permute-done.8.refs_0_, ...), custom_call_target="tpu_custom_call" | custom-call | flops 80000000 | bytes 80000000 | tf_op jit(solution)/shard_map/last_inner/pallas_call | solution.py:220
  80.5 0.7 collective-permute-done.7.refs_1_
  81.2 6.3 %last_edge.1 = f32[2,2,64,4096]{3,2,1,0:T(8,128)} custom-call(s32[2,2]{1,0:T(2,128)S(1)} %copy-done, f32[960,128]{1,0:T(8,128)S(1)} %collective-permute-done.6.refs_0_, f32[960,128]{1,0:T(8,128)S(1)} %collective-permute-done.7.refs_1_, f32[960,128]{1,0:T(8,128)S(1)} %get-tuple-element.50.refs_2_, ...), custom_call_target="tpu_custom_call", output_to_operand_aliasing={{}: (11, {})} | custom-call | flops 8000000 | bytes 8000000 | tf_op jit(solution)/shard_map/last_edge/pallas_call | solution.py:220
  (9 shorter events, 0.7 us)
Async XLA Ops:
  0.0 0.7 copy-start.1
  0.7 0.7 copy-start.2
  3.7 19.6 %collective-permute-start = (f32[2,33,24,128]{3,2,1,0:T(8,128)S(1)}, f32[2,33,24,128]{3,2,1,0:T(8,128)S(1)}, u32[]{:S(2)}, u32[]{:S(2)}) collective-permute-start(f32[2,33,24,128]{3,2,1,0:T(8,128)S(1)} %get-tuple-element.32), channel_id=1, source_target_pairs={{0,1},{1,2},{2,3},{3,4},{4,5},{5,6},{6,7},{8,9},{9,10},{10,11},{11... | collective-permute-start | bytes 2433032 | tf_op jit(solution)/shard_map/ppermute | solution.py:689
  5.6 19.3 %collective-permute-start.1 = (f32[2,33,24,128]{3,2,1,0:T(8,128)S(1)}, f32[2,33,24,128]{3,2,1,0:T(8,128)S(1)}, u32[]{:S(2)}, u32[]{:S(2)}) collective-permute-start(f32[2,33,24,128]{3,2,1,0:T(8,128)S(1)} %get-tuple-element.33), channel_id=1, source_target_pairs={{1,0},{2,1},{3,2},{4,3},{5,4},{6,5},{7,6},{9,8},{10,9},{11,10},{12... | collective-permute-start | bytes 2433032 | tf_op jit(solution)/shard_map/ppermute | solution.py:689
  18.5 21.4 %collective-permute-start.4 = (f32[32,48,128]{2,1,0:T(8,128)S(1)}, f32[32,48,128]{2,1,0:T(8,128)S(1)}, u32[]{:S(2)}, u32[]{:S(2)}) collective-permute-start(f32[32,48,128]{2,1,0:T(8,128)S(1)} %get-tuple-element.43.refs_3_), channel_id=1, source_target_pairs={{0,8},{8,16},{16,24},{1,9},{9,17},{17,25},{2,10},{10,18},{18,26},{... | collective-permute-start | bytes 2359304 | tf_op jit(solution)/shard_map/ppermute | solution.py:689
  22.0 22.3 %collective-permute-start.5 = (f32[32,48,128]{2,1,0:T(8,128)S(1)}, f32[32,48,128]{2,1,0:T(8,128)S(1)}, u32[]{:S(2)}, u32[]{:S(2)}) collective-permute-start(f32[32,48,128]{2,1,0:T(8,128)S(1)} %get-tuple-element.44.refs_2_), channel_id=1, source_target_pairs={{8,0},{16,8},{24,16},{9,1},{17,9},{25,17},{10,2},{18,10},{26,18},{... | collective-permute-start | bytes 2359304 | tf_op jit(solution)/shard_map/ppermute | solution.py:689
  25.0 19.3 %copy-start = (s32[2,2]{1,0:T(2,128)S(1)}, s32[2,2]{1,0:T(2,128)}, u32[]{:S(2)}) copy-start(s32[2,2]{1,0:T(2,128)} %weights.7) | copy-start | bytes 52
  32.0 24.4 %collective-permute-start.2 = (f32[896,128]{1,0:T(8,128)S(1)}, f32[896,128]{1,0:T(8,128)S(1)}, u32[]{:S(2)}, u32[]{:S(2)}) collective-permute-start(f32[896,128]{1,0:T(8,128)S(1)} %get-tuple-element.37.refs_3_), channel_id=1, source_target_pairs={{0,8},{8,16},{16,24},{1,9},{9,17},{17,25},{2,10},{10,18},{18,26},{... | collective-permute-start | bytes 1376264 | tf_op jit(solution)/shard_map/ppermute | solution.py:689
  35.5 20.9 %collective-permute-start.3 = (f32[896,128]{1,0:T(8,128)S(1)}, f32[896,128]{1,0:T(8,128)S(1)}, u32[]{:S(2)}, u32[]{:S(2)}) collective-permute-start(f32[896,128]{1,0:T(8,128)S(1)} %get-tuple-element.38.refs_2_), channel_id=1, source_target_pairs={{8,0},{16,8},{24,16},{9,1},{17,9},{25,17},{10,2},{18,10},{26,18},{... | collective-permute-start | bytes 1376264 | tf_op jit(solution)/shard_map/ppermute | solution.py:689
  51.6 17.9 %collective-permute-start.8 = (f32[32,40,128]{2,1,0:T(8,128)S(1)}, f32[32,40,128]{2,1,0:T(8,128)S(1)}, u32[]{:S(2)}, u32[]{:S(2)}) collective-permute-start(f32[32,40,128]{2,1,0:T(8,128)S(1)} %get-tuple-element.52.refs_3_), channel_id=1, source_target_pairs={{0,8},{8,16},{16,24},{1,9},{9,17},{17,25},{2,10},{10,18},{18,26},{... | collective-permute-start | bytes 1966088 | tf_op jit(solution)/shard_map/ppermute | solution.py:689
  55.1 18.6 %collective-permute-start.9 = (f32[32,40,128]{2,1,0:T(8,128)S(1)}, f32[32,40,128]{2,1,0:T(8,128)S(1)}, u32[]{:S(2)}, u32[]{:S(2)}) collective-permute-start(f32[32,40,128]{2,1,0:T(8,128)S(1)} %get-tuple-element.53.refs_2_), channel_id=1, source_target_pairs={{8,0},{16,8},{24,16},{9,1},{17,9},{25,17},{10,2},{18,10},{26,18},{... | collective-permute-start | bytes 1966088 | tf_op jit(solution)/shard_map/ppermute | solution.py:689
  62.1 18.4 %collective-permute-start.6 = (f32[960,128]{1,0:T(8,128)S(1)}, f32[960,128]{1,0:T(8,128)S(1)}, u32[]{:S(2)}, u32[]{:S(2)}) collective-permute-start(f32[960,128]{1,0:T(8,128)S(1)} %get-tuple-element.49.refs_3_), channel_id=1, source_target_pairs={{0,8},{8,16},{16,24},{1,9},{9,17},{17,25},{2,10},{10,18},{18,26},{... | collective-permute-start | bytes 1474568 | tf_op jit(solution)/shard_map/ppermute | solution.py:689
  66.6 14.6 %collective-permute-start.7 = (f32[960,128]{1,0:T(8,128)S(1)}, f32[960,128]{1,0:T(8,128)S(1)}, u32[]{:S(2)}, u32[]{:S(2)}) collective-permute-start(f32[960,128]{1,0:T(8,128)S(1)} %get-tuple-element.50.refs_2_), channel_id=1, source_target_pairs={{8,0},{16,8},{24,16},{9,1},{17,9},{25,17},{10,2},{18,10},{26,18},{... | collective-permute-start | bytes 1474568 | tf_op jit(solution)/shard_map/ppermute | solution.py:689

commit v3 on v0

v3 whole, which is shorter than its diff:
```python
import functools

import jax
import jax.numpy as jnp
from jax import lax
from jax.experimental import pallas as pl
from jax.experimental.pallas import tpu as pltpu
from jax.sharding import PartitionSpec as P


relax_scale = 0.2**3
softening = 0.25
F32 = jnp.float32
REACH = 12
BELOW = 6
HALF = BELOW // 2
PACKED = REACH + 2 * BELOW
LANES = 128
ROWS = 8
VMEM_LIMIT = 20 * 1024 * 1024


def iotas():
    return (
        lax.broadcasted_iota(jnp.int32, (ROWS, LANES), 0),
        lax.broadcasted_iota(jnp.int32, (ROWS, LANES), 1),
    )


def cols(j):
    return slice(j * LANES, (j + 1) * LANES)


def tile(i):
    if isinstance(i, int):
        return slice(i * ROWS, (i + 1) * ROWS)
    return pl.ds(pl.multiple_of(i * ROWS, ROWS), ROWS)


def eight(row):
    return pl.ds(row, ROWS)


def groups(first, last):
    starts = list(range(first, last - ROWS + 2, ROWS))
    if starts[-1] + ROWS - 1 < last:
        starts.append(last - ROWS + 1)
    return starts


def col_before(here, left, lane_last):
    return pltpu.roll(lax.select(lane_last, left, here), 1, 1)


def col_after(here, right, lane_first):
    return pltpu.roll(lax.select(lane_first, right, here), LANES - 1, 1)


class Group(tuple):
    def __new__(cls, key, start, offset=0):
        return super().__new__(cls, (key, start, offset))

    def __add__(self, n):
        return Group(self[0], self[1], self[2] + n)

    def __sub__(self, n):
        return Group(self[0], self[1], self[2] - n)


def sweep(prepare, load, starts, columns, finish):
    _, lane = iotas()
    lane_first, lane_last = lane == 0, lane == LANES - 1
    zero = jnp.zeros((ROWS, LANES), F32)
    prepare(0)
    left = [zero] * len(starts)
    here = [load(0, start) for start in starts]
    for j in range(columns):
        if j + 1 < columns:
            prepare(j + 1)
        right = [load(j + 1, start) if j + 1 < columns else zero for start in starts]
        sums = []
        for k, start in enumerate(starts):
            total = here[k] + (load(j, start - 1) + load(j, start + 1))
            sums.append(
                total + (col_before(here[k], left[k], lane_last) + col_after(here[k], right[k], lane_first))
            )
        finish(j, sums)
        left, here = here, right


def nothing(j):
    pass


def derive(load, starts, columns, body):
    _, lane = iotas()
    lane_first, lane_last = lane == 0, lane == LANES - 1
    zero = jnp.zeros((ROWS, LANES), F32)
    left = [zero] * len(starts)
    here = [load(0, start) for start in starts]
    for j in range(columns):
        right = [load(j + 1, start) if j + 1 < columns else zero for start in starts]
        for k, start in enumerate(starts):
            grad_rows = 0.5 * (load(j, start + 1) - load(j, start - 1))
            grad_cols = 0.5 * (col_after(here[k], right[k], lane_first) - col_before(here[k], left[k], lane_last))
            body(j, start, here[k], grad_rows, grad_cols)
        left, here = here, right


def warp(jobs, columns):
    row, lane = iotas()
    zero = jnp.zeros((ROWS, LANES), F32)
    state = []
    for pick, (row_shift, col_shift, row_part, col_part), store in jobs:
        within = jnp.where(row_shift < 0, row_shift + ROWS, row_shift)
        turn = jnp.where(within == 0, 0, ROWS - within)
        side = jnp.where(col_shift < 0, col_shift + LANES, col_shift)
        back = jnp.where(side == 0, 0, LANES - side)
        state.append(
            dict(
                pick=pick, store=store, turn=turn, turn_next=ROWS - 1 - within, back=back,
                back_next=LANES - 1 - side, row_part=row_part, col_part=col_part,
                rows=row < within, rows_next=row < within + 1, wraps=lane < side, wraps_next=lane < side + 1,
                up=jnp.broadcast_to(row_shift, (ROWS, LANES)) < 0,
                back_first=jnp.broadcast_to(col_shift, (ROWS, LANES)) < 0,
            )
        )

    def line(job, j):
        if not 0 <= j < columns:
            return zero
        a, b = job["pick"](j, job["up"])
        upper = pltpu.roll(lax.select(job["rows"], b, a), job["turn"], 0)
        lower = pltpu.roll(lax.select(job["rows_next"], b, a), job["turn_next"], 0)
        return (1.0 - job["row_part"]) * upper + job["row_part"] * lower

    for job in state:
        job["line"] = line(job, 0)
        job["here"] = lax.select(job["back_first"], zero, job["line"])
    for j in range(columns):
        for job in state:
            next_line = line(job, j + 1)
            after = lax.select(job["back_first"], job["line"], next_line)
            first = pltpu.roll(lax.select(job["wraps"], after, job["here"]), job["back"], 1)
            second = pltpu.roll(lax.select(job["wraps_next"], after, job["here"]), job["back_next"], 1)
            job["store"](j, (1.0 - job["col_part"]) * first + job["col_part"] * second)
            job["line"], job["here"] = next_line, after


def force(linear, lower, upper, grad_rows, grad_cols, weight_lower, weight_upper):
    denominator = grad_rows * grad_rows + grad_cols * grad_cols + softening
    lower_diff = lower - linear
    upper_diff = upper - linear
    below = denominator + lower_diff * lower_diff
    above = denominator + upper_diff * upper_diff
    top = (weight_lower * lower_diff) * above + (weight_upper * upper_diff) * below
    bottom = below * above
    inverse = pl.reciprocal(bottom, approx=True)
    inverse = inverse * (2.0 - bottom * inverse)
    return top * inverse


def half_weights(weights_ref, s, sections):
    number = lax.axis_index("sec") * sections + s
    lower = jnp.where(number > 0, weights_ref[s, 0], 0).astype(F32) * 0.5
    upper = jnp.where(number < sections * lax.axis_size("sec") - 1, weights_ref[s, 1], 0).astype(F32) * 0.5
    return lower, upper


def spread_weights(weights_ref, halves, sections):
    for s in range(sections):
        for k, weight in enumerate(half_weights(weights_ref, s, sections)):
            halves[s, k] = jnp.broadcast_to(weight, (ROWS, LANES))


def shift_of(offsets_ref, fractions_ref, s):
    return (
        offsets_ref[s, 0, 0],
        offsets_ref[s, 0, 1],
        fractions_ref[s, 0, 0].astype(F32) * (1.0 / 256.0),
        fractions_ref[s, 0, 1].astype(F32) * (1.0 / 256.0),
    )


def copy_in(pairs, sems):
    copies = [pltpu.make_async_copy(a, b, sems.at[k]) for k, (a, b) in enumerate(pairs)]
    for copy in copies:
        copy.start()
    return copies


class Strip:
    def __init__(self, rows):
        self.rows = rows

    def mirror(self, side, starts):
        return starts if side == 0 else [self.rows - ROWS - start for start in starts]

    def keep(self, side, start):
        row, _ = iotas()
        strip = lax.axis_index("tile")
        if start < 0:
            return row >= jnp.where(strip > 0, -ROWS, -start)
        if start + ROWS > self.rows:
            return row < jnp.where(strip < lax.axis_size("tile") - 1, 2 * ROWS, self.rows - start)
        return None


def masked(keep, value):
    return value if keep is None else lax.select(keep, value, jnp.zeros_like(value))


def vmem(*shape):
    return pltpu.VMEM(shape, F32)


def hbm(*shape):
    return jax.ShapeDtypeStruct(shape, F32)


SPECS = {
    "s": pl.BlockSpec(memory_space=pltpu.SMEM),
    "v": pl.BlockSpec(memory_space=pltpu.VMEM),
    "h": pl.BlockSpec(memory_space=pltpu.HBM),
    "a": pl.BlockSpec(memory_space=pl.ANY),
}


def run(kernel, name, ins, outs, scratch, cost, aliases=None):
    return pl.pallas_call(
        kernel,
        out_shape=[shape for _, shape in outs],
        in_specs=[SPECS[kind] for kind, _ in ins],
        out_specs=[SPECS[kind] for kind, _ in outs],
        scratch_shapes=scratch,
        input_output_aliases=aliases or {},
        cost_estimate=pl.CostEstimate(flops=cost, bytes_accessed=cost, transcendentals=0),
        compiler_params=pltpu.CompilerParams(vmem_limit_bytes=VMEM_LIMIT),
        name=name,
    )(*[value for _, value in ins])


def pack_kernel(
    far_offsets, far_fractions, sections, field, to_next, to_last,
    plane, edge_field, sems, offsets, fractions, scalar_sems,
):
    count, rows, width = sections.shape
    columns = width // LANES
    _, lane = iotas()
    lane = lane[:1]
    scalars = copy_in([(far_offsets, offsets), (far_fractions, fractions)], scalar_sems)
    loads = load_edges(sections, field, plane, edge_field, sems)
    for copy in scalars:
        copy.wait()
    for s in range(count):
        values = jnp.zeros((1, LANES), F32)
        for k, value in enumerate(
            (offsets[s, 0, 0], offsets[s, 0, 1], fractions[s, 0, 0], fractions[s, 0, 1])
        ):
            values = jnp.where(lane == k, value.astype(F32), values)
        values = jnp.broadcast_to(values, (PACKED, LANES))
        to_next[s, columns] = values
        to_last[s, columns] = values
    for copy in loads:
        copy.wait()
    for s in range(count):
        for j in range(columns):
            to_next[s, j, :REACH, :] = plane[s, 1, 2 * ROWS - REACH :, cols(j)]
            to_last[s, j, :REACH, :] = plane[s, 0, :REACH, cols(j)]
            for c in range(2):
                part = slice(REACH + c * BELOW, REACH + (c + 1) * BELOW)
                to_next[s, j, part, :] = edge_field[s, c, 1, ROWS - BELOW :, cols(j)]
                to_last[s, j, part, :] = edge_field[s, c, 0, :BELOW, cols(j)]


def load_edges(sections, field, plane, edge_field, sems):
    rows = sections.shape[1]
    reach = 2 * ROWS
    return copy_in(
        [
            (sections.at[:, pl.ds(0, reach)], plane.at[:, 0]),
            (sections.at[:, pl.ds(rows - reach, reach)], plane.at[:, 1]),
            (field.at[:, :, pl.ds(0, ROWS)], edge_field.at[:, :, 0]),
            (field.at[:, :, pl.ds(rows - ROWS, ROWS)], edge_field.at[:, :, 1]),
        ],
        sems,
    )


def edge_scratch(count, width):
    return [
        vmem(count, 2, 2 * ROWS, width),
        vmem(count, 2, 2, ROWS, width),
        pltpu.SemaphoreType.DMA((4,)),
    ]


def first_inner_kernel(count, offsets, fractions, sections, field, *refs):
    for s in range(count):
        first_inner_section(s, offsets, fractions, sections, field, *refs[4 * s : 4 * s + 4])


def first_inner_section(s, offsets, fractions, sections, field, warped, grow, gcol, linear):
    _, rows, width = sections.shape
    columns = width // LANES
    tiles = rows // ROWS
    first = 2 * ROWS - BELOW
    at_once = 4 if tiles % 4 == 0 else 1
    shift = shift_of(offsets, fractions, s)

    def step(group, carry):
        def job(i):
            base = i + jnp.where(shift[0] < 0, -1, 0)

            def pick(j, negative):
                return tuple(sections[s, tile(jnp.clip(base + k, 0, tiles - 1)), cols(j)] for k in range(2))

            def store(j, value):
                warped[j, tile(i), :] = value

            return pick, shift, store

        warp([job(group * at_once + k) for k in range(at_once)], columns)
        return carry

    lax.fori_loop(0, tiles // at_once, step, 0)

    def body(j, start, here, grad_rows, grad_cols):
        at = (j, eight(start - first))
        grow[at] = grad_rows
        gcol[at] = grad_cols
        u = field_rows(field, s, 0, j, start)
        v = field_rows(field, s, 1, j, start)
        linear[eight(inner_row(rows, BELOW, j, start)), :] = here + u * grad_rows + v * grad_cols

    derive(lambda j, start: warped[j, eight(start), :], groups(first, rows - first - 1), columns, body)


def field_rows(field, s, c, j, start):
    i, within = divmod(start, ROWS)
    here = field[s, c, tile(i), cols(j)]
    if within == 0:
        return here
    row, _ = iotas()
    return pltpu.roll(lax.select(row < within, field[s, c, tile(i + 1), cols(j)], here), ROWS - within, 0)


def inner_row(rows, halo, j, row):
    return j * (rows - 2 * (2 * ROWS - halo)) + row - (2 * ROWS - halo)


def edge_row(rows, halo, j, row):
    return j * 4 * ROWS + (row + halo if row < rows // 2 else row - (rows - 2 * ROWS + halo) + 2 * ROWS)


def edge_at(rows, halo, row):
    return row + halo if row < rows // 2 else row - (rows + halo - 3 * ROWS)


def first_edge_kernel(
    count, rows, offsets, fractions, weights, sections, field, from_last, from_next,
    *refs
):
    inner_refs, (warped, grow, gcol, field_band, halves, *linear) = refs[: 3 * count], refs[3 * count :]
    spread_weights(weights, halves, count)
    width = sections.shape[2]
    columns = width // LANES
    tiles = rows // ROWS
    _, lane = iotas()
    received = (from_last, from_next)
    for s in range(count):
        own = shift_of(offsets, fractions, s)

        def theirs(side):
            block = received[side][s, columns, 0:1, :]
            values = [jnp.sum(jnp.where(lane[:1] == k, block, 0.0)) for k in range(4)]
            return (
                values[0].astype(jnp.int32),
                values[1].astype(jnp.int32),
                values[2] * (1.0 / 256.0),
                values[3] * (1.0 / 256.0),
            )

        def near(i, j):
            if 0 <= i < tiles:
                return sections[s, tile(i), cols(j)]
            if i == -1:
                return from_last[s, j, eight(REACH - ROWS), :]
            if i == -2:
                return pltpu.roll(from_last[s, j, eight(0), :], 2 * ROWS - REACH, 0)
            if i == tiles:
                return from_next[s, j, eight(0), :]
            return pltpu.roll(from_next[s, j, eight(REACH - ROWS), :], REACH - ROWS, 0)

        def job(i, shift):
            def pick(j, negative):
                here = near(i, j)
                return lax.select(negative, near(i - 1, j), here), lax.select(negative, here, near(i + 1, j))

            side = 0 if i < tiles // 2 else 1

            def store(j, value):
                warped[s, side, j, eight(edge_at(rows, ROWS, i * ROWS)), :] = value

            return pick, shift, store

        warp([job(-1, theirs(0)), job(0, own), job(tiles - 1, own), job(tiles, theirs(1))], columns)

        for j in range(columns):
            for side in range(2):
                beside = ROWS if side == 0 else rows - 2 * ROWS
                warped[s, side, j, eight(edge_at(rows, ROWS, beside)), :] = inner_refs[s][j, eight(beside), :]
                first = 2 * ROWS - BELOW
                beside = first if side == 0 else rows - first - ROWS
                here = eight(edge_at(rows, BELOW, beside))
                grow[s, side, j, here, :] = inner_refs[count + s][j, eight(beside - first), :]
                gcol[s, side, j, here, :] = inner_refs[2 * count + s][j, eight(beside - first), :]
            for c in range(2):
                part = slice(REACH + c * BELOW, REACH + (c + 1) * BELOW)
                field_band[s, 0, c, j, :BELOW, :] = from_last[s, j, part, :]
                field_band[s, 1, c, j, 3 * ROWS - BELOW :, :] = from_next[s, j, part, :]
                for i in (0, 1, tiles - 2, tiles - 1):
                    at = eight(edge_at(rows, BELOW, i * ROWS))
                    field_band[s, 0 if i < 2 else 1, c, j, at, :] = field[s, c, tile(i), cols(j)]

        starts = [
            Group(0, -BELOW), Group(0, ROWS - BELOW), Group(1, rows - 2 * ROWS + BELOW), Group(1, rows - ROWS + BELOW)
        ]

        def body(j, group, here, grad_rows, grad_cols):
            side, start, _ = group
            at = (j, eight(edge_at(rows, BELOW, start)))
            grow[(s, side) + at] = grad_rows
            gcol[(s, side) + at] = grad_cols
            u = field_band[(s, side, 0) + at]
            v = field_band[(s, side, 1) + at]
            linear[s][eight(edge_row(rows, BELOW, j, start)), :] = here + u * grad_rows + v * grad_cols

        def load(j, group):
            side, start, offset = group
            return warped[s, side, j, eight(edge_at(rows, ROWS, start) + offset), :]

        derive(load, starts, columns, body)


def inner_kernel(count, rows, s, last, order, weights, lower, linear, upper, *refs):
    if last:
        grow, gcol, field, *refs = refs
        moved, once, twice, stage = refs[order:]
        halo = HALF
    else:
        grow, gcol, warped, field, *refs = refs
        moved, once, twice, next_field, next_linear = refs[order:]
        halo = BELOW
    first = 2 * ROWS - halo
    columns = grow.shape[0]
    end = rows - first - 1
    weight_lower, weight_upper = weights[s, 0], weights[s, 1]

    def move(j):
        for start in groups(first, end):
            at = (eight(inner_row(rows, halo, j, start)), slice(None))
            grad_rows = grow[j, eight(start - 2 * ROWS + BELOW), :]
            grad_cols = gcol[j, eight(start - 2 * ROWS + BELOW), :]
            half = force(linear[at], lower[at], upper[at], grad_rows, grad_cols, weight_lower, weight_upper)
            for c, grad in enumerate((grad_rows, grad_cols)):
                old = field[c, j, eight(start - first), :] if last else field_rows(field, s, c, j, start)
                moved[c, j, eight(start - first), :] = old + half * grad

    def stage_of(ref, base, starts):
        def load(j, group):
            c, start, offset = group
            return ref[c, j, eight(start + offset - base), :]

        return load, [Group(c, start) for start in starts for c in range(2)]

    def keep_in(ref, base, names):
        def finish(j, sums):
            for (c, start, _), value in zip(names, sums):
                ref[c, j, eight(start - base), :] = value

        return finish

    load, _ = stage_of(moved, first, [])
    _, names = stage_of(None, 0, groups(first + 1, end - 1))
    sweep(move, load, names, columns, keep_in(once, first + 1, names))
    load, _ = stage_of(once, first + 1, [])
    _, names = stage_of(None, 0, groups(first + 2, end - 2))
    sweep(nothing, load, names, columns, keep_in(twice, first + 2, names))
    load, _ = stage_of(twice, first + 2, [])
    _, names = stage_of(None, 0, groups(first + 3, end - 3))

    def finish(j, sums):
        sums = [value * relax_scale for value in sums]
        if last:
            for (c, start, _), value in zip(names, sums):
                stage[c, start - 2 * ROWS : start - ROWS, cols(j)] = value
            return
        for k in range(0, len(names), 2):
            start = names[k][1]
            at = (j, eight(start - first))
            for c in range(2):
                next_field[c, j, eight(start - first - 3), :] = sums[k + c]
            next_linear[eight(inner_row(rows, HALF, j, start)), :] = (
                warped[j, eight(start), :] + sums[k] * grow[at] + sums[k + 1] * gcol[at]
            )

    sweep(nothing, load, names, columns, finish)


PARTS = 4


def send_part(j, columns, copies, source, target, sems):
    stops = [columns // 2, columns // 2 + columns // 4, columns - columns // 16, columns]
    if j + 1 not in stops:
        return
    n = stops.index(j + 1)
    begin = stops[n - 1] if n else 0
    part = pl.ds(begin * LANES, (j + 1 - begin) * LANES)
    copy = pltpu.make_async_copy(source(part), target(part), sems.at[n])
    copy.start()
    copies.append(copy)


def edge_kernel(count, rows, s, last, order, weights, lower, linear, upper, *refs):
    final = last and s == 0
    if last:
        grow, gcol, field, inner_moved, inner_once, inner_twice, *refs = refs
        before, refs = refs[:order], refs[order:]
        halo = HALF
        if final:
            result, moved, once, twice, stage, sems, stage_sems = refs
        else:
            stage, moved, once, twice = refs
    else:
        grow, gcol, warped, field, inner_moved, inner_once, inner_twice, *refs = refs
        next_field, next_linear, moved, once, twice = refs[order:]
        field = field.at[s]
        halo = BELOW
    columns = grow.shape[2]
    strip = Strip(rows)
    weight_lower, weight_upper = weights[s, 0], weights[s, 1]

    def starts(side, number):
        return strip.mirror(side, [number - halo, number - halo + ROWS])

    def where(number, row):
        return eight(edge_at(rows, halo - number, row))

    def move(j):
        for side in range(2):
            for start in starts(side, 0):
                at = (eight(edge_row(rows, halo, j, start)), slice(None))
                grad_rows = grow[s, side, j, eight(edge_at(rows, BELOW, start)), :]
                grad_cols = gcol[s, side, j, eight(edge_at(rows, BELOW, start)), :]
                half = force(
                    linear[at], lower[at], upper[at], grad_rows, grad_cols, weight_lower, weight_upper
                )
                for c, grad in enumerate((grad_rows, grad_cols)):
                    value = field[side, c, j, where(0, start), :] + half * grad
                    moved[c, side, j, where(0, start), :] = masked(keeps[side, start], value)
        fill(moved, 0, inner_moved, j)

    def fill(target, number, inner, j):
        first = 2 * ROWS - halo + number
        for side in range(2):
            (there,) = strip.mirror(side, [first])
            for c in range(2):
                target[c, side, j, where(number, there), :] = inner[c, j, eight(there - first), :]

    keeps = {
        (side, start): strip.keep(side, start)
        for side in range(2)
        for number in range(4)
        for start in starts(side, number)
    }

    def names_of(number):
        return [
            Group((c, side), start)
            for side in range(2)
            for start in starts(side, number)
            for c in range(2)
        ]

    def load_from(ref, number):
        def load(j, group):
            (c, side), start, offset = group
            return ref[c, side, j, eight(edge_at(rows, halo - number, start) + offset), :]

        return load

    def keep_in(ref, number):
        def finish(j, sums):
            for ((c, side), start, _), value in zip(names_of(number), sums):
                ref[c, side, j, where(number, start), :] = masked(keeps[side, start], value)

        return finish

    def ready_once(j):
        fill(once, 1, inner_once, j)

    def ready_twice(j):
        fill(twice, 2, inner_twice, j)

    def ends(side):
        return pl.ds(0 if side == 0 else rows - 2 * ROWS, 2 * ROWS)

    copies = []
    if final:
        middle = pl.ds(2 * ROWS, rows - 4 * ROWS)
        for n in range(count):
            copies.append(pltpu.make_async_copy(before[n], result.at[n, :, middle], stage_sems.at[n, 0]))
            if n != s:
                for side in range(2):
                    copies.append(
                        pltpu.make_async_copy(
                            before[count + n - 1].at[side], result.at[n, :, ends(side)], stage_sems.at[n, 1 + side]
                        )
                    )
        for copy in copies:
            copy.start()

    def finish(j, sums):
        names = names_of(3)
        for k in range(0, len(names), 2):
            (_, side), start, _ = names[k]
            values = [masked(keeps[side, start], value * relax_scale) for value in sums[k : k + 2]]
            if last:
                at = start if side == 0 else start - (rows - 2 * ROWS)
                for c, value in enumerate(values):
                    stage[side, c, at : at + ROWS, cols(j)] = value
                continue
            for c, value in enumerate(values):
                next_field[side, c, j, where(3, start), :] = value
            at = (s, side, j, eight(edge_at(rows, BELOW, start)))
            next_linear[eight(edge_row(rows, HALF, j, start)), :] = (
                warped[s, side, j, eight(edge_at(rows, ROWS, start)), :]
                + values[0] * grow[at]
                + values[1] * gcol[at]
            )
        if final:
            for side in range(2):
                send_part(j, columns, copies, lambda part: stage.at[side, :, :, part],
                          lambda part: result.at[s, :, ends(side), part], sems.at[side])

    sweep(move, load_from(moved, 0), names_of(1), columns, keep_in(once, 1))
    sweep(ready_once, load_from(once, 1), names_of(2), columns, keep_in(twice, 2))
    sweep(ready_twice, load_from(twice, 2), names_of(3), columns, finish)
    for copy in copies:
        copy.wait()


def exchange(low, high, axis):
    count = lax.axis_size(axis)
    forward = [(i, i + 1) for i in range(count - 1)]
    backward = [(i + 1, i) for i in range(count - 1)]
    return lax.ppermute(high, axis, forward), lax.ppermute(low, axis, backward)


def local(sections, displacement, offsets, fractions, weights):
    count, rows, width = sections.shape
    columns = width // LANES
    inner = columns * (rows - 4 * ROWS + 2 * BELOW)
    core = columns * (rows - 4 * ROWS + 2 * HALF)
    edge = columns * 4 * ROWS
    held = rows - 2 * ROWS
    sem = pltpu.SemaphoreType.DMA
    s, v, h = "s", "v", "h"
    near_sections = pltpu.with_memory_space_constraint(sections, pltpu.VMEM)
    near_displacement = pltpu.with_memory_space_constraint(displacement, pltpu.VMEM)
    far_offsets = pltpu.with_memory_space_constraint(offsets, pltpu.HBM)
    far_fractions = pltpu.with_memory_space_constraint(fractions, pltpu.HBM)
    sections = pltpu.with_memory_space_constraint(sections, pltpu.HBM)
    displacement = pltpu.with_memory_space_constraint(displacement, pltpu.HBM)

    def band(*lead, height):
        return (v, vmem(*lead, columns, height, LANES))

    def many(items):
        return [(v, item) for item in items]

    to_next, to_last = run(
        pack_kernel,
        "pack",
        [(h, far_offsets), (h, far_fractions), (h, sections), (h, displacement)],
        [(v, vmem(count, columns + 1, PACKED, LANES))] * 2,
        edge_scratch(count, width) + [pltpu.SMEM(offsets.shape, jnp.int32)] * 2 + [sem((2,))],
        1_000_000,
    )
    from_last, from_next = exchange(to_last, to_next, "tile")

    outs = run(
        functools.partial(first_inner_kernel, count),
        "first_inner",
        [(s, offsets), (s, fractions), (v, near_sections), (v, near_displacement)],
        ([band(height=rows)] + [band(height=held)] * 2 + [(v, vmem(inner, LANES))]) * count,
        [],
        8_000_000,
    )
    warpeds, grows, gcols, linear = (outs[k::4] for k in range(4))
    low_1, high_1 = exchange(linear[0], linear[-1], "sec")

    edge_warped, edge_grow, edge_gcol, edge_field, halves, *edge_linear = run(
        functools.partial(first_edge_kernel, count, rows),
        "first_edge",
        [(s, offsets), (s, fractions), (s, weights), (v, near_sections), (v, near_displacement)]
        + many((from_last, from_next))
        + many((*warpeds, *grows, *gcols)),
        [band(count, 2, height=3 * ROWS)] * 3
        + [band(count, 2, 2, height=3 * ROWS), (v, vmem(count, 2, ROWS, LANES))]
        + [(v, vmem(edge, LANES))] * count,
        [],
        5_000_000,
    )
    low_2, high_2 = exchange(edge_linear[0], edge_linear[-1], "sec")

    def around(linear, low, high, n):
        below = low if n == 0 else linear[n - 1]
        above = high if n == count - 1 else linear[n + 1]
        return below, linear[n], above

    inners = [None] * count
    order = [high_1]
    for n in range(count):
        inners[n] = run(
            functools.partial(inner_kernel, count, rows, n, False, len(order)),
            f"inner_{n}",
            [(v, halves)]
            + many((*around(linear, low_1, high_1, n), grows[n], gcols[n], warpeds[n], near_displacement, *order)),
            [band(2, height=held)] * 4 + [(v, vmem(core, LANES))],
            [],
            8_000_000,
        )
        order = [inners[n][4]]
    inner_linear = [outs[4] for outs in inners]
    low_3, high_3 = exchange(inner_linear[0], inner_linear[-1], "sec")

    span = [vmem(2, 2, columns, 3 * ROWS, LANES)] * 3
    edges = [None] * count
    for n in reversed(range(count)):
        edges[n] = run(
            functools.partial(edge_kernel, count, rows, n, False, len(order)),
            f"edge_{n}",
            [(v, halves)]
            + many((*around(edge_linear, low_2, high_2, n), edge_grow, edge_gcol, edge_warped, edge_field))
            + many((*inners[n][:3], *order)),
            [band(2, 2, height=3 * ROWS), (v, vmem(edge, LANES))],
            span,
            8_000_000,
        )
        order = [edges[n][1]]
    edge_linear = [outs[1] for outs in edges]
    low_4, high_4 = exchange(edge_linear[0], edge_linear[-1], "sec")

    lasts = [None] * count
    order = []
    for n in reversed(range(count)):
        lasts[n] = run(
            functools.partial(inner_kernel, count, rows, n, True, len(order)),
            f"last_inner_{n}",
            [(v, halves)]
            + many((*around(inner_linear, low_3, high_3, n), grows[n], gcols[n], inners[n][3], *order)),
            [band(2, height=held)] * 3 + [(v, vmem(2, rows - 4 * ROWS, width))],
            [],
            40_000_000,
        )
        order = [lasts[n][3]]
    middles = [outs[3] for outs in lasts]
    staged = []
    ends = (2, 2, 2 * ROWS, width)
    for n in reversed(range(count)):
        final = n == 0
        before = middles + staged[::-1] if final else staged[-1:] or middles[:1]
        (outcome,) = run(
            functools.partial(edge_kernel, count, rows, n, True, len(before)),
            f"last_edge_{n}",
            [(v, halves)]
            + many((*around(edge_linear, low_4, high_4, n), edge_grow, edge_gcol, edges[n][0], *lasts[n][:3]))
            + many(before),
            [(h, hbm(count, 2, rows, width)) if final else (v, vmem(*ends))],
            span + ([vmem(*ends), sem((2, PARTS)), sem((count, 3))] if final else []),
            8_000_000,
        )
        staged.append(outcome)
    return outcome


def solution(mesh):
    return jax.shard_map(
        local,
        mesh=mesh,
        in_specs=(
            P("sec", "tile", None),
            P("sec", None, "tile", None),
            P("sec", "tile", None),
            P("sec", "tile", None),
            P("sec", None),
        ),
        out_specs=P("sec", None, "tile", None),
        check_vma=False,
    )
```

time: 182 us -> 73.5 us (0.40)
  the two profiles are of different devices: /device:TPU:4 before, /device:TPU:2 now
where the time goes in v3:
time: 73.5 us; the launch traced here: 72.3 us
  starting transfers between devices  29.8 us (41%)
  Pallas kernels  27.2 us (37%)
  waiting for transfers between devices  14.8 us (20%)
    pallas_call x11, Pallas kernels, run(): pl.pallas_call(kernel, out_shape=[shape for _, shape in outs], in_specs=[...  27.2 us
    ppermute x5, starting transfers between devices, exchange(): lax.ppermute(high, axis, forward)  21 us
    ppermute x5, waiting for transfers between devices, exchange(): lax.ppermute(low, axis, backward)  13.1 us
    ppermute x5, starting transfers between devices, exchange(): lax.ppermute(low, axis, backward)  8.81 us
    ppermute x5, waiting for transfers between devices, exchange(): lax.ppermute(high, axis, forward)  1.69 us
  transfers between devices with their start and end apart: 10, of which 6 were waited for; matrix products, arithmetic and copies ran while one was open for 0% of the time, Pallas kernels for 30%

profile of v3, /device:TPU:2, one launch (start us, length us, event | category | flops | bytes accessed | tf_op | source)
XLA Modules:
  0.0 72.3 jit_solution(10810980529651905112)
XLA Ops:
  0.0 1.9 %pack.1 = (f32[2,33,24,128]{3,2,1,0:T(8,128)S(1)}, f32[2,33,24,128]{3,2,1,0:T(8,128)S(1)}) custom-call(s32[2,1,2]{2,1,0:T(1,128)} %offsets.3, s32[2,1,2]{2,1,0:T(1,128)} %fractions.3, f32[2,64,4096]{2,1,0:T(8,128)} %sections.5, f32[2,2,64,4096]{3,2,1,0:T(8,128)} %refs_3_.3), custom_call_target="tpu_custom_call" | custom-call | flops 1000000 | bytes 1000000 | tf_op jit(solution)/shard_map/pack/pallas_call | solution.py:230
  1.9 2.1 %collective-permute-start = (f32[2,33,24,128]{3,2,1,0:T(8,128)S(1)}, f32[2,33,24,128]{3,2,1,0:T(8,128)S(1)}, u32[]{:S(2)}, u32[]{:S(2)}) collective-permute-start(f32[2,33,24,128]{3,2,1,0:T(8,128)S(1)} %get-tuple-element.44), channel_id=1, source_target_pairs={{0,1},{1,2},{2,3},{3,4},{4,5},{5,6},{6,7},{8,9},{9,10},{10,11},{11... | collective-permute-start | bytes 2433032 | tf_op jit(solution)/shard_map/ppermute | solution.py:659
  4.0 3.6 %collective-permute-start.1 = (f32[2,33,24,128]{3,2,1,0:T(8,128)S(1)}, f32[2,33,24,128]{3,2,1,0:T(8,128)S(1)}, u32[]{:S(2)}, u32[]{:S(2)}) collective-permute-start(f32[2,33,24,128]{3,2,1,0:T(8,128)S(1)} %get-tuple-element.45), channel_id=1, source_target_pairs={{1,0},{2,1},{3,2},{4,3},{5,4},{6,5},{7,6},{9,8},{10,9},{11,10},{12... | collective-permute-start | bytes 2433032 | tf_op jit(solution)/shard_map/ppermute | solution.py:659
  7.7 3.1 %first_inner.1 = (f32[32,64,128]{2,1,0:T(8,128)S(1)}, f32[32,48,128]{2,1,0:T(8,128)S(1)}, f32[32,48,128]{2,1,0:T(8,128)S(1)}, f32[1408,128]{1,0:T(8,128)S(1)}, f...) custom-call(s32[2,1,2]{2,1,0:T(1,128)S(1)} %copy-done.2, ...), custom_call_target="tpu_custom_call" | custom-call | flops 8000000 | bytes 8000000 | tf_op jit(solution)/shard_map/first_inner/pallas_call | solution.py:230
  10.8 1.3 %collective-permute-start.3 = (f32[1408,128]{1,0:T(8,128)S(1)}, f32[1408,128]{1,0:T(8,128)S(1)}, u32[]{:S(2)}, u32[]{:S(2)}) collective-permute-start(f32[1408,128]{1,0:T(8,128)S(1)} %get-tuple-element.59.linear.lower), channel_id=1, source_target_pairs={{8,0},{16,8},{24,16},{9,1},{17,9},{25,17},{10,2},{18,10},{26,18},{... | collective-permute-start | bytes 2162696 | tf_op jit(solution)/shard_map/ppermute | solution.py:659
  12.1 4.6 %collective-permute-start.4 = (f32[1408,128]{1,0:T(8,128)S(1)}, f32[1408,128]{1,0:T(8,128)S(1)}, u32[]{:S(2)}, u32[]{:S(2)}) collective-permute-start(f32[1408,128]{1,0:T(8,128)S(1)} %get-tuple-element.60.upper.linear), channel_id=1, source_target_pairs={{0,8},{8,16},{16,24},{1,9},{9,17},{17,25},{2,10},{10,18},{18,26},{... | collective-permute-start | bytes 2162696 | tf_op jit(solution)/shard_map/ppermute | solution.py:659
  16.7 6.6 %collective-permute-done.1.from_next = f32[2,33,24,128]{3,2,1,0:T(8,128)S(1)} collective-permute-done((f32[2,33,24,128]{3,2,1,0:T(8,128)S(1)}, f32[2,33,24,128]{3,2,1,0:T(8,128)S(1)}, u32[]{:S(2)}, u32[]{:S(2)}) %collective-permute-start.1) | collective-permute-done | bytes 811040 | tf_op jit(solution)/shard_map/ppermute | solution.py:659
  23.3 2.3 %first_edge.1 = (f32[2,2,32,24,128]{4,3,2,1,0:T(8,128)S(1)}, f32[2,2,32,24,128]{4,3,2,1,0:T(8,128)S(1)}, f32[2,2,32,24,128]{4,3,2,1,0:T(8,128)S(1)}, f32[2,2,2,3...) custom-call(s32[2,1,2]{2,1,0:T(1,128)S(1)} %copy-done.2, ...), custom_call_target="tpu_custom_call" | custom-call | flops 5000000 | bytes 5000000 | tf_op jit(solution)/shard_map/first_edge/pallas_call | solution.py:230
  25.6 1.3 %collective-permute-start.2 = (f32[1024,128]{1,0:T(8,128)S(1)}, f32[1024,128]{1,0:T(8,128)S(1)}, u32[]{:S(2)}, u32[]{:S(2)}) collective-permute-start(f32[1024,128]{1,0:T(8,128)S(1)} %get-tuple-element.53.lower.linear), channel_id=1, source_target_pairs={{8,0},{16,8},{24,16},{9,1},{17,9},{25,17},{10,2},{18,10},{26,18},{... | collective-permute-start | bytes 1572872 | tf_op jit(solution)/shard_map/ppermute | solution.py:659
  26.9 4.6 %collective-permute-start.6 = (f32[1024,128]{1,0:T(8,128)S(1)}, f32[1024,128]{1,0:T(8,128)S(1)}, u32[]{:S(2)}, u32[]{:S(2)}) collective-permute-start(f32[1024,128]{1,0:T(8,128)S(1)} %get-tuple-element.54.linear.upper), channel_id=1, source_target_pairs={{0,8},{8,16},{16,24},{1,9},{9,17},{17,25},{2,10},{10,18},{18,26},{... | collective-permute-start | bytes 1572872 | tf_op jit(solution)/shard_map/ppermute | solution.py:659
  31.8 2.8 %inner_0.1 = (f32[2,32,48,128]{3,2,1,0:T(8,128)S(1)}, f32[2,32,48,128]{3,2,1,0:T(8,128)S(1)}, f32[2,32,48,128]{3,2,1,0:T(8,128)S(1)}, f32[2,32,48,128]{3,2,1,0:T(8,128)S(1)}, f32[1216,128]{1,0:T(8,128)S(1)}) custom-call(f32[2,2,8,128]{3,2,1,0:T(8,128)S(1)} %get-tuple-element.52.weights, f32[1408,128]{1,0:T(8,128)S(1)} %collective-permute-done.4.lower, ...), custom_call_target="tpu_custom_call" | custom-call | flops 8000000 | bytes 8000000 | tf_op jit(solution)/shard_map/inner_0/pallas_call | solution.py:230
  34.6 1.3 %collective-permute-start.8 = (f32[1216,128]{1,0:T(8,128)S(1)}, f32[1216,128]{1,0:T(8,128)S(1)}, u32[]{:S(2)}, u32[]{:S(2)}) collective-permute-start(f32[1216,128]{1,0:T(8,128)S(1)} %get-tuple-element.61.refs_4_.lower.linear), channel_id=1, source_target_pairs={{8,0},{16,8},{24,16},{9,1},{17,9},{25,17},{10,2},{18,10},{26,18},{... | collective-permute-start | bytes 1867784 | tf_op jit(solution)/shard_map/ppermute | solution.py:659
  35.9 2.8 %inner_1.1 = (f32[2,32,48,128]{3,2,1,0:T(8,128)S(1)}, f32[2,32,48,128]{3,2,1,0:T(8,128)S(1)}, f32[2,32,48,128]{3,2,1,0:T(8,128)S(1)}, f32[2,32,48,128]{3,2,1,0:T(8,128)S(1)}, f32[1216,128]{1,0:T(8,128)S(1)}) custom-call(f32[2,2,8,128]{3,2,1,0:T(8,128)S(1)} %get-tuple-element.52.weights, f32[1408,128]{1,0:T(8,128)S(1)} %get-tuple-element.59.linear.lower, ...), custom_call_target="tpu_custom_call" | custom-call | flops 8000000 | bytes 8000000 | tf_op jit(solution)/shard_map/inner_1/pallas_call | solution.py:230
  38.7 5.2 %collective-permute-start.7 = (f32[1216,128]{1,0:T(8,128)S(1)}, f32[1216,128]{1,0:T(8,128)S(1)}, u32[]{:S(2)}, u32[]{:S(2)}) collective-permute-start(f32[1216,128]{1,0:T(8,128)S(1)} %get-tuple-element.65.refs_7_.linear.upper), channel_id=1, source_target_pairs={{0,8},{8,16},{16,24},{1,9},{9,17},{17,25},{2,10},{10,18},{18,26},{... | collective-permute-start | bytes 1867784 | tf_op jit(solution)/shard_map/ppermute | solution.py:659
  44.0 2.0 %edge_1.1 = (f32[2,2,32,24,128]{4,3,2,1,0:T(8,128)S(1)}, f32[1024,128]{1,0:T(8,128)S(1)}) custom-call(f32[2,2,8,128]{3,2,1,0:T(8,128)S(1)} %get-tuple-element.52.weights, f32[1024,128]{1,0:T(8,128)S(1)} %get-tuple-element.53.lower.linear, f32[1024,128]{1,0:T(8,128)S(1)} %get-tuple-element.54.linear.upper, f32[1024,128]{1,0:T(8,128)S(1)} %collective-permute-done.2.upper, ...), custom_call_target="tpu_custom_call" | custom-call | flops 8000000 | bytes 8000000 | tf_op jit(solution)/shard_map/edge_1/pallas_call | solution.py:230
  46.1 2.1 %edge_0.1 = (f32[2,2,32,24,128]{4,3,2,1,0:T(8,128)S(1)}, f32[1024,128]{1,0:T(8,128)S(1)}) custom-call(f32[2,2,8,128]{3,2,1,0:T(8,128)S(1)} %get-tuple-element.52.weights, f32[1024,128]{1,0:T(8,128)S(1)} %collective-permute-done.6.lower, f32[1024,128]{1,0:T(8,128)S(1)} %get-tuple-element.53.lower.linear, f32[1024,128]{1,0:T(8,128)S(1)} %get-tuple-element.54.linear.upper, ...), custom_call_target="tpu_custom_call" | custom-call | flops 8000000 | bytes 8000000 | tf_op jit(solution)/shard_map/edge_0/pallas_call | solution.py:230
  48.1 1.3 %collective-permute-start.9 = (f32[1024,128]{1,0:T(8,128)S(1)}, f32[1024,128]{1,0:T(8,128)S(1)}, u32[]{:S(2)}, u32[]{:S(2)}) collective-permute-start(f32[1024,128]{1,0:T(8,128)S(1)} %get-tuple-element.70.lower.linear), channel_id=1, source_target_pairs={{8,0},{16,8},{24,16},{9,1},{17,9},{25,17},{10,2},{18,10},{26,18},{... | collective-permute-start | bytes 1572872 | tf_op jit(solution)/shard_map/ppermute | solution.py:659
  49.4 4.6 %collective-permute-start.5 = (f32[1024,128]{1,0:T(8,128)S(1)}, f32[1024,128]{1,0:T(8,128)S(1)}, u32[]{:S(2)}, u32[]{:S(2)}) collective-permute-start(f32[1024,128]{1,0:T(8,128)S(1)} %get-tuple-element.66.refs_7_.linear.upper), channel_id=1, source_target_pairs={{0,8},{8,16},{16,24},{1,9},{9,17},{17,25},{2,10},{10,18},{18,26},{... | collective-permute-start | bytes 1572872 | tf_op jit(solution)/shard_map/ppermute | solution.py:659
  54.9 2.3 %last_inner_1.1 = (f32[2,32,48,128]{3,2,1,0:T(8,128)S(1)}, f32[2,32,48,128]{3,2,1,0:T(8,128)S(1)}, f32[2,32,48,128]{3,2,1,0:T(8,128)S(1)}, f32[2,32,4096]{2,1,0:T(8,128)S(1)}) custom-call(f32[2,2,8,128]{3,2,1,0:T(8,128)S(1)} %get-tuple-element.52.weights, f32[1216,128]{1,0:T(8,128)S(1)} %get-tuple-element.61.refs_4_.lower.linear, ...), custom_call_target="tpu_custom_call" | custom-call | flops 40000000 | bytes 40000000 | tf_op jit(solution)/shard_map/last_inner_1/pallas_call | solution.py:230
  57.2 0.9 %collective-permute-done.7.lower = f32[1216,128]{1,0:T(8,128)S(1)} collective-permute-done((f32[1216,128]{1,0:T(8,128)S(1)}, f32[1216,128]{1,0:T(8,128)S(1)}, u32[]{:S(2)}, u32[]{:S(2)}) %collective-permute-start.7) | collective-permute-done | bytes 622624 | tf_op jit(solution)/shard_map/ppermute | solution.py:659
  58.1 2.4 %last_inner_0.1 = (f32[2,32,48,128]{3,2,1,0:T(8,128)S(1)}, f32[2,32,48,128]{3,2,1,0:T(8,128)S(1)}, f32[2,32,48,128]{3,2,1,0:T(8,128)S(1)}, f32[2,32,4096]{2,1,0:T(8,128)S(1)}) custom-call(f32[2,2,8,128]{3,2,1,0:T(8,128)S(1)} %get-tuple-element.52.weights, f32[1216,128]{1,0:T(8,128)S(1)} %collective-permute-done.7.lower, ...), custom_call_target="tpu_custom_call" | custom-call | flops 40000000 | bytes 40000000 | tf_op jit(solution)/shard_map/last_inner_0/pallas_call | solution.py:230
  60.5 5.6 %collective-permute-done.9.upper = f32[1024,128]{1,0:T(8,128)S(1)} collective-permute-done((f32[1024,128]{1,0:T(8,128)S(1)}, f32[1024,128]{1,0:T(8,128)S(1)}, u32[]{:S(2)}, u32[]{:S(2)}) %collective-permute-start.9) | collective-permute-done | bytes 524320 | tf_op jit(solution)/shard_map/ppermute | solution.py:659
  66.1 2.0 %last_edge_1.1.refs_8_ = f32[2,2,16,4096]{3,2,1,0:T(8,128)S(1)} custom-call(f32[2,2,8,128]{3,2,1,0:T(8,128)S(1)} %get-tuple-element.52.weights, f32[1024,128]{1,0:T(8,128)S(1)} %get-tuple-element.70.lower.linear, f32[1024,128]{1,0:T(8,128)S(1)} %get-tuple-element.66.refs_7_.linear.upper, f32[1024,128]{1,0:T(8,128)S(1)} %collective-permute-done.9.upper, ...), custom_call_target="tpu_custom_call" | custom-call | flops 8000000 | bytes 8000000 | tf_op jit(solution)/shard_map/last_edge_1/pallas_call | solution.py:230
  68.7 3.4 %last_edge_0.1 = f32[2,2,64,4096]{3,2,1,0:T(8,128)} custom-call(f32[2,2,8,128]{3,2,1,0:T(8,128)S(1)} %get-tuple-element.52.weights, f32[1024,128]{1,0:T(8,128)S(1)} %collective-permute-done.5.lower, f32[1024,128]{1,0:T(8,128)S(1)} %get-tuple-element.70.lower.linear, f32[1024,128]{1,0:T(8,128)S(1)} %get-tuple-element.66.refs_7_.linear.upper, ...), custom_call_target="tpu_custom_call" | custom-call | flops 8000000 | bytes 8000000 | tf_op jit(solution)/shard_map/last_edge_0/pallas_call | solution.py:230
  (17 shorter events, 1.7 us)
Async XLA Ops:
  0.0 7.6 %copy-start.2 = (s32[2,1,2]{2,1,0:T(1,128)S(1)}, s32[2,1,2]{2,1,0:T(1,128)}, u32[]{:S(2)}) copy-start(s32[2,1,2]{2,1,0:T(1,128)} %offsets.3) | copy-start | bytes 52
  0.0 7.6 %copy-start.3 = (s32[2,1,2]{2,1,0:T(1,128)S(1)}, s32[2,1,2]{2,1,0:T(1,128)}, u32[]{:S(2)}) copy-start(s32[2,1,2]{2,1,0:T(1,128)} %fractions.3) | copy-start | bytes 52
  0.0 7.6 %copy-start.1 = (f32[2,64,4096]{2,1,0:T(8,128)S(1)}, f32[2,64,4096]{2,1,0:T(8,128)}, u32[]{:S(2)}) copy-start(f32[2,64,4096]{2,1,0:T(8,128)} %sections.5) | copy-start | bytes 6291460
  0.0 7.6 %copy-start = (f32[2,2,64,4096]{3,2,1,0:T(8,128)S(1)}, f32[2,2,64,4096]{3,2,1,0:T(8,128)}, u32[]{:S(2)}) copy-start(f32[2,2,64,4096]{3,2,1,0:T(8,128)} %refs_3_.3) | copy-start | bytes 12582916
  1.9 14.8 %collective-permute-start = (f32[2,33,24,128]{3,2,1,0:T(8,128)S(1)}, f32[2,33,24,128]{3,2,1,0:T(8,128)S(1)}, u32[]{:S(2)}, u32[]{:S(2)}) collective-permute-start(f32[2,33,24,128]{3,2,1,0:T(8,128)S(1)} %get-tuple-element.44), channel_id=1, source_target_pairs={{0,1},{1,2},{2,3},{3,4},{4,5},{5,6},{6,7},{8,9},{9,10},{10,11},{11... | collective-permute-start | bytes 2433032 | tf_op jit(solution)/shard_map/ppermute | solution.py:659
  4.0 19.3 %copy-start.4 = (s32[2,2]{1,0:T(2,128)S(1)}, s32[2,2]{1,0:T(2,128)}, u32[]{:S(2)}) copy-start(s32[2,2]{1,0:T(2,128)} %weights.1) | copy-start | bytes 52
  4.0 19.3 %collective-permute-start.1 = (f32[2,33,24,128]{3,2,1,0:T(8,128)S(1)}, f32[2,33,24,128]{3,2,1,0:T(8,128)S(1)}, u32[]{:S(2)}, u32[]{:S(2)}) collective-permute-start(f32[2,33,24,128]{3,2,1,0:T(8,128)S(1)} %get-tuple-element.45), channel_id=1, source_target_pairs={{1,0},{2,1},{3,2},{4,3},{5,4},{6,5},{7,6},{9,8},{10,9},{11,10},{12... | collective-permute-start | bytes 2433032 | tf_op jit(solution)/shard_map/ppermute | solution.py:659
  10.8 20.7 %collective-permute-start.3 = (f32[1408,128]{1,0:T(8,128)S(1)}, f32[1408,128]{1,0:T(8,128)S(1)}, u32[]{:S(2)}, u32[]{:S(2)}) collective-permute-start(f32[1408,128]{1,0:T(8,128)S(1)} %get-tuple-element.59.linear.lower), channel_id=1, source_target_pairs={{8,0},{16,8},{24,16},{9,1},{17,9},{25,17},{10,2},{18,10},{26,18},{... | collective-permute-start | bytes 2162696 | tf_op jit(solution)/shard_map/ppermute | solution.py:659
  12.1 19.7 %collective-permute-start.4 = (f32[1408,128]{1,0:T(8,128)S(1)}, f32[1408,128]{1,0:T(8,128)S(1)}, u32[]{:S(2)}, u32[]{:S(2)}) collective-permute-start(f32[1408,128]{1,0:T(8,128)S(1)} %get-tuple-element.60.upper.linear), channel_id=1, source_target_pairs={{0,8},{8,16},{16,24},{1,9},{9,17},{17,25},{2,10},{10,18},{18,26},{... | collective-permute-start | bytes 2162696 | tf_op jit(solution)/shard_map/ppermute | solution.py:659
  25.6 18.4 %collective-permute-start.2 = (f32[1024,128]{1,0:T(8,128)S(1)}, f32[1024,128]{1,0:T(8,128)S(1)}, u32[]{:S(2)}, u32[]{:S(2)}) collective-permute-start(f32[1024,128]{1,0:T(8,128)S(1)} %get-tuple-element.53.lower.linear), channel_id=1, source_target_pairs={{8,0},{16,8},{24,16},{9,1},{17,9},{25,17},{10,2},{18,10},{26,18},{... | collective-permute-start | bytes 1572872 | tf_op jit(solution)/shard_map/ppermute | solution.py:659
  26.9 19.1 %collective-permute-start.6 = (f32[1024,128]{1,0:T(8,128)S(1)}, f32[1024,128]{1,0:T(8,128)S(1)}, u32[]{:S(2)}, u32[]{:S(2)}) collective-permute-start(f32[1024,128]{1,0:T(8,128)S(1)} %get-tuple-element.54.linear.upper), channel_id=1, source_target_pairs={{0,8},{8,16},{16,24},{1,9},{9,17},{17,25},{2,10},{10,18},{18,26},{... | collective-permute-start | bytes 1572872 | tf_op jit(solution)/shard_map/ppermute | solution.py:659
  34.6 20.3 %collective-permute-start.8 = (f32[1216,128]{1,0:T(8,128)S(1)}, f32[1216,128]{1,0:T(8,128)S(1)}, u32[]{:S(2)}, u32[]{:S(2)}) collective-permute-start(f32[1216,128]{1,0:T(8,128)S(1)} %get-tuple-element.61.refs_4_.lower.linear), channel_id=1, source_target_pairs={{8,0},{16,8},{24,16},{9,1},{17,9},{25,17},{10,2},{18,10},{26,18},{... | collective-permute-start | bytes 1867784 | tf_op jit(solution)/shard_map/ppermute | solution.py:659
  38.7 19.4 %collective-permute-start.7 = (f32[1216,128]{1,0:T(8,128)S(1)}, f32[1216,128]{1,0:T(8,128)S(1)}, u32[]{:S(2)}, u32[]{:S(2)}) collective-permute-start(f32[1216,128]{1,0:T(8,128)S(1)} %get-tuple-element.65.refs_7_.linear.upper), channel_id=1, source_target_pairs={{0,8},{8,16},{16,24},{1,9},{9,17},{17,25},{2,10},{10,18},{18,26},{... | collective-permute-start | bytes 1867784 | tf_op jit(solution)/shard_map/ppermute | solution.py:659
  48.1 18.0 %collective-permute-start.9 = (f32[1024,128]{1,0:T(8,128)S(1)}, f32[1024,128]{1,0:T(8,128)S(1)}, u32[]{:S(2)}, u32[]{:S(2)}) collective-permute-start(f32[1024,128]{1,0:T(8,128)S(1)} %get-tuple-element.70.lower.linear), channel_id=1, source_target_pairs={{8,0},{16,8},{24,16},{9,1},{17,9},{25,17},{10,2},{18,10},{26,18},{... | collective-permute-start | bytes 1572872 | tf_op jit(solution)/shard_map/ppermute | solution.py:659
  49.4 19.2 %collective-permute-start.5 = (f32[1024,128]{1,0:T(8,128)S(1)}, f32[1024,128]{1,0:T(8,128)S(1)}, u32[]{:S(2)}, u32[]{:S(2)}) collective-permute-start(f32[1024,128]{1,0:T(8,128)S(1)} %get-tuple-element.66.refs_7_.linear.upper), channel_id=1, source_target_pairs={{0,8},{8,16},{16,24},{1,9},{9,17},{17,25},{2,10},{10,18},{18,26},{... | collective-permute-start | bytes 1572872 | tf_op jit(solution)/shard_map/ppermute | solution.py:659

commit v4 on v3

--- a/solution.py
+++ b/solution.py
@@ -446,7 +446,11 @@
 def inner_kernel(count, rows, s, last, order, weights, lower, linear, upper, *refs):
     if last:
         grow, gcol, field, *refs = refs
-        moved, once, twice, stage = refs[order:]
+        before, refs = refs[:order], refs[order:]
+        if s == 0:
+            moved, once, twice, result, stage, sems = refs
+        else:
+            moved, once, twice, stage = refs
         halo = HALF
     else:
         grow, gcol, warped, field, *refs = refs
@@ -455,6 +459,17 @@
     first = 2 * ROWS - halo
     columns = grow.shape[0]
     end = rows - first - 1
+    copies = []
+
+    def send(source, n):
+        target = result.at[n, :, pl.ds(2 * ROWS, rows - 4 * ROWS)]
+        copy = pltpu.make_async_copy(source, target, sems.at[n])
+        copy.start()
+        copies.append(copy)
+
+    if last and s == 0:
+        for k, source in enumerate(before):
+            send(source, count - 1 - k)
     weight_lower, weight_upper = weights[s, 0], weights[s, 1]
 
     def move(j):
@@ -506,6 +521,10 @@
             )
 
     sweep(nothing, load, names, columns, finish)
+    if last and s == 0:
+        send(stage, 0)
+    for copy in copies:
+        copy.wait()
 
 
 PARTS = 4
@@ -609,16 +628,12 @@
 
     copies = []
     if final:
-        middle = pl.ds(2 * ROWS, rows - 4 * ROWS)
-        for n in range(count):
-            copies.append(pltpu.make_async_copy(before[n], result.at[n, :, middle], stage_sems.at[n, 0]))
-            if n != s:
-                for side in range(2):
-                    copies.append(
-                        pltpu.make_async_copy(
-                            before[count + n - 1].at[side], result.at[n, :, ends(side)], stage_sems.at[n, 1 + side]
-                        )
-                    )
+        for k, source in enumerate(before[:-1]):
+            n = count - 1 - k
+            for side in range(2):
+                copies.append(
+                    pltpu.make_async_copy(source.at[side], result.at[n, :, ends(side)], stage_sems.at[n, side])
+                )
         for copy in copies:
             copy.start()
 
@@ -755,35 +770,37 @@
     low_4, high_4 = exchange(edge_linear[0], edge_linear[-1], "sec")
 
     lasts = [None] * count
-    order = []
+    stages = []
     for n in reversed(range(count)):
         lasts[n] = run(
-            functools.partial(inner_kernel, count, rows, n, True, len(order)),
+            functools.partial(inner_kernel, count, rows, n, True, len(stages)),
             f"last_inner_{n}",
             [(v, halves)]
-            + many((*around(inner_linear, low_3, high_3, n), grows[n], gcols[n], inners[n][3], *order)),
-            [band(2, height=held)] * 3 + [(v, vmem(2, rows - 4 * ROWS, width))],
-            [],
+            + many((*around(inner_linear, low_3, high_3, n), grows[n], gcols[n], inners[n][3], *stages)),
+            [band(2, height=held)] * 3
+            + [(v, vmem(2, rows - 4 * ROWS, width)) if n else (h, hbm(count, 2, rows, width))],
+            [] if n else [vmem(2, rows - 4 * ROWS, width), sem((count,))],
             40_000_000,
         )
-        order = [lasts[n][3]]
-    middles = [outs[3] for outs in lasts]
-    staged = []
+        stages.append(lasts[n][3])
+    result = stages[-1]
     ends = (2, 2, 2 * ROWS, width)
+    stages = []
     for n in reversed(range(count)):
-        final = n == 0
-        before = middles + staged[::-1] if final else staged[-1:] or middles[:1]
+        before = many((stages[-1:] or lasts[0][:1]) if n else stages)
         (outcome,) = run(
-            functools.partial(edge_kernel, count, rows, n, True, len(before)),
+            functools.partial(edge_kernel, count, rows, n, True, len(before) + (n == 0)),
             f"last_edge_{n}",
             [(v, halves)]
             + many((*around(edge_linear, low_4, high_4, n), edge_grow, edge_gcol, edges[n][0], *lasts[n][:3]))
-            + many(before),
-            [(h, hbm(count, 2, rows, width)) if final else (v, vmem(*ends))],
-            span + ([vmem(*ends), sem((2, PARTS)), sem((count, 3))] if final else []),
+            + before
+            + ([] if n else [(h, result)]),
+            [(v, vmem(*ends)) if n else (h, hbm(count, 2, rows, width))],
+            span + ([] if n else [vmem(*ends), sem((2, PARTS)), sem((count, 2))]),
             8_000_000,
+            aliases=None if n else {10 + len(before): 0},
         )
-        staged.append(outcome)
+        stages.append(outcome)
     return outcome
 
 

time: 73.5 us -> 73.1 us (level)
  waiting for transfers between devices: 14.8 us -> 13.9 us
    ppermute x5, waiting for transfers between devices: 13.1 us -> 12.1 us  [exchange(): lax.ppermute(low, axis, backward)]
  transfers between devices with their start and end apart: 10 -> 10, of which waited for: 6 -> 6; matrix products, arithmetic and copies ran while one was open for 0% -> 0% of each run, Pallas kernels for 30% -> 32%
where the time goes in v4:
time: 73.1 us; the launch traced here: 71.8 us
  starting transfers between devices  29.8 us (41%)
  Pallas kernels  27.7 us (38%)
  waiting for transfers between devices  13.9 us (19%)
    pallas_call x11, Pallas kernels, run(): pl.pallas_call(kernel, out_shape=[shape for _, shape in outs], in_specs=[...  27.7 us
    ppermute x5, starting transfers between devices, exchange(): lax.ppermute(high, axis, forward)  21 us
    ppermute x5, waiting for transfers between devices, exchange(): lax.ppermute(low, axis, backward)  12.1 us
    ppermute x5, starting transfers between devices, exchange(): lax.ppermute(low, axis, backward)  8.81 us
    ppermute x5, waiting for transfers between devices, exchange(): lax.ppermute(high, axis, forward)  1.74 us
  transfers between devices with their start and end apart: 10, of which 6 were waited for; matrix products, arithmetic and copies ran while one was open for 0% of the time, Pallas kernels for 32%

profile of v4, /device:TPU:2, one launch (start us, length us, event | category | flops | bytes accessed | tf_op | source)
XLA Modules:
  0.0 71.8 jit_solution(9647103813878958351)
XLA Ops:
  0.0 1.9 %pack.1 = (f32[2,33,24,128]{3,2,1,0:T(8,128)S(1)}, f32[2,33,24,128]{3,2,1,0:T(8,128)S(1)}) custom-call(s32[2,1,2]{2,1,0:T(1,128)} %offsets.3, s32[2,1,2]{2,1,0:T(1,128)} %fractions.3, f32[2,64,4096]{2,1,0:T(8,128)} %sections.5, f32[2,2,64,4096]{3,2,1,0:T(8,128)} %refs_3_.3), custom_call_target="tpu_custom_call" | custom-call | flops 1000000 | bytes 1000000 | tf_op jit(solution)/shard_map/pack/pallas_call | solution.py:230
  1.9 2.1 %collective-permute-start = (f32[2,33,24,128]{3,2,1,0:T(8,128)S(1)}, f32[2,33,24,128]{3,2,1,0:T(8,128)S(1)}, u32[]{:S(2)}, u32[]{:S(2)}) collective-permute-start(f32[2,33,24,128]{3,2,1,0:T(8,128)S(1)} %get-tuple-element.44), channel_id=1, source_target_pairs={{0,1},{1,2},{2,3},{3,4},{4,5},{5,6},{6,7},{8,9},{9,10},{10,11},{11... | collective-permute-start | bytes 2433032 | tf_op jit(solution)/shard_map/ppermute | solution.py:674
  4.0 3.6 %collective-permute-start.1 = (f32[2,33,24,128]{3,2,1,0:T(8,128)S(1)}, f32[2,33,24,128]{3,2,1,0:T(8,128)S(1)}, u32[]{:S(2)}, u32[]{:S(2)}) collective-permute-start(f32[2,33,24,128]{3,2,1,0:T(8,128)S(1)} %get-tuple-element.45), channel_id=1, source_target_pairs={{1,0},{2,1},{3,2},{4,3},{5,4},{6,5},{7,6},{9,8},{10,9},{11,10},{12... | collective-permute-start | bytes 2433032 | tf_op jit(solution)/shard_map/ppermute | solution.py:674
  7.7 3.1 %first_inner.1 = (f32[32,64,128]{2,1,0:T(8,128)S(1)}, f32[32,48,128]{2,1,0:T(8,128)S(1)}, f32[32,48,128]{2,1,0:T(8,128)S(1)}, f32[1408,128]{1,0:T(8,128)S(1)}, f...) custom-call(s32[2,1,2]{2,1,0:T(1,128)S(1)} %copy-done.2, ...), custom_call_target="tpu_custom_call" | custom-call | flops 8000000 | bytes 8000000 | tf_op jit(solution)/shard_map/first_inner/pallas_call | solution.py:230
  10.8 1.3 %collective-permute-start.3 = (f32[1408,128]{1,0:T(8,128)S(1)}, f32[1408,128]{1,0:T(8,128)S(1)}, u32[]{:S(2)}, u32[]{:S(2)}) collective-permute-start(f32[1408,128]{1,0:T(8,128)S(1)} %get-tuple-element.59.linear.lower), channel_id=1, source_target_pairs={{8,0},{16,8},{24,16},{9,1},{17,9},{25,17},{10,2},{18,10},{26,18},{... | collective-permute-start | bytes 2162696 | tf_op jit(solution)/shard_map/ppermute | solution.py:674
  12.1 4.6 %collective-permute-start.4 = (f32[1408,128]{1,0:T(8,128)S(1)}, f32[1408,128]{1,0:T(8,128)S(1)}, u32[]{:S(2)}, u32[]{:S(2)}) collective-permute-start(f32[1408,128]{1,0:T(8,128)S(1)} %get-tuple-element.60.upper.linear), channel_id=1, source_target_pairs={{0,8},{8,16},{16,24},{1,9},{9,17},{17,25},{2,10},{10,18},{18,26},{... | collective-permute-start | bytes 2162696 | tf_op jit(solution)/shard_map/ppermute | solution.py:674
  16.7 6.6 %collective-permute-done.1.from_next = f32[2,33,24,128]{3,2,1,0:T(8,128)S(1)} collective-permute-done((f32[2,33,24,128]{3,2,1,0:T(8,128)S(1)}, f32[2,33,24,128]{3,2,1,0:T(8,128)S(1)}, u32[]{:S(2)}, u32[]{:S(2)}) %collective-permute-start.1) | collective-permute-done | bytes 811040 | tf_op jit(solution)/shard_map/ppermute | solution.py:674
  23.3 2.3 %first_edge.1 = (f32[2,2,32,24,128]{4,3,2,1,0:T(8,128)S(1)}, f32[2,2,32,24,128]{4,3,2,1,0:T(8,128)S(1)}, f32[2,2,32,24,128]{4,3,2,1,0:T(8,128)S(1)}, f32[2,2,2,3...) custom-call(s32[2,1,2]{2,1,0:T(1,128)S(1)} %copy-done.2, ...), custom_call_target="tpu_custom_call" | custom-call | flops 5000000 | bytes 5000000 | tf_op jit(solution)/shard_map/first_edge/pallas_call | solution.py:230
  25.6 1.3 %collective-permute-start.2 = (f32[1024,128]{1,0:T(8,128)S(1)}, f32[1024,128]{1,0:T(8,128)S(1)}, u32[]{:S(2)}, u32[]{:S(2)}) collective-permute-start(f32[1024,128]{1,0:T(8,128)S(1)} %get-tuple-element.53.lower.linear), channel_id=1, source_target_pairs={{8,0},{16,8},{24,16},{9,1},{17,9},{25,17},{10,2},{18,10},{26,18},{... | collective-permute-start | bytes 1572872 | tf_op jit(solution)/shard_map/ppermute | solution.py:674
  26.9 4.6 %collective-permute-start.6 = (f32[1024,128]{1,0:T(8,128)S(1)}, f32[1024,128]{1,0:T(8,128)S(1)}, u32[]{:S(2)}, u32[]{:S(2)}) collective-permute-start(f32[1024,128]{1,0:T(8,128)S(1)} %get-tuple-element.54.linear.upper), channel_id=1, source_target_pairs={{0,8},{8,16},{16,24},{1,9},{9,17},{17,25},{2,10},{10,18},{18,26},{... | collective-permute-start | bytes 1572872 | tf_op jit(solution)/shard_map/ppermute | solution.py:674
  31.8 2.9 %inner_0.1 = (f32[2,32,48,128]{3,2,1,0:T(8,128)S(1)}, f32[2,32,48,128]{3,2,1,0:T(8,128)S(1)}, f32[2,32,48,128]{3,2,1,0:T(8,128)S(1)}, f32[2,32,48,128]{3,2,1,0:T(8,128)S(1)}, f32[1216,128]{1,0:T(8,128)S(1)}) custom-call(f32[2,2,8,128]{3,2,1,0:T(8,128)S(1)} %get-tuple-element.52.weights, f32[1408,128]{1,0:T(8,128)S(1)} %collective-permute-done.4.lower, ...), custom_call_target="tpu_custom_call" | custom-call | flops 8000000 | bytes 8000000 | tf_op jit(solution)/shard_map/inner_0/pallas_call | solution.py:230
  34.6 1.3 %collective-permute-start.8 = (f32[1216,128]{1,0:T(8,128)S(1)}, f32[1216,128]{1,0:T(8,128)S(1)}, u32[]{:S(2)}, u32[]{:S(2)}) collective-permute-start(f32[1216,128]{1,0:T(8,128)S(1)} %get-tuple-element.61.refs_4_.lower.linear), channel_id=1, source_target_pairs={{8,0},{16,8},{24,16},{9,1},{17,9},{25,17},{10,2},{18,10},{26,18},{... | collective-permute-start | bytes 1867784 | tf_op jit(solution)/shard_map/ppermute | solution.py:674
  35.9 2.8 %inner_1.1 = (f32[2,32,48,128]{3,2,1,0:T(8,128)S(1)}, f32[2,32,48,128]{3,2,1,0:T(8,128)S(1)}, f32[2,32,48,128]{3,2,1,0:T(8,128)S(1)}, f32[2,32,48,128]{3,2,1,0:T(8,128)S(1)}, f32[1216,128]{1,0:T(8,128)S(1)}) custom-call(f32[2,2,8,128]{3,2,1,0:T(8,128)S(1)} %get-tuple-element.52.weights, f32[1408,128]{1,0:T(8,128)S(1)} %get-tuple-element.59.linear.lower, ...), custom_call_target="tpu_custom_call" | custom-call | flops 8000000 | bytes 8000000 | tf_op jit(solution)/shard_map/inner_1/pallas_call | solution.py:230
  38.8 5.2 %collective-permute-start.7 = (f32[1216,128]{1,0:T(8,128)S(1)}, f32[1216,128]{1,0:T(8,128)S(1)}, u32[]{:S(2)}, u32[]{:S(2)}) collective-permute-start(f32[1216,128]{1,0:T(8,128)S(1)} %get-tuple-element.65.refs_7_.linear.upper), channel_id=1, source_target_pairs={{0,8},{8,16},{16,24},{1,9},{9,17},{17,25},{2,10},{10,18},{18,26},{... | collective-permute-start | bytes 1867784 | tf_op jit(solution)/shard_map/ppermute | solution.py:674
  44.0 2.0 %edge_1.1 = (f32[2,2,32,24,128]{4,3,2,1,0:T(8,128)S(1)}, f32[1024,128]{1,0:T(8,128)S(1)}) custom-call(f32[2,2,8,128]{3,2,1,0:T(8,128)S(1)} %get-tuple-element.52.weights, f32[1024,128]{1,0:T(8,128)S(1)} %get-tuple-element.53.lower.linear, f32[1024,128]{1,0:T(8,128)S(1)} %get-tuple-element.54.linear.upper, f32[1024,128]{1,0:T(8,128)S(1)} %collective-permute-done.2.upper, ...), custom_call_target="tpu_custom_call" | custom-call | flops 8000000 | bytes 8000000 | tf_op jit(solution)/shard_map/edge_1/pallas_call | solution.py:230
  46.1 2.1 %edge_0.1 = (f32[2,2,32,24,128]{4,3,2,1,0:T(8,128)S(1)}, f32[1024,128]{1,0:T(8,128)S(1)}) custom-call(f32[2,2,8,128]{3,2,1,0:T(8,128)S(1)} %get-tuple-element.52.weights, f32[1024,128]{1,0:T(8,128)S(1)} %collective-permute-done.6.lower, f32[1024,128]{1,0:T(8,128)S(1)} %get-tuple-element.53.lower.linear, f32[1024,128]{1,0:T(8,128)S(1)} %get-tuple-element.54.linear.upper, ...), custom_call_target="tpu_custom_call" | custom-call | flops 8000000 | bytes 8000000 | tf_op jit(solution)/shard_map/edge_0/pallas_call | solution.py:230
  48.2 1.3 %collective-permute-start.9 = (f32[1024,128]{1,0:T(8,128)S(1)}, f32[1024,128]{1,0:T(8,128)S(1)}, u32[]{:S(2)}, u32[]{:S(2)}) collective-permute-start(f32[1024,128]{1,0:T(8,128)S(1)} %get-tuple-element.70.lower.linear), channel_id=1, source_target_pairs={{8,0},{16,8},{24,16},{9,1},{17,9},{25,17},{10,2},{18,10},{26,18},{... | collective-permute-start | bytes 1572872 | tf_op jit(solution)/shard_map/ppermute | solution.py:674
  49.5 4.6 %collective-permute-start.5 = (f32[1024,128]{1,0:T(8,128)S(1)}, f32[1024,128]{1,0:T(8,128)S(1)}, u32[]{:S(2)}, u32[]{:S(2)}) collective-permute-start(f32[1024,128]{1,0:T(8,128)S(1)} %get-tuple-element.66.refs_7_.linear.upper), channel_id=1, source_target_pairs={{0,8},{8,16},{16,24},{1,9},{9,17},{17,25},{2,10},{10,18},{18,26},{... | collective-permute-start | bytes 1572872 | tf_op jit(solution)/shard_map/ppermute | solution.py:674
  54.9 2.3 %last_inner_1.1 = (f32[2,32,48,128]{3,2,1,0:T(8,128)S(1)}, f32[2,32,48,128]{3,2,1,0:T(8,128)S(1)}, f32[2,32,48,128]{3,2,1,0:T(8,128)S(1)}, f32[2,32,4096]{2,1,0:T(8,128)S(1)}) custom-call(f32[2,2,8,128]{3,2,1,0:T(8,128)S(1)} %get-tuple-element.52.weights, f32[1216,128]{1,0:T(8,128)S(1)} %get-tuple-element.61.refs_4_.lower.linear, ...), custom_call_target="tpu_custom_call" | custom-call | flops 40000000 | bytes 40000000 | tf_op jit(solution)/shard_map/last_inner_1/pallas_call | solution.py:230
  57.2 0.9 %collective-permute-done.7.lower = f32[1216,128]{1,0:T(8,128)S(1)} collective-permute-done((f32[1216,128]{1,0:T(8,128)S(1)}, f32[1216,128]{1,0:T(8,128)S(1)}, u32[]{:S(2)}, u32[]{:S(2)}) %collective-permute-start.7) | collective-permute-done | bytes 622624 | tf_op jit(solution)/shard_map/ppermute | solution.py:674
  58.1 3.3 %last_inner_0.1 = (f32[2,32,48,128]{3,2,1,0:T(8,128)S(1)}, f32[2,32,48,128]{3,2,1,0:T(8,128)S(1)}, f32[2,32,48,128]{3,2,1,0:T(8,128)S(1)}, f32[2,2,64,4096]{3,2,1,0:T(8,128)}) custom-call(f32[2,2,8,128]{3,2,1,0:T(8,128)S(1)} %get-tuple-element.52.weights, f32[1216,128]{1,0:T(8,128)S(1)} %collective-permute-done.7.lower, ...), custom_call_target="tpu_custom_call" | custom-call | flops 40000000 | bytes 40000000 | tf_op jit(solution)/shard_map/last_inner_0/pallas_call | solution.py:230
  61.5 4.6 %collective-permute-done.9.upper = f32[1024,128]{1,0:T(8,128)S(1)} collective-permute-done((f32[1024,128]{1,0:T(8,128)S(1)}, f32[1024,128]{1,0:T(8,128)S(1)}, u32[]{:S(2)}, u32[]{:S(2)}) %collective-permute-start.9) | collective-permute-done | bytes 524320 | tf_op jit(solution)/shard_map/ppermute | solution.py:674
  66.1 2.0 %last_edge_1.1.refs_6_ = f32[2,2,16,4096]{3,2,1,0:T(8,128)S(1)} custom-call(f32[2,2,8,128]{3,2,1,0:T(8,128)S(1)} %get-tuple-element.52.weights, f32[1024,128]{1,0:T(8,128)S(1)} %get-tuple-element.70.lower.linear, f32[1024,128]{1,0:T(8,128)S(1)} %get-tuple-element.66.refs_7_.linear.upper, f32[1024,128]{1,0:T(8,128)S(1)} %collective-permute-done.9.upper, ...), custom_call_target="tpu_custom_call" | custom-call | flops 8000000 | bytes 8000000 | tf_op jit(solution)/shard_map/last_edge_1/pallas_call | solution.py:230
  68.7 3.0 %last_edge_0.1 = f32[2,2,64,4096]{3,2,1,0:T(8,128)} custom-call(f32[2,2,8,128]{3,2,1,0:T(8,128)S(1)} %get-tuple-element.52.weights, f32[1024,128]{1,0:T(8,128)S(1)} %collective-permute-done.5.lower, f32[1024,128]{1,0:T(8,128)S(1)} %get-tuple-element.70.lower.linear, ...), custom_call_target="tpu_custom_call", output_to_operand_aliasing={{}: (11, {})} | custom-call | flops 8000000 | bytes 8000000 | tf_op jit(solution)/shard_map/last_edge_0/pallas_call | solution.py:230
  (17 shorter events, 1.7 us)
Async XLA Ops:
  0.0 7.6 %copy-start.2 = (s32[2,1,2]{2,1,0:T(1,128)S(1)}, s32[2,1,2]{2,1,0:T(1,128)}, u32[]{:S(2)}) copy-start(s32[2,1,2]{2,1,0:T(1,128)} %offsets.3) | copy-start | bytes 52
  0.0 7.6 %copy-start.3 = (s32[2,1,2]{2,1,0:T(1,128)S(1)}, s32[2,1,2]{2,1,0:T(1,128)}, u32[]{:S(2)}) copy-start(s32[2,1,2]{2,1,0:T(1,128)} %fractions.3) | copy-start | bytes 52
  0.0 7.6 %copy-start.1 = (f32[2,64,4096]{2,1,0:T(8,128)S(1)}, f32[2,64,4096]{2,1,0:T(8,128)}, u32[]{:S(2)}) copy-start(f32[2,64,4096]{2,1,0:T(8,128)} %sections.5) | copy-start | bytes 6291460
  0.0 7.6 %copy-start = (f32[2,2,64,4096]{3,2,1,0:T(8,128)S(1)}, f32[2,2,64,4096]{3,2,1,0:T(8,128)}, u32[]{:S(2)}) copy-start(f32[2,2,64,4096]{3,2,1,0:T(8,128)} %refs_3_.3) | copy-start | bytes 12582916
  1.9 14.8 %collective-permute-start = (f32[2,33,24,128]{3,2,1,0:T(8,128)S(1)}, f32[2,33,24,128]{3,2,1,0:T(8,128)S(1)}, u32[]{:S(2)}, u32[]{:S(2)}) collective-permute-start(f32[2,33,24,128]{3,2,1,0:T(8,128)S(1)} %get-tuple-element.44), channel_id=1, source_target_pairs={{0,1},{1,2},{2,3},{3,4},{4,5},{5,6},{6,7},{8,9},{9,10},{10,11},{11... | collective-permute-start | bytes 2433032 | tf_op jit(solution)/shard_map/ppermute | solution.py:674
  4.0 19.3 %copy-start.4 = (s32[2,2]{1,0:T(2,128)S(1)}, s32[2,2]{1,0:T(2,128)}, u32[]{:S(2)}) copy-start(s32[2,2]{1,0:T(2,128)} %weights.1) | copy-start | bytes 52
  4.0 19.3 %collective-permute-start.1 = (f32[2,33,24,128]{3,2,1,0:T(8,128)S(1)}, f32[2,33,24,128]{3,2,1,0:T(8,128)S(1)}, u32[]{:S(2)}, u32[]{:S(2)}) collective-permute-start(f32[2,33,24,128]{3,2,1,0:T(8,128)S(1)} %get-tuple-element.45), channel_id=1, source_target_pairs={{1,0},{2,1},{3,2},{4,3},{5,4},{6,5},{7,6},{9,8},{10,9},{11,10},{12... | collective-permute-start | bytes 2433032 | tf_op jit(solution)/shard_map/ppermute | solution.py:674
  10.8 20.7 %collective-permute-start.3 = (f32[1408,128]{1,0:T(8,128)S(1)}, f32[1408,128]{1,0:T(8,128)S(1)}, u32[]{:S(2)}, u32[]{:S(2)}) collective-permute-start(f32[1408,128]{1,0:T(8,128)S(1)} %get-tuple-element.59.linear.lower), channel_id=1, source_target_pairs={{8,0},{16,8},{24,16},{9,1},{17,9},{25,17},{10,2},{18,10},{26,18},{... | collective-permute-start | bytes 2162696 | tf_op jit(solution)/shard_map/ppermute | solution.py:674
  12.1 19.7 %collective-permute-start.4 = (f32[1408,128]{1,0:T(8,128)S(1)}, f32[1408,128]{1,0:T(8,128)S(1)}, u32[]{:S(2)}, u32[]{:S(2)}) collective-permute-start(f32[1408,128]{1,0:T(8,128)S(1)} %get-tuple-element.60.upper.linear), channel_id=1, source_target_pairs={{0,8},{8,16},{16,24},{1,9},{9,17},{17,25},{2,10},{10,18},{18,26},{... | collective-permute-start | bytes 2162696 | tf_op jit(solution)/shard_map/ppermute | solution.py:674
  25.6 18.4 %collective-permute-start.2 = (f32[1024,128]{1,0:T(8,128)S(1)}, f32[1024,128]{1,0:T(8,128)S(1)}, u32[]{:S(2)}, u32[]{:S(2)}) collective-permute-start(f32[1024,128]{1,0:T(8,128)S(1)} %get-tuple-element.53.lower.linear), channel_id=1, source_target_pairs={{8,0},{16,8},{24,16},{9,1},{17,9},{25,17},{10,2},{18,10},{26,18},{... | collective-permute-start | bytes 1572872 | tf_op jit(solution)/shard_map/ppermute | solution.py:674
  26.9 19.1 %collective-permute-start.6 = (f32[1024,128]{1,0:T(8,128)S(1)}, f32[1024,128]{1,0:T(8,128)S(1)}, u32[]{:S(2)}, u32[]{:S(2)}) collective-permute-start(f32[1024,128]{1,0:T(8,128)S(1)} %get-tuple-element.54.linear.upper), channel_id=1, source_target_pairs={{0,8},{8,16},{16,24},{1,9},{9,17},{17,25},{2,10},{10,18},{18,26},{... | collective-permute-start | bytes 1572872 | tf_op jit(solution)/shard_map/ppermute | solution.py:674
  34.6 20.3 %collective-permute-start.8 = (f32[1216,128]{1,0:T(8,128)S(1)}, f32[1216,128]{1,0:T(8,128)S(1)}, u32[]{:S(2)}, u32[]{:S(2)}) collective-permute-start(f32[1216,128]{1,0:T(8,128)S(1)} %get-tuple-element.61.refs_4_.lower.linear), channel_id=1, source_target_pairs={{8,0},{16,8},{24,16},{9,1},{17,9},{25,17},{10,2},{18,10},{26,18},{... | collective-permute-start | bytes 1867784 | tf_op jit(solution)/shard_map/ppermute | solution.py:674
  38.8 19.4 %collective-permute-start.7 = (f32[1216,128]{1,0:T(8,128)S(1)}, f32[1216,128]{1,0:T(8,128)S(1)}, u32[]{:S(2)}, u32[]{:S(2)}) collective-permute-start(f32[1216,128]{1,0:T(8,128)S(1)} %get-tuple-element.65.refs_7_.linear.upper), channel_id=1, source_target_pairs={{0,8},{8,16},{16,24},{1,9},{9,17},{17,25},{2,10},{10,18},{18,26},{... | collective-permute-start | bytes 1867784 | tf_op jit(solution)/shard_map/ppermute | solution.py:674
  48.2 18.0 %collective-permute-start.9 = (f32[1024,128]{1,0:T(8,128)S(1)}, f32[1024,128]{1,0:T(8,128)S(1)}, u32[]{:S(2)}, u32[]{:S(2)}) collective-permute-start(f32[1024,128]{1,0:T(8,128)S(1)} %get-tuple-element.70.lower.linear), channel_id=1, source_target_pairs={{8,0},{16,8},{24,16},{9,1},{17,9},{25,17},{10,2},{18,10},{26,18},{... | collective-permute-start | bytes 1572872 | tf_op jit(solution)/shard_map/ppermute | solution.py:674
  49.5 19.2 %collective-permute-start.5 = (f32[1024,128]{1,0:T(8,128)S(1)}, f32[1024,128]{1,0:T(8,128)S(1)}, u32[]{:S(2)}, u32[]{:S(2)}) collective-permute-start(f32[1024,128]{1,0:T(8,128)S(1)} %get-tuple-element.66.refs_7_.linear.upper), channel_id=1, source_target_pairs={{0,8},{8,16},{16,24},{1,9},{9,17},{17,25},{2,10},{10,18},{18,26},{... | collective-permute-start | bytes 1572872 | tf_op jit(solution)/shard_map/ppermute | solution.py:674

commit v5 on v4

--- a/solution.py
+++ b/solution.py
@@ -135,16 +135,15 @@
         return (1.0 - job["row_part"]) * upper + job["row_part"] * lower
 
     for job in state:
-        job["line"] = line(job, 0)
-        job["here"] = lax.select(job["back_first"], zero, job["line"])
-    for j in range(columns):
-        for job in state:
+        here_line = line(job, 0)
+        here = lax.select(job["back_first"], zero, here_line)
+        for j in range(columns):
             next_line = line(job, j + 1)
-            after = lax.select(job["back_first"], job["line"], next_line)
-            first = pltpu.roll(lax.select(job["wraps"], after, job["here"]), job["back"], 1)
-            second = pltpu.roll(lax.select(job["wraps_next"], after, job["here"]), job["back_next"], 1)
+            after = lax.select(job["back_first"], here_line, next_line)
+            first = pltpu.roll(lax.select(job["wraps"], after, here), job["back"], 1)
+            second = pltpu.roll(lax.select(job["wraps_next"], after, here), job["back_next"], 1)
             job["store"](j, (1.0 - job["col_part"]) * first + job["col_part"] * second)
-            job["line"], job["here"] = next_line, after
+            here_line, here = next_line, after
 
 
 def force(linear, lower, upper, grad_rows, grad_cols, weight_lower, weight_upper):
@@ -305,7 +304,7 @@
     columns = width // LANES
     tiles = rows // ROWS
     first = 2 * ROWS - BELOW
-    at_once = 4 if tiles % 4 == 0 else 1
+    at_once = 3 if (tiles - 2) % 3 == 0 else 1
     shift = shift_of(offsets, fractions, s)
 
     def step(group, carry):
@@ -313,17 +312,17 @@
             base = i + jnp.where(shift[0] < 0, -1, 0)
 
             def pick(j, negative):
-                return tuple(sections[s, tile(jnp.clip(base + k, 0, tiles - 1)), cols(j)] for k in range(2))
+                return tuple(sections[s, tile(base + k), cols(j)] for k in range(2))
 
             def store(j, value):
                 warped[j, tile(i), :] = value
 
             return pick, shift, store
 
-        warp([job(group * at_once + k) for k in range(at_once)], columns)
+        warp([job(1 + group * at_once + k) for k in range(at_once)], columns)
         return carry
 
-    lax.fori_loop(0, tiles // at_once, step, 0)
+    lax.fori_loop(0, (tiles - 2) // at_once, step, 0)
 
     def body(j, start, here, grad_rows, grad_cols):
         at = (j, eight(start - first))

time: 73.1 us -> 73 us (level)
    ppermute x5, waiting for transfers between devices: 12.1 us -> 13 us  [exchange(): lax.ppermute(low, axis, backward)]
  transfers between devices with their start and end apart: 10 -> 10, of which waited for: 6 -> 5; matrix products, arithmetic and copies ran while one was open for 0% -> 0% of each run, Pallas kernels for 32% -> 31%
where the time goes in v5:
time: 73 us; the launch traced here: 71.7 us
  starting transfers between devices  29.8 us (41%)
  Pallas kernels  27.3 us (37%)
  waiting for transfers between devices  14.2 us (19%)
    pallas_call x11, Pallas kernels, run(): pl.pallas_call(kernel, out_shape=[shape for _, shape in outs], in_specs=[...  27.3 us
    ppermute x5, starting transfers between devices, exchange(): lax.ppermute(high, axis, forward)  21 us
    ppermute x5, waiting for transfers between devices, exchange(): lax.ppermute(low, axis, backward)  13 us
    ppermute x5, starting transfers between devices, exchange(): lax.ppermute(low, axis, backward)  8.81 us
  transfers between devices with their start and end apart: 10, of which 5 were waited for; matrix products, arithmetic and copies ran while one was open for 0% of the time, Pallas kernels for 31%

profile of v5, /device:TPU:2, one launch (start us, length us, event | category | flops | bytes accessed | tf_op | source)
XLA Modules:
  0.0 71.7 jit_solution(17885477002434909222)
XLA Ops:
  0.0 1.9 %pack.1 = (f32[2,33,24,128]{3,2,1,0:T(8,128)S(1)}, f32[2,33,24,128]{3,2,1,0:T(8,128)S(1)}) custom-call(s32[2,1,2]{2,1,0:T(1,128)} %offsets.3, s32[2,1,2]{2,1,0:T(1,128)} %fractions.3, f32[2,64,4096]{2,1,0:T(8,128)} %sections.5, f32[2,2,64,4096]{3,2,1,0:T(8,128)} %refs_3_.3), custom_call_target="tpu_custom_call" | custom-call | flops 1000000 | bytes 1000000 | tf_op jit(solution)/shard_map/pack/pallas_call | solution.py:229
  1.9 2.1 %collective-permute-start = (f32[2,33,24,128]{3,2,1,0:T(8,128)S(1)}, f32[2,33,24,128]{3,2,1,0:T(8,128)S(1)}, u32[]{:S(2)}, u32[]{:S(2)}) collective-permute-start(f32[2,33,24,128]{3,2,1,0:T(8,128)S(1)} %get-tuple-element.44), channel_id=1, source_target_pairs={{0,1},{1,2},{2,3},{3,4},{4,5},{5,6},{6,7},{8,9},{9,10},{10,11},{11... | collective-permute-start | bytes 2433032 | tf_op jit(solution)/shard_map/ppermute | solution.py:673
  4.0 3.6 %collective-permute-start.1 = (f32[2,33,24,128]{3,2,1,0:T(8,128)S(1)}, f32[2,33,24,128]{3,2,1,0:T(8,128)S(1)}, u32[]{:S(2)}, u32[]{:S(2)}) collective-permute-start(f32[2,33,24,128]{3,2,1,0:T(8,128)S(1)} %get-tuple-element.45), channel_id=1, source_target_pairs={{1,0},{2,1},{3,2},{4,3},{5,4},{6,5},{7,6},{9,8},{10,9},{11,10},{12... | collective-permute-start | bytes 2433032 | tf_op jit(solution)/shard_map/ppermute | solution.py:673
  7.7 2.8 %first_inner.1 = (f32[32,64,128]{2,1,0:T(8,128)S(1)}, f32[32,48,128]{2,1,0:T(8,128)S(1)}, f32[32,48,128]{2,1,0:T(8,128)S(1)}, f32[1408,128]{1,0:T(8,128)S(1)}, f...) custom-call(s32[2,1,2]{2,1,0:T(1,128)S(1)} %copy-done.2, ...), custom_call_target="tpu_custom_call" | custom-call | flops 8000000 | bytes 8000000 | tf_op jit(solution)/shard_map/first_inner/pallas_call | solution.py:229
  10.4 1.3 %collective-permute-start.3 = (f32[1408,128]{1,0:T(8,128)S(1)}, f32[1408,128]{1,0:T(8,128)S(1)}, u32[]{:S(2)}, u32[]{:S(2)}) collective-permute-start(f32[1408,128]{1,0:T(8,128)S(1)} %get-tuple-element.59.linear.lower), channel_id=1, source_target_pairs={{8,0},{16,8},{24,16},{9,1},{17,9},{25,17},{10,2},{18,10},{26,18},{... | collective-permute-start | bytes 2162696 | tf_op jit(solution)/shard_map/ppermute | solution.py:673
  11.7 4.6 %collective-permute-start.4 = (f32[1408,128]{1,0:T(8,128)S(1)}, f32[1408,128]{1,0:T(8,128)S(1)}, u32[]{:S(2)}, u32[]{:S(2)}) collective-permute-start(f32[1408,128]{1,0:T(8,128)S(1)} %get-tuple-element.60.upper.linear), channel_id=1, source_target_pairs={{0,8},{8,16},{16,24},{1,9},{9,17},{17,25},{2,10},{10,18},{18,26},{... | collective-permute-start | bytes 2162696 | tf_op jit(solution)/shard_map/ppermute | solution.py:673
  16.4 7.0 %collective-permute-done.1.from_next = f32[2,33,24,128]{3,2,1,0:T(8,128)S(1)} collective-permute-done((f32[2,33,24,128]{3,2,1,0:T(8,128)S(1)}, f32[2,33,24,128]{3,2,1,0:T(8,128)S(1)}, u32[]{:S(2)}, u32[]{:S(2)}) %collective-permute-start.1) | collective-permute-done | bytes 811040 | tf_op jit(solution)/shard_map/ppermute | solution.py:673
  23.3 2.2 %first_edge.1 = (f32[2,2,32,24,128]{4,3,2,1,0:T(8,128)S(1)}, f32[2,2,32,24,128]{4,3,2,1,0:T(8,128)S(1)}, f32[2,2,32,24,128]{4,3,2,1,0:T(8,128)S(1)}, f32[2,2,2,3...) custom-call(s32[2,1,2]{2,1,0:T(1,128)S(1)} %copy-done.2, ...), custom_call_target="tpu_custom_call" | custom-call | flops 5000000 | bytes 5000000 | tf_op jit(solution)/shard_map/first_edge/pallas_call | solution.py:229
  25.6 1.3 %collective-permute-start.2 = (f32[1024,128]{1,0:T(8,128)S(1)}, f32[1024,128]{1,0:T(8,128)S(1)}, u32[]{:S(2)}, u32[]{:S(2)}) collective-permute-start(f32[1024,128]{1,0:T(8,128)S(1)} %get-tuple-element.53.lower.linear), channel_id=1, source_target_pairs={{8,0},{16,8},{24,16},{9,1},{17,9},{25,17},{10,2},{18,10},{26,18},{... | collective-permute-start | bytes 1572872 | tf_op jit(solution)/shard_map/ppermute | solution.py:673
  26.9 4.6 %collective-permute-start.6 = (f32[1024,128]{1,0:T(8,128)S(1)}, f32[1024,128]{1,0:T(8,128)S(1)}, u32[]{:S(2)}, u32[]{:S(2)}) collective-permute-start(f32[1024,128]{1,0:T(8,128)S(1)} %get-tuple-element.54.linear.upper), channel_id=1, source_target_pairs={{0,8},{8,16},{16,24},{1,9},{9,17},{17,25},{2,10},{10,18},{18,26},{... | collective-permute-start | bytes 1572872 | tf_op jit(solution)/shard_map/ppermute | solution.py:673
  31.5 2.9 %inner_0.1 = (f32[2,32,48,128]{3,2,1,0:T(8,128)S(1)}, f32[2,32,48,128]{3,2,1,0:T(8,128)S(1)}, f32[2,32,48,128]{3,2,1,0:T(8,128)S(1)}, f32[2,32,48,128]{3,2,1,0:T(8,128)S(1)}, f32[1216,128]{1,0:T(8,128)S(1)}) custom-call(f32[2,2,8,128]{3,2,1,0:T(8,128)S(1)} %get-tuple-element.52.weights, f32[1408,128]{1,0:T(8,128)S(1)} %collective-permute-done.4.lower, ...), custom_call_target="tpu_custom_call" | custom-call | flops 8000000 | bytes 8000000 | tf_op jit(solution)/shard_map/inner_0/pallas_call | solution.py:229
  34.3 1.3 %collective-permute-start.8 = (f32[1216,128]{1,0:T(8,128)S(1)}, f32[1216,128]{1,0:T(8,128)S(1)}, u32[]{:S(2)}, u32[]{:S(2)}) collective-permute-start(f32[1216,128]{1,0:T(8,128)S(1)} %get-tuple-element.61.refs_4_.lower.linear), channel_id=1, source_target_pairs={{8,0},{16,8},{24,16},{9,1},{17,9},{25,17},{10,2},{18,10},{26,18},{... | collective-permute-start | bytes 1867784 | tf_op jit(solution)/shard_map/ppermute | solution.py:673
  35.6 2.8 %inner_1.1 = (f32[2,32,48,128]{3,2,1,0:T(8,128)S(1)}, f32[2,32,48,128]{3,2,1,0:T(8,128)S(1)}, f32[2,32,48,128]{3,2,1,0:T(8,128)S(1)}, f32[2,32,48,128]{3,2,1,0:T(8,128)S(1)}, f32[1216,128]{1,0:T(8,128)S(1)}) custom-call(f32[2,2,8,128]{3,2,1,0:T(8,128)S(1)} %get-tuple-element.52.weights, f32[1408,128]{1,0:T(8,128)S(1)} %get-tuple-element.59.linear.lower, ...), custom_call_target="tpu_custom_call" | custom-call | flops 8000000 | bytes 8000000 | tf_op jit(solution)/shard_map/inner_1/pallas_call | solution.py:229
  38.5 5.2 %collective-permute-start.7 = (f32[1216,128]{1,0:T(8,128)S(1)}, f32[1216,128]{1,0:T(8,128)S(1)}, u32[]{:S(2)}, u32[]{:S(2)}) collective-permute-start(f32[1216,128]{1,0:T(8,128)S(1)} %get-tuple-element.65.refs_7_.linear.upper), channel_id=1, source_target_pairs={{0,8},{8,16},{16,24},{1,9},{9,17},{17,25},{2,10},{10,18},{18,26},{... | collective-permute-start | bytes 1867784 | tf_op jit(solution)/shard_map/ppermute | solution.py:673
  43.7 2.0 %edge_1.1 = (f32[2,2,32,24,128]{4,3,2,1,0:T(8,128)S(1)}, f32[1024,128]{1,0:T(8,128)S(1)}) custom-call(f32[2,2,8,128]{3,2,1,0:T(8,128)S(1)} %get-tuple-element.52.weights, f32[1024,128]{1,0:T(8,128)S(1)} %get-tuple-element.53.lower.linear, f32[1024,128]{1,0:T(8,128)S(1)} %get-tuple-element.54.linear.upper, f32[1024,128]{1,0:T(8,128)S(1)} %collective-permute-done.2.upper, ...), custom_call_target="tpu_custom_call" | custom-call | flops 8000000 | bytes 8000000 | tf_op jit(solution)/shard_map/edge_1/pallas_call | solution.py:229
  45.7 2.1 %edge_0.1 = (f32[2,2,32,24,128]{4,3,2,1,0:T(8,128)S(1)}, f32[1024,128]{1,0:T(8,128)S(1)}) custom-call(f32[2,2,8,128]{3,2,1,0:T(8,128)S(1)} %get-tuple-element.52.weights, f32[1024,128]{1,0:T(8,128)S(1)} %collective-permute-done.6.lower, f32[1024,128]{1,0:T(8,128)S(1)} %get-tuple-element.53.lower.linear, f32[1024,128]{1,0:T(8,128)S(1)} %get-tuple-element.54.linear.upper, ...), custom_call_target="tpu_custom_call" | custom-call | flops 8000000 | bytes 8000000 | tf_op jit(solution)/shard_map/edge_0/pallas_call | solution.py:229
  47.8 1.3 %collective-permute-start.9 = (f32[1024,128]{1,0:T(8,128)S(1)}, f32[1024,128]{1,0:T(8,128)S(1)}, u32[]{:S(2)}, u32[]{:S(2)}) collective-permute-start(f32[1024,128]{1,0:T(8,128)S(1)} %get-tuple-element.70.lower.linear), channel_id=1, source_target_pairs={{8,0},{16,8},{24,16},{9,1},{17,9},{25,17},{10,2},{18,10},{26,18},{... | collective-permute-start | bytes 1572872 | tf_op jit(solution)/shard_map/ppermute | solution.py:673
  49.1 4.6 %collective-permute-start.5 = (f32[1024,128]{1,0:T(8,128)S(1)}, f32[1024,128]{1,0:T(8,128)S(1)}, u32[]{:S(2)}, u32[]{:S(2)}) collective-permute-start(f32[1024,128]{1,0:T(8,128)S(1)} %get-tuple-element.66.refs_7_.linear.upper), channel_id=1, source_target_pairs={{0,8},{8,16},{16,24},{1,9},{9,17},{17,25},{2,10},{10,18},{18,26},{... | collective-permute-start | bytes 1572872 | tf_op jit(solution)/shard_map/ppermute | solution.py:673
  53.7 1.1 %collective-permute-done.8.upper = f32[1216,128]{1,0:T(8,128)S(1)} collective-permute-done((f32[1216,128]{1,0:T(8,128)S(1)}, f32[1216,128]{1,0:T(8,128)S(1)}, u32[]{:S(2)}, u32[]{:S(2)}) %collective-permute-start.8) | collective-permute-done | bytes 622624 | tf_op jit(solution)/shard_map/ppermute | solution.py:673
  54.8 2.3 %last_inner_1.1 = (f32[2,32,48,128]{3,2,1,0:T(8,128)S(1)}, f32[2,32,48,128]{3,2,1,0:T(8,128)S(1)}, f32[2,32,48,128]{3,2,1,0:T(8,128)S(1)}, f32[2,32,4096]{2,1,0:T(8,128)S(1)}) custom-call(f32[2,2,8,128]{3,2,1,0:T(8,128)S(1)} %get-tuple-element.52.weights, f32[1216,128]{1,0:T(8,128)S(1)} %get-tuple-element.61.refs_4_.lower.linear, ...), custom_call_target="tpu_custom_call" | custom-call | flops 40000000 | bytes 40000000 | tf_op jit(solution)/shard_map/last_inner_1/pallas_call | solution.py:229
  57.8 3.3 %last_inner_0.1 = (f32[2,32,48,128]{3,2,1,0:T(8,128)S(1)}, f32[2,32,48,128]{3,2,1,0:T(8,128)S(1)}, f32[2,32,48,128]{3,2,1,0:T(8,128)S(1)}, f32[2,2,64,4096]{3,2,1,0:T(8,128)}) custom-call(f32[2,2,8,128]{3,2,1,0:T(8,128)S(1)} %get-tuple-element.52.weights, f32[1216,128]{1,0:T(8,128)S(1)} %collective-permute-done.7.lower, ...), custom_call_target="tpu_custom_call" | custom-call | flops 40000000 | bytes 40000000 | tf_op jit(solution)/shard_map/last_inner_0/pallas_call | solution.py:229
  61.1 4.9 %collective-permute-done.9.upper = f32[1024,128]{1,0:T(8,128)S(1)} collective-permute-done((f32[1024,128]{1,0:T(8,128)S(1)}, f32[1024,128]{1,0:T(8,128)S(1)}, u32[]{:S(2)}, u32[]{:S(2)}) %collective-permute-start.9) | collective-permute-done | bytes 524320 | tf_op jit(solution)/shard_map/ppermute | solution.py:673
  66.1 2.0 %last_edge_1.1.refs_6_ = f32[2,2,16,4096]{3,2,1,0:T(8,128)S(1)} custom-call(f32[2,2,8,128]{3,2,1,0:T(8,128)S(1)} %get-tuple-element.52.weights, f32[1024,128]{1,0:T(8,128)S(1)} %get-tuple-element.70.lower.linear, f32[1024,128]{1,0:T(8,128)S(1)} %get-tuple-element.66.refs_7_.linear.upper, f32[1024,128]{1,0:T(8,128)S(1)} %collective-permute-done.9.upper, ...), custom_call_target="tpu_custom_call" | custom-call | flops 8000000 | bytes 8000000 | tf_op jit(solution)/shard_map/last_edge_1/pallas_call | solution.py:229
  68.6 3.0 %last_edge_0.1 = f32[2,2,64,4096]{3,2,1,0:T(8,128)} custom-call(f32[2,2,8,128]{3,2,1,0:T(8,128)S(1)} %get-tuple-element.52.weights, f32[1024,128]{1,0:T(8,128)S(1)} %collective-permute-done.5.lower, f32[1024,128]{1,0:T(8,128)S(1)} %get-tuple-element.70.lower.linear, ...), custom_call_target="tpu_custom_call", output_to_operand_aliasing={{}: (11, {})} | custom-call | flops 8000000 | bytes 8000000 | tf_op jit(solution)/shard_map/last_edge_0/pallas_call | solution.py:229
  (17 shorter events, 1.2 us)
Async XLA Ops:
  0.0 7.6 %copy-start.2 = (s32[2,1,2]{2,1,0:T(1,128)S(1)}, s32[2,1,2]{2,1,0:T(1,128)}, u32[]{:S(2)}) copy-start(s32[2,1,2]{2,1,0:T(1,128)} %offsets.3) | copy-start | bytes 52
  0.0 7.6 %copy-start.3 = (s32[2,1,2]{2,1,0:T(1,128)S(1)}, s32[2,1,2]{2,1,0:T(1,128)}, u32[]{:S(2)}) copy-start(s32[2,1,2]{2,1,0:T(1,128)} %fractions.3) | copy-start | bytes 52
  0.0 7.6 %copy-start.1 = (f32[2,64,4096]{2,1,0:T(8,128)S(1)}, f32[2,64,4096]{2,1,0:T(8,128)}, u32[]{:S(2)}) copy-start(f32[2,64,4096]{2,1,0:T(8,128)} %sections.5) | copy-start | bytes 6291460
  0.0 7.6 %copy-start = (f32[2,2,64,4096]{3,2,1,0:T(8,128)S(1)}, f32[2,2,64,4096]{3,2,1,0:T(8,128)}, u32[]{:S(2)}) copy-start(f32[2,2,64,4096]{3,2,1,0:T(8,128)} %refs_3_.3) | copy-start | bytes 12582916
  1.9 14.4 %collective-permute-start = (f32[2,33,24,128]{3,2,1,0:T(8,128)S(1)}, f32[2,33,24,128]{3,2,1,0:T(8,128)S(1)}, u32[]{:S(2)}, u32[]{:S(2)}) collective-permute-start(f32[2,33,24,128]{3,2,1,0:T(8,128)S(1)} %get-tuple-element.44), channel_id=1, source_target_pairs={{0,1},{1,2},{2,3},{3,4},{4,5},{5,6},{6,7},{8,9},{9,10},{10,11},{11... | collective-permute-start | bytes 2433032 | tf_op jit(solution)/shard_map/ppermute | solution.py:673
  4.0 19.3 %copy-start.4 = (s32[2,2]{1,0:T(2,128)S(1)}, s32[2,2]{1,0:T(2,128)}, u32[]{:S(2)}) copy-start(s32[2,2]{1,0:T(2,128)} %weights.1) | copy-start | bytes 52
  4.0 19.3 %collective-permute-start.1 = (f32[2,33,24,128]{3,2,1,0:T(8,128)S(1)}, f32[2,33,24,128]{3,2,1,0:T(8,128)S(1)}, u32[]{:S(2)}, u32[]{:S(2)}) collective-permute-start(f32[2,33,24,128]{3,2,1,0:T(8,128)S(1)} %get-tuple-element.45), channel_id=1, source_target_pairs={{1,0},{2,1},{3,2},{4,3},{5,4},{6,5},{7,6},{9,8},{10,9},{11,10},{12... | collective-permute-start | bytes 2433032 | tf_op jit(solution)/shard_map/ppermute | solution.py:673
  10.4 21.0 %collective-permute-start.3 = (f32[1408,128]{1,0:T(8,128)S(1)}, f32[1408,128]{1,0:T(8,128)S(1)}, u32[]{:S(2)}, u32[]{:S(2)}) collective-permute-start(f32[1408,128]{1,0:T(8,128)S(1)} %get-tuple-element.59.linear.lower), channel_id=1, source_target_pairs={{8,0},{16,8},{24,16},{9,1},{17,9},{25,17},{10,2},{18,10},{26,18},{... | collective-permute-start | bytes 2162696 | tf_op jit(solution)/shard_map/ppermute | solution.py:673
  11.7 19.7 %collective-permute-start.4 = (f32[1408,128]{1,0:T(8,128)S(1)}, f32[1408,128]{1,0:T(8,128)S(1)}, u32[]{:S(2)}, u32[]{:S(2)}) collective-permute-start(f32[1408,128]{1,0:T(8,128)S(1)} %get-tuple-element.60.upper.linear), channel_id=1, source_target_pairs={{0,8},{8,16},{16,24},{1,9},{9,17},{17,25},{2,10},{10,18},{18,26},{... | collective-permute-start | bytes 2162696 | tf_op jit(solution)/shard_map/ppermute | solution.py:673
  25.6 18.1 %collective-permute-start.2 = (f32[1024,128]{1,0:T(8,128)S(1)}, f32[1024,128]{1,0:T(8,128)S(1)}, u32[]{:S(2)}, u32[]{:S(2)}) collective-permute-start(f32[1024,128]{1,0:T(8,128)S(1)} %get-tuple-element.53.lower.linear), channel_id=1, source_target_pairs={{8,0},{16,8},{24,16},{9,1},{17,9},{25,17},{10,2},{18,10},{26,18},{... | collective-permute-start | bytes 1572872 | tf_op jit(solution)/shard_map/ppermute | solution.py:673
  26.9 18.9 %collective-permute-start.6 = (f32[1024,128]{1,0:T(8,128)S(1)}, f32[1024,128]{1,0:T(8,128)S(1)}, u32[]{:S(2)}, u32[]{:S(2)}) collective-permute-start(f32[1024,128]{1,0:T(8,128)S(1)} %get-tuple-element.54.linear.upper), channel_id=1, source_target_pairs={{0,8},{8,16},{16,24},{1,9},{9,17},{17,25},{2,10},{10,18},{18,26},{... | collective-permute-start | bytes 1572872 | tf_op jit(solution)/shard_map/ppermute | solution.py:673
  34.3 20.5 %collective-permute-start.8 = (f32[1216,128]{1,0:T(8,128)S(1)}, f32[1216,128]{1,0:T(8,128)S(1)}, u32[]{:S(2)}, u32[]{:S(2)}) collective-permute-start(f32[1216,128]{1,0:T(8,128)S(1)} %get-tuple-element.61.refs_4_.lower.linear), channel_id=1, source_target_pairs={{8,0},{16,8},{24,16},{9,1},{17,9},{25,17},{10,2},{18,10},{26,18},{... | collective-permute-start | bytes 1867784 | tf_op jit(solution)/shard_map/ppermute | solution.py:673
  38.5 19.3 %collective-permute-start.7 = (f32[1216,128]{1,0:T(8,128)S(1)}, f32[1216,128]{1,0:T(8,128)S(1)}, u32[]{:S(2)}, u32[]{:S(2)}) collective-permute-start(f32[1216,128]{1,0:T(8,128)S(1)} %get-tuple-element.65.refs_7_.linear.upper), channel_id=1, source_target_pairs={{0,8},{8,16},{16,24},{1,9},{9,17},{17,25},{2,10},{10,18},{18,26},{... | collective-permute-start | bytes 1867784 | tf_op jit(solution)/shard_map/ppermute | solution.py:673
  47.8 18.2 %collective-permute-start.9 = (f32[1024,128]{1,0:T(8,128)S(1)}, f32[1024,128]{1,0:T(8,128)S(1)}, u32[]{:S(2)}, u32[]{:S(2)}) collective-permute-start(f32[1024,128]{1,0:T(8,128)S(1)} %get-tuple-element.70.lower.linear), channel_id=1, source_target_pairs={{8,0},{16,8},{24,16},{9,1},{17,9},{25,17},{10,2},{18,10},{26,18},{... | collective-permute-start | bytes 1572872 | tf_op jit(solution)/shard_map/ppermute | solution.py:673
  49.1 19.5 %collective-permute-start.5 = (f32[1024,128]{1,0:T(8,128)S(1)}, f32[1024,128]{1,0:T(8,128)S(1)}, u32[]{:S(2)}, u32[]{:S(2)}) collective-permute-start(f32[1024,128]{1,0:T(8,128)S(1)} %get-tuple-element.66.refs_7_.linear.upper), channel_id=1, source_target_pairs={{0,8},{8,16},{16,24},{1,9},{9,17},{17,25},{2,10},{10,18},{18,26},{... | collective-permute-start | bytes 1572872 | tf_op jit(solution)/shard_map/ppermute | solution.py:673
